TPU v7x, 32 devices: a whole 2x2x4 slice. The times are simulated.
32 devices in a mesh: groups: 2 (over y), rows: 4 (over z), cols: 2 (over x), sub: 2 (over core).
Axes of the slice: x: 2, y: 2, z: 4, core: 2. Of those that a mesh axis runs over, the one named last changes fastest.
Arguments:
- elevation: float32 [256, 16384], P(('groups', 'rows', 'sub'), 'cols'), parts along dimension 0, may hold values from -6 to 6
- fill_depth: float32 [256, 16384], P(('groups', 'rows', 'sub'), 'cols'), parts along dimension 0, may hold values from 0.5 to 4
- edge_rows: int32 [4, 16384], P('groups', 'cols'), parts along dimension 0, may hold values 0 or 1
- edge_sides: int32 [4, 128], P('groups', ('rows', 'sub')), parts along dimension 0, may hold values 0 or 1
- adjacency: int32 [16, 6], P('groups'), parts along dimension 0, may hold values from 0 to 7
Outputs:
- filled: float32 [256, 16384], P(('groups', 'rows', 'sub'), 'cols'), parts along dimension 0
There are 2 independent parts, one for each index of `groups`. A program takes and returns all parts, laid end to end along the dimension named above; each array names one. Nothing has to cross between parts.
Inputs may be any that keep to these rules, and one draw needn't show every extreme that they name: `adjacency`: tile numbers count tiles row by row.
All inputs are finite; a program needn't handle non-finite values. No bound on the sum of `edge_rows` or of `edge_sides` on one device may be relied on, other than what follows from the above.
Results may differ from a plain program's by a relative error of at most 0.00002.
Values sent between devices are 32-bit elements; how exact they have to be, the bound alone decides.
No kernel may reach another device: no remote copies, remote signals or barrier semaphores. Data moves between devices by JAX's collectives and lax.ppermute only.
A program may use at most 64 MiB of HBM per device.

v0:
```python
import jax
import jax.numpy as jnp
from jax import lax
from jax.experimental import pallas as pl
from jax.experimental.pallas import tpu as pltpu
from jax.sharding import PartitionSpec as P

PASSES = 8
FINAL = 4
ROUNDS = 4
HALO = PASSES + FINAL
SUBS = 8
LANES = 128
AHEAD = 5

unreached = 1000000000.0
rise_step = 0.01
hop_rise = 0.05
spill_lift = 3.0


def matching(count, first):
    pairs = []
    for low in range(first, count - 1, 2):
        pairs += [(low, low + 1), (low + 1, low)]
    return pairs


def closed(pairs, count):
    used = {source for source, _ in pairs}
    return pairs + [(place, place) for place in range(count) if place not in used]


def cross(row_pairs, col_pairs, cols, subs):
    def device(place, col):
        return (place // subs * cols + col) * subs + place % subs

    return [
        (device(row, col), device(row_to, col_to))
        for row, row_to in row_pairs
        for col, col_to in col_pairs
    ]


def chain_place():
    subs = lax.axis_size("sub")
    return lax.axis_index("rows") * subs + lax.axis_index("sub"), lax.axis_size("rows") * subs


def position():
    sub = lax.broadcasted_iota(jnp.int32, (SUBS, LANES), 0)
    lane = lax.broadcasted_iota(jnp.int32, (SUBS, LANES), 1)
    return sub, lane


def aligned(start):
    return start if isinstance(start, int) else pl.multiple_of(start, SUBS)


def rows_at(first, count, size):
    return pl.ds(aligned(first * size), count * size)


def register(row, slot, size):
    return pl.ds(aligned(row * size + slot * SUBS), SUBS)


def side_marks(sides_ref):
    height = sides_ref.shape[1]
    square = (height, height)
    diagonal = lax.broadcasted_iota(jnp.int32, square, 0) == lax.broadcasted_iota(jnp.int32, square, 1)
    marks = sides_ref[...].astype(jnp.float32)
    return [
        jnp.sum(jnp.where(diagonal, marks[side : side + 1, :], 0.0), axis=1, keepdims=True)
        for side in range(2)
    ]


def start_all(copies):
    for copy in copies:
        copy.start()
    return copies


def wait_all(copies):
    for copy in copies:
        copy.wait()


def edge_kernel(
    ground_hbm, depth_hbm, rows_hbm, sides_hbm,
    far_ref, near_ref, even_ref, odd_ref,
    ground_ref, depth_ref, marks_ref, sides_ref, sems, small_sems,
):
    height, width = ground_hbm.shape
    groups = height // SUBS
    last_tile = width // LANES - 1
    place, places = chain_place()
    col, cols = lax.axis_index("cols"), lax.axis_size("cols")
    small = [pltpu.make_async_copy(sides_hbm, sides_ref, small_sems.at[0])]
    for side, tile in enumerate((0, last_tile)):
        columns = pl.ds(tile * LANES, LANES)
        small.append(pltpu.make_async_copy(rows_hbm.at[:, columns], marks_ref.at[side], small_sems.at[1 + side]))
    copies = start_own(ground_hbm, depth_hbm, ground_ref, depth_ref, sems)
    start_all(small)
    sub, lane = position()
    wait_all(small)
    marks = side_marks(sides_ref)
    at_edges = [(lane == 0) & (col == 0), (lane == LANES - 1) & (col == cols - 1)]
    for copy in copies:
        wait_all(copy)

    def raised(group, tile):
        rows, columns = pl.ds(group * SUBS, SUBS), pl.ds(tile * LANES, LANES)
        ground = ground_ref[rows, columns]
        surface = ground + depth_ref[rows, columns]
        if tile in (0, last_tile):
            side = 0 if tile == 0 else 1
            chosen = marks[side][group * SUBS : (group + 1) * SUBS]
            surface = jnp.where((chosen > 0.5) & at_edges[side], ground, surface)
        return ground, surface

    def pack(up_ref, down_ref):
        tiles = width // (SUBS * LANES)
        size = tiles * SUBS
        skipped = height - HALO
        for tile in range(last_tile + 1):
            start = tile % tiles * SUBS + tile // tiles
            for out_ref, ground_slot, surface_slot, shift, keep in (
                (up_ref, 0, HALO - 1, 0, range(0, HALO)),
                (down_ref, HALO - 1, 0, skipped, range(skipped, height)),
            ):
                values = [raised(group, tile) for group in range(groups)]
                for kind, slot in enumerate((ground_slot, surface_slot)):
                    for group in range(groups):
                        inside = [row for row in range(group * SUBS, (group + 1) * SUBS) if row in keep]
                        first, count = inside[0], len(inside)
                        offset = first - group * SUBS
                        row = slot + first - shift
                        out_ref[pl.ds(row * size + start, count, stride=size), :] = values[group][kind][
                            offset : offset + count
                        ]

    top = place % 2 == 0
    pl.when(top)(lambda: pack(far_ref, near_ref))
    pl.when(jnp.logical_not(top))(lambda: pack(near_ref, far_ref))
    rightward = col % 2 == 0
    for group in range(groups):
        values = []
        for side, tile in enumerate((0, last_tile)):
            ground, surface = raised(group, tile)
            if group == 0:
                outlet = (marks_ref[side, 0:1] == 1) & (sub == 0) & (place == 0)
                surface = jnp.where(outlet, ground, surface)
            if group == groups - 1:
                outlet = (marks_ref[side, 1:2] == 1) & (sub == SUBS - 1) & (place == places - 1)
                surface = jnp.where(outlet, ground, surface)
            values.append((ground, surface))
        for kind in range(2):
            rows = pl.ds(kind * height + group * SUBS, SUBS)
            even_ref[rows, :] = jnp.where(rightward, values[1][kind], values[0][kind])
            odd_ref[rows, :] = jnp.where(rightward, values[0][kind], values[1][kind])


def start_own(ground_hbm, depth_hbm, ground_ref, depth_ref, sems):
    height, width = ground_hbm.shape
    groups = height // SUBS
    pieces = sems.shape[1] // groups
    part = width // pieces
    copies = []
    for group in range(groups):
        for piece in range(pieces):
            where = (pl.ds(group * SUBS, SUBS), pl.ds(piece * part, part))
            number = group * pieces + piece
            copies.append(
                start_all(
                    [
                        pltpu.make_async_copy(ground_hbm.at[where], ground_ref.at[where], sems.at[0, number]),
                        pltpu.make_async_copy(depth_hbm.at[where], depth_ref.at[where], sems.at[1, number]),
                    ]
                )
            )
    return copies


def fold_own(copies, ground_ref, depth_ref, rows_ref, sides_ref, ground_out, surface_out):
    height, width = ground_ref.shape
    groups = height // SUBS
    tiles = width // (SUBS * LANES)
    last_tile = width // LANES - 1
    pieces = len(copies) // groups
    part = width // pieces
    size = (tiles + 1) * SUBS
    place, places = chain_place()
    col, cols = lax.axis_index("cols"), lax.axis_size("cols")
    sub, lane = position()
    marks = side_marks(sides_ref)
    for group in range(groups):
        rows = pl.ds(group * SUBS, SUBS)
        for tile in range(last_tile + 1):
            if tile * LANES % part == 0:
                wait_all(copies[group * pieces + tile * LANES // part])
            columns = pl.ds(tile * LANES, LANES)
            ground = ground_ref[rows, columns]
            surface = ground + depth_ref[rows, columns]
            outlets = []
            if group == 0:
                outlets.append((rows_ref[0:1, columns] == 1) & (sub == 0) & (place == 0))
            if group == groups - 1:
                outlets.append(
                    (rows_ref[1:2, columns] == 1) & (sub == SUBS - 1) & (place == places - 1)
                )
            if tile == 0:
                outlets.append(
                    (marks[0][group * SUBS : (group + 1) * SUBS] > 0.5) & (lane == 0) & (col == 0)
                )
            if tile == last_tile:
                outlets.append(
                    (marks[1][group * SUBS : (group + 1) * SUBS] > 0.5)
                    & (lane == LANES - 1)
                    & (col == cols - 1)
                )
            for outlet in outlets:
                surface = jnp.where(outlet, ground, surface)
            chunk, slot = tile // tiles, tile % tiles
            start = (HALO + group * SUBS) * size + slot * SUBS + chunk
            ground_out[pl.ds(start, SUBS, stride=size), :] = ground
            surface_out[pl.ds(start, SUBS, stride=size), :] = surface


def unpack_rows(rows_ref, first, is_top, present, strip_refs, strip_rows, ground_ref, surface_ref, tiles):
    packed = tiles * SUBS
    size = packed + SUBS
    bases = (jnp.where(is_top, HALO - 1, 0), jnp.where(is_top, 0, HALO - 1))
    for base, out_ref, strip_row in zip(bases, (ground_ref, surface_ref), strip_rows):

        def body(row, carry):
            values = [
                jnp.where(present, rows_ref[register(base + row, slot, packed), :], unreached)
                for slot in range(tiles)
            ]
            for slot in range(tiles):
                out_ref[register(first + row, slot, size), :] = values[slot]
            fill_seam(out_ref, first + row, values[0], values[-1], strip_refs, strip_row + row, present, tiles)
            return carry

        lax.fori_loop(0, HALO, body, 0, unroll=4)


def fill_seam(out_ref, row, first_tile, last_tile, strip_refs, strip_row, present, tiles):
    col, cols = lax.axis_index("cols"), lax.axis_size("cols")
    sub, lane = position()
    rightward = col % 2 == 0
    even, odd = [ref[pl.ds(strip_row, 1), :] for ref in strip_refs]
    after = jnp.where(present & (col < cols - 1), jnp.where(rightward, even, odd), unreached)
    before = jnp.where(present & (col > 0), jnp.where(rightward, odd, even), unreached)
    after = jnp.where(sub == SUBS - 1, after, pltpu.roll(first_tile, SUBS - 1, 0))
    before = jnp.where(sub == 0, before, pltpu.roll(last_tile, 1, 0))
    out_ref[register(row, tiles, (tiles + 1) * SUBS), :] = jnp.where(lane < LANES // 2, after, before)


def relax_rows(source, target, ground, first, count, ring):
    size = ring * SUBS
    _, lane = position()
    at_first = lane == 0
    at_last = lane == LANES - 1
    order = [ring - 1] + list(range(ring - 1))
    made = {}

    def make(pair, slot):
        row = first + 2 * pair
        values = [source[register(row + step, slot, size), :] for step in range(-1, 3)]
        both = jnp.minimum(values[1], values[2])
        for one, column in enumerate((jnp.minimum(values[0], both), jnp.minimum(both, values[3]))):
            made[pair, one, slot] = (column, pltpu.roll(column, 1, 1), pltpu.roll(column, LANES - 1, 1))

    def finish(pair, slot):
        for one in range(2):
            row = first + 2 * pair + one
            before, here, after = [made[pair, one, (slot + step) % ring] for step in (-1, 0, 1)]
            from_left = jnp.where(at_first, before[1], here[1])
            from_right = jnp.where(at_last, after[2], here[2])
            lowest = jnp.minimum(jnp.minimum(from_left, from_right), here[0])
            where = register(row, slot, size)
            raised = jnp.minimum(source[where, :], lowest + rise_step)
            target[where, :] = jnp.maximum(ground[where, :], raised)

    makes = [(pair, slot) for pair in range(count // 2) for slot in order]
    finishes = [(pair, slot) for pair in range(count // 2) for slot in range(ring)]
    done = 0
    for number, item in enumerate(makes):
        make(*item)
        if number >= AHEAD:
            finish(*finishes[done])
            done += 1
    for item in finishes[done:]:
        finish(*item)


def hop_counts(links_ref, hops_ref, needed):
    tiles, degree = links_ref.shape
    links = links_ref[...]
    number = lax.broadcasted_iota(jnp.int32, (tiles, tiles), 1)
    linked = links[:, 0:1] == number
    for edge in range(1, degree):
        linked = linked | (links[:, edge : edge + 1] == number)
    linked = linked.astype(jnp.float32)
    tile = lax.broadcasted_iota(jnp.int32, (tiles, LANES), 0)
    lane = lax.broadcasted_iota(jnp.int32, (tiles, LANES), 1)
    reached = jnp.zeros((tiles, LANES), jnp.float32)
    for index, wanted in enumerate(needed):
        reached = jnp.where((lane == index) & (tile == wanted), 1.0, reached)
    hops = jnp.where(reached > 0.5, 0.0, float(ROUNDS + 1))
    for hop in range(1, ROUNDS + 1):
        reached = lax.dot_general(
            linked, reached, (((0,), (0,)), ((), ())), preferred_element_type=jnp.float32
        )
        reached = jnp.where(reached > 0.5, 1.0, 0.0)
        hops = jnp.minimum(hops, jnp.where(reached > 0.5, float(hop), float(ROUNDS + 1)))
    for index in range(len(needed)):
        hops_ref[pl.ds(index * tiles, tiles), :] = jnp.broadcast_to(
            hops[:, index : index + 1], (tiles, LANES)
        )


def needed_tiles():
    row, rows = lax.axis_index("rows"), lax.axis_size("rows")
    col, cols = lax.axis_index("cols"), lax.axis_size("cols")
    sub, subs = lax.axis_index("sub"), lax.axis_size("sub")
    above = jnp.maximum(jnp.where(sub == 0, row - 1, row), 0)
    below = jnp.minimum(jnp.where(sub == subs - 1, row + 1, row), rows - 1)
    left = jnp.maximum(col - 1, 0)
    right = jnp.minimum(col + 1, cols - 1)
    return [r * cols + c for r in (above, row, below) for c in (left, col, right)]


def inner_kernel(
    ground_hbm, depth_hbm, rows_hbm, sides_hbm, links_hbm,
    near_ref, own_even_ref, own_odd_ref, near_even_ref, near_odd_ref,
    ground_ref, surface_ref, other_ref, hops_ref,
    raw_ground_ref, raw_depth_ref, rows_ref, sides_ref, links_ref, sems, small_sems,
):
    height, width = ground_hbm.shape
    tiles = width // (SUBS * LANES)
    small = start_all(
        [
            pltpu.make_async_copy(source, target, small_sems.at[number])
            for number, (source, target) in enumerate(
                ((rows_hbm, rows_ref), (sides_hbm, sides_ref), (links_hbm, links_ref))
            )
        ]
    )
    copies = start_own(ground_hbm, depth_hbm, raw_ground_ref, raw_depth_ref, sems)
    own_strips, near_strips = (own_even_ref, own_odd_ref), (near_even_ref, near_odd_ref)
    ring = tiles + 1
    size = ring * SUBS
    place, places = chain_place()
    top = place % 2 == 0
    has_near = jnp.where(top, place < places - 1, place > 0)
    unpack_rows(
        near_ref,
        jnp.where(top, HALO + height, 0),
        jnp.logical_not(top),
        has_near,
        near_strips,
        [kind * height + jnp.where(top, 0, height - HALO) for kind in range(2)],
        ground_ref,
        surface_ref,
        tiles,
    )
    wait_all(small)
    hop_counts(links_ref, hops_ref, needed_tiles())
    fold_own(copies, raw_ground_ref, raw_depth_ref, rows_ref, sides_ref, ground_ref, surface_ref)
    for kind, out_ref in enumerate((ground_ref, surface_ref)):

        def body(row, carry):
            first_tile = out_ref[register(HALO + row, 0, size), :]
            last_tile = out_ref[register(HALO + row, tiles - 1, size), :]
            fill_seam(
                out_ref, HALO + row, first_tile, last_tile, own_strips, kind * height + row, place >= 0, tiles
            )
            return carry

        lax.fori_loop(0, height, body, 0, unroll=4)
    buffers = (surface_ref, other_ref)
    for step in range(1, PASSES + 1):
        first = step + jnp.where(top, HALO, 0)
        count = height + HALO - 2 * step
        relax_rows(buffers[(step + 1) % 2], buffers[step % 2], ground_ref, first, count, ring)


def outer_kernel(height, tiles, far_ref, even_ref, odd_ref, *refs):
    ground_ref, surface_ref, other_ref, level_ref = refs[3:7]
    ring = tiles + 1
    size = ring * SUBS
    place, places = chain_place()
    top = place % 2 == 0
    has_far = jnp.where(top, place > 0, place < places - 1)
    unpack_rows(
        far_ref,
        jnp.where(top, 0, HALO + height),
        top,
        has_far,
        (even_ref, odd_ref),
        [kind * height + jnp.where(top, height - HALO, 0) for kind in range(2)],
        ground_ref,
        surface_ref,
        tiles,
    )
    buffers = (surface_ref, other_ref)
    for step in range(1, PASSES + 1):
        first = jnp.where(top, step, HALO + height - step)
        relax_rows(buffers[(step + 1) % 2], buffers[step % 2], ground_ref, first, HALO, ring)
    band, bands = lax.axis_index("sub"), lax.axis_size("sub")
    sub, lane = position()

    def at(row, slot):
        return surface_ref[register(HALO + row, slot, size), :]

    first_cell = (sub == 0) & (lane == 0)
    last_cell = (sub == SUBS - 1) & (lane == LANES - 1)
    first_lows, last_lows, row_lows = [], [], []
    for row in range(height):
        first_lows.append(at(row, 0))
        last_lows.append(at(row, tiles - 1))
    for slot in range(tiles):
        row_lows.append(jnp.where(band == 0, at(0, slot), unreached))
        row_lows.append(jnp.where(band == bands - 1, at(height - 1, slot), unreached))
    lowest = jnp.minimum(
        least(row_lows),
        jnp.minimum(
            jnp.where(first_cell, least(first_lows), unreached),
            jnp.where(last_cell, least(last_lows), unreached),
        ),
    )
    lowest = jnp.min(jnp.min(lowest, axis=0, keepdims=True), axis=1, keepdims=True)
    level_ref[...] = jnp.broadcast_to(lowest, level_ref.shape)


def least(values):
    values = list(values)
    while len(values) > 1:
        values = [
            jnp.minimum(*values[number : number + 2]) if number + 1 < len(values) else values[number]
            for number in range(0, len(values), 2)
        ]
    return values[0]


def late_kernel(
    height, tiles, ground_ref, surface_ref, floors_ref, hops_ref, out_hbm,
    one_ref, two_ref, out_ref, sems,
):
    ring = tiles + 1
    size = ring * SUBS
    sub, lane = position()
    bands = lax.axis_size("sub")
    count = floors_ref.shape[0] // bands
    level = least(floors_ref[pl.ds(band, count, stride=bands), :] for band in range(bands))
    raised = [level]
    for hop in range(ROUNDS):
        raised.append(raised[-1] + hop_rise)
    ceilings = []
    for index in range(9):
        hops = hops_ref[pl.ds(index * count, count), :]
        lowest = jnp.full((count, LANES), unreached, jnp.float32)
        for hop in range(ROUNDS + 1):
            lowest = jnp.where(hops == float(hop), raised[hop], lowest)
        lowest = jnp.min(lowest, axis=0, keepdims=True) + spill_lift
        ceilings.append(jnp.broadcast_to(lowest, (SUBS, LANES)))
    pairs = []
    for region in range(3):
        left, middle, right = ceilings[3 * region : 3 * region + 3]
        seam = jnp.where(
            lane < LANES // 2,
            jnp.where(sub == SUBS - 1, right, middle),
            jnp.where(sub == 0, left, middle),
        )
        pairs.append((middle, seam))
    spans = ((HALO - FINAL, FINAL), (HALO, height), (HALO + height, FINAL))
    for (first, rows), (middle, seam) in zip(spans, pairs):

        def body(row, carry):
            for slot in range(ring):
                where = register(first + row, slot, size)
                value = jnp.minimum(surface_ref[where, :], seam if slot == tiles else middle)
                one_ref[where, :] = jnp.maximum(ground_ref[where, :], value)
            return carry

        lax.fori_loop(0, rows, body, 0, unroll=4)
    buffers = (one_ref, two_ref)
    for step in range(1, FINAL):
        first = HALO - FINAL + step
        relax_rows(
            buffers[(step + 1) % 2], buffers[step % 2], ground_ref, first, 2 * HALO + height - 2 * first, ring
        )
    source, target = buffers[(FINAL + 1) % 2], buffers[FINAL % 2]
    copies = []
    for group in range(height // SUBS):
        first = HALO + group * SUBS
        relax_rows(source, target, ground_ref, first, SUBS, ring)
        for tile in range(tiles * SUBS):
            chunk, slot = tile // tiles, tile % tiles
            out_ref[pl.ds(group * SUBS, SUBS), pl.ds(tile * LANES, LANES)] = target[
                pl.ds(first * size + slot * SUBS + chunk, SUBS, stride=size), :
            ]
        where = (pl.ds(group * SUBS, SUBS), slice(None))
        copies += start_all([pltpu.make_async_copy(out_ref.at[where], out_hbm.at[where], sems.at[group])])
    wait_all(copies)


def in_vmem(count):
    return [pl.BlockSpec(memory_space=pltpu.VMEM)] * count


def in_hbm(count):
    return [pl.BlockSpec(memory_space=pltpu.HBM)] * count


def per_device(elevation, fill_depth, edge_rows, edge_sides, adjacency):
    height, width = elevation.shape
    tiles = width // (SUBS * LANES)
    groups = height // SUBS
    f32 = jnp.float32
    packed = tiles * SUBS
    size = packed + SUBS
    tile_count = adjacency.shape[0]
    places = lax.axis_size(("rows", "sub"))
    cols, subs = lax.axis_size("cols"), lax.axis_size("sub")
    short = pl.CostEstimate(flops=1024, bytes_accessed=1024, transcendentals=0)
    limit = pltpu.CompilerParams(vmem_limit_bytes=24 << 20)
    arguments = [
        pltpu.with_memory_space_constraint(value, pltpu.HBM)
        for value in (elevation, fill_depth, edge_rows, edge_sides, adjacency)
    ]
    sent = pltpu.VMEM(((2 * HALO - 1) * packed, LANES), f32)
    strip = pltpu.VMEM((2 * height, LANES), f32)
    far, near, even, odd = pl.pallas_call(
        edge_kernel,
        out_shape=[sent, sent, strip, strip],
        in_specs=in_hbm(4),
        out_specs=in_vmem(4),
        scratch_shapes=[
            pltpu.VMEM((height, width), f32),
            pltpu.VMEM((height, width), f32),
            pltpu.VMEM((2, 2, LANES), jnp.int32),
            pltpu.VMEM(edge_sides.shape, jnp.int32),
            pltpu.SemaphoreType.DMA((2, 4 * groups)),
            pltpu.SemaphoreType.DMA((3,)),
        ],
        compiler_params=limit,
        cost_estimate=short,
        name="edge_rows",
    )(*arguments[:4])

    near_pairs, far_pairs = [matching(places, first) for first in range(2)]
    col_pairs = closed(matching(cols, 0), cols)
    ends = [(place, place) for place in range(places) if place not in dict(far_pairs)]
    same_col = [(col, col) for col in range(cols)]
    far_all = cross(far_pairs, same_col, cols, subs) + cross(ends, col_pairs, cols, subs)
    stay = [(place, place) for place in range(places)]
    device_axes = ("rows", "cols", "sub")

    def swap_strips(pieces, row_pairs):
        arrived = []
        for first, piece in enumerate(pieces):
            pairs = cross(row_pairs, matching(cols, first), cols, subs)
            arrived.append(lax.ppermute(piece, device_axes, pairs) if pairs else piece)
        return arrived

    far_strips = swap_strips((even, odd), far_pairs + ends)
    far_rows = lax.ppermute(far, device_axes, far_all)
    near_rows = lax.ppermute(near, ("rows", "sub"), near_pairs)
    strips = swap_strips((even, odd), stay) + swap_strips((even, odd), near_pairs)

    work = pltpu.VMEM(((height + 2 * HALO) * size, LANES), f32)
    work_scratch = pltpu.VMEM(((height + 2 * HALO) * size, LANES), f32)
    ground, surface, other, hops = pl.pallas_call(
        inner_kernel,
        out_shape=[work, work, work, pltpu.VMEM((9 * tile_count, LANES), f32)],
        in_specs=in_hbm(5) + in_vmem(5),
        out_specs=in_vmem(4),
        scratch_shapes=[
            pltpu.VMEM((height, width), f32),
            pltpu.VMEM((height, width), f32),
            pltpu.VMEM(edge_rows.shape, jnp.int32),
            pltpu.VMEM(edge_sides.shape, jnp.int32),
            pltpu.VMEM(adjacency.shape, jnp.int32),
            pltpu.SemaphoreType.DMA((2, 4 * groups)),
            pltpu.SemaphoreType.DMA((3,)),
        ],
        compiler_params=limit,
        cost_estimate=short,
        name="inner_passes",
    )(*arguments, near_rows, *strips)

    def outer(far_ref, *refs):
        outer_kernel(height, tiles, far_ref, *refs)

    devices = lax.axis_size(device_axes)
    ground, surface, other, floors = pl.pallas_call(
        outer,
        out_shape=[work, work, work, pltpu.VMEM((devices, LANES), f32)],
        in_specs=in_vmem(6),
        out_specs=in_vmem(4),
        input_output_aliases={3: 0, 4: 1, 5: 2},
        compiler_params=limit,
        cost_estimate=short,
        name="outer_passes",
    )(far_rows, *far_strips, ground, surface, other)

    floors = lax.all_to_all(floors, device_axes, 0, 0, tiled=True)

    def late(*refs):
        late_kernel(height, tiles, *refs)

    return pl.pallas_call(
        late,
        out_shape=jax.ShapeDtypeStruct((height, width), f32),
        in_specs=in_vmem(4),
        out_specs=pl.BlockSpec(memory_space=pltpu.HBM),
        scratch_shapes=[
            work_scratch,
            work_scratch,
            pltpu.VMEM((height, width), f32),
            pltpu.SemaphoreType.DMA((groups,)),
        ],
        compiler_params=limit,
        cost_estimate=short,
        name="final_passes",
    )(ground, surface, floors, hops)


def solution(mesh):
    placed = (
        P(("groups", "rows", "sub"), "cols"),
        P(("groups", "rows", "sub"), "cols"),
        P("groups", "cols"),
        P("groups", ("rows", "sub")),
        P("groups", None),
    )
    return jax.shard_map(
        per_device,
        mesh=mesh,
        in_specs=placed,
        out_specs=P(("groups", "rows", "sub"), "cols"),
        check_vma=False,
    )
```

profile of v0, /device:TPU:0, one launch (start us, length us, event | category | flops | bytes accessed | tf_op | source)
XLA Modules:
  0.0 38.7 jit_solution(9255610234952983898)
XLA Ops:
  0.0 2.4 %edge_rows.1 = (f32[1472,128]{1,0:T(8,128)S(1)}, f32[1472,128]{1,0:T(8,128)S(1)}, f32[32,128]{1,0:T(8,128)S(1)}, f32[32,128]{1,0:T(8,128)S(1)}) custom-call(f32[16,8192]{1,0:T(8,128)} %ground_hbm.3, f32[16,8192]{1,0:T(8,128)} %depth_hbm.3, s32[2,8192]{1,0:T(2,128)} %rows_hbm.3, s32[2,16]{1,0:T(2,128)} %sides_hbm.3), custom_call_target="tpu_custom_call" | custom-call | flops 1024 | bytes 1024 | tf_op jit(solution)/shard_map/edge_rows/pallas_call | solution.py:538
  2.4 0.5 %collective-permute-start.2 = (f32[1472,128]{1,0:T(8,128)S(1)}, f32[1472,128]{1,0:T(8,128)S(1)}, u32[]{:S(2)}, u32[]{:S(2)}) collective-permute-start(f32[1472,128]{1,0:T(8,128)S(1)} %get-tuple-element.19), channel_id=1, source_target_pairs={{0,1},{1,0},{4,5},{5,4},{8,9},{9,8},{12,13},{13,12},{2,3},{3,2},{6... | collective-permute-start | bytes 2261000 | tf_op jit(solution)/shard_map/ppermute | solution.py:573
  3.0 2.6 %collective-permute-start = (f32[1472,128]{1,0:T(8,128)S(1)}, f32[1472,128]{1,0:T(8,128)S(1)}, u32[]{:S(2)}, u32[]{:S(2)}) collective-permute-start(f32[1472,128]{1,0:T(8,128)S(1)} %get-tuple-element.16), channel_id=1, source_target_pairs={{1,4},{3,6},{4,1},{6,3},{5,8},{7,10},{8,5},{10,7},{9,12},{11,14},{... | collective-permute-start | bytes 2261000 | tf_op jit(solution)/shard_map/ppermute | solution.py:572
  5.5 1.3 %collective-permute-start.4 = (f32[32,128]{1,0:T(8,128)S(1)}, f32[32,128]{1,0:T(8,128)S(1)}, u32[]{:S(2)}, u32[]{:S(2)}) collective-permute-start(f32[32,128]{1,0:T(8,128)S(1)} %get-tuple-element.17), channel_id=1, source_target_pairs={{0,3},{2,1},{1,2},{3,0},{4,7},{6,5},{5,6},{7,4},{8,11},{10,9},{9,1... | collective-permute-start | bytes 49160 | tf_op jit(solution)/shard_map/ppermute | solution.py:568
  6.8 0.5 %collective-permute-start.3 = (f32[32,128]{1,0:T(8,128)S(1)}, f32[32,128]{1,0:T(8,128)S(1)}, u32[]{:S(2)}, u32[]{:S(2)}) collective-permute-start(f32[32,128]{1,0:T(8,128)S(1)} %get-tuple-element.17), channel_id=1, source_target_pairs={{0,2},{2,0},{1,3},{3,1},{4,6},{6,4},{5,7},{7,5},{8,10},{10,8},{9,1... | collective-permute-start | bytes 49160 | tf_op jit(solution)/shard_map/ppermute | solution.py:568
  7.4 1.5 %collective-permute-start.1 = (f32[32,128]{1,0:T(8,128)S(1)}, f32[32,128]{1,0:T(8,128)S(1)}, u32[]{:S(2)}, u32[]{:S(2)}) collective-permute-start(f32[32,128]{1,0:T(8,128)S(1)} %get-tuple-element.17), channel_id=1, source_target_pairs={{1,6},{3,4},{4,3},{6,1},{5,10},{7,8},{8,7},{10,5},{9,14},{11,12},{... | collective-permute-start | bytes 49160 | tf_op jit(solution)/shard_map/ppermute | solution.py:568
  8.9 6.4 %collective-permute-done.4.near_even_ref = f32[32,128]{1,0:T(8,128)S(1)} collective-permute-done((f32[32,128]{1,0:T(8,128)S(1)}, f32[32,128]{1,0:T(8,128)S(1)}, u32[]{:S(2)}, u32[]{:S(2)}) %collective-permute-start.4) | collective-permute-done | bytes 16416 | tf_op jit(solution)/shard_map/ppermute | solution.py:568
  15.2 0.6 %collective-permute-done.3.own_even_ref = f32[32,128]{1,0:T(8,128)S(1)} collective-permute-done((f32[32,128]{1,0:T(8,128)S(1)}, f32[32,128]{1,0:T(8,128)S(1)}, u32[]{:S(2)}, u32[]{:S(2)}) %collective-permute-start.3) | collective-permute-done | bytes 16416 | tf_op jit(solution)/shard_map/ppermute | solution.py:568
  15.8 0.0 collective-permute-done.2.near_ref
  15.9 5.7 %inner_passes.1 = (f32[2880,128]{1,0:T(8,128)S(1)}, f32[2880,128]{1,0:T(8,128)S(1)}, f32[2880,128]{1,0:T(8,128)S(1)}, f32[72,128]{1,0:T(8,128)S(1)}) custom-call(f32[16,8192]{1,0:T(8,128)} %ground_hbm.3, f32[16,8192]{1,0:T(8,128)} %depth_hbm.3, s32[2,8192]{1,0:T(2,128)} %rows_hbm.3, s32[2,16]{1,0:T(2,128)} %sides_hbm.3, s32[8,6]{1,0:T(8,128)} %links_hbm.1, ...), custom_call_target="tpu_custom_call" | custom-call | flops 1024 | bytes 1024 | tf_op jit(solution)/shard_map/inner_passes/pallas_call | solution.py:578
  21.5 0.0 collective-permute-done.1.refs_0_
  21.6 0.0 collective-permute-done.far_ref
  21.6 2.4 %outer_passes.1 = (f32[2880,128]{1,0:T(8,128)S(1)}, f32[2880,128]{1,0:T(8,128)S(1)}, f32[2880,128]{1,0:T(8,128)S(1)}, f32[16,128]{1,0:T(8,128)S(1)}) custom-call(f32[1472,128]{1,0:T(8,128)S(1)} %collective-permute-done.far_ref, f32[32,128]{1,0:T(8,128)S(1)} %collective-permute-done.1.refs_0_, ...), custom_call_target="tpu_custom_call", output_to_operand_aliasing={{0}: (3, {}), {1}: (4, {}), {2}: (5, {})} | custom-call | flops 1024 | bytes 1024 | tf_op jit(solution)/shard_map/outer_passes/pallas_call | solution.py:601
  24.0 12.1 %all_to_all.11 = f32[16,1,128]{2,1,0:T(1,128)S(1)} all-to-all(f32[16,1,128]{2,1,0:T(1,128)S(1)} %bitcast.5), channel_id=1, replica_groups=mesh['groups'=2,'rows'=4,'cols'=2,'sub'=2] {'rows','cols','sub'}, dimensions={0} | all-to-all | bytes 16384 | tf_op jit(solution)/shard_map/all_to_all | solution.py:612
  36.1 2.5 %final_passes.1 = f32[16,8192]{1,0:T(8,128)} custom-call(f32[2880,128]{1,0:T(8,128)S(1)} %get-tuple-element.23.refs_0_, f32[2880,128]{1,0:T(8,128)S(1)} %get-tuple-element.24.refs_1_, f32[16,128]{1,0:T(8,128)S(1)} %bitcast.4, f32[72,128]{1,0:T(8,128)S(1)} %get-tuple-element.26.refs_3_), custom_call_target="tpu_custom_call" | custom-call | flops 1024 | bytes 1024 | tf_op jit(solution)/shard_map/final_passes/pallas_call | solution.py:617
Async XLA Ops:
  2.4 13.4 %collective-permute-start.2 = (f32[1472,128]{1,0:T(8,128)S(1)}, f32[1472,128]{1,0:T(8,128)S(1)}, u32[]{:S(2)}, u32[]{:S(2)}) collective-permute-start(f32[1472,128]{1,0:T(8,128)S(1)} %get-tuple-element.19), channel_id=1, source_target_pairs={{0,1},{1,0},{4,5},{5,4},{8,9},{9,8},{12,13},{13,12},{2,3},{3,2},{6... | collective-permute-start | bytes 2261000 | tf_op jit(solution)/shard_map/ppermute | solution.py:573
  3.0 18.6 %collective-permute-start = (f32[1472,128]{1,0:T(8,128)S(1)}, f32[1472,128]{1,0:T(8,128)S(1)}, u32[]{:S(2)}, u32[]{:S(2)}) collective-permute-start(f32[1472,128]{1,0:T(8,128)S(1)} %get-tuple-element.16), channel_id=1, source_target_pairs={{1,4},{3,6},{4,1},{6,3},{5,8},{7,10},{8,5},{10,7},{9,12},{11,14},{... | collective-permute-start | bytes 2261000 | tf_op jit(solution)/shard_map/ppermute | solution.py:572
  5.5 9.7 %collective-permute-start.4 = (f32[32,128]{1,0:T(8,128)S(1)}, f32[32,128]{1,0:T(8,128)S(1)}, u32[]{:S(2)}, u32[]{:S(2)}) collective-permute-start(f32[32,128]{1,0:T(8,128)S(1)} %get-tuple-element.17), channel_id=1, source_target_pairs={{0,3},{2,1},{1,2},{3,0},{4,7},{6,5},{5,6},{7,4},{8,11},{10,9},{9,1... | collective-permute-start | bytes 49160 | tf_op jit(solution)/shard_map/ppermute | solution.py:568
  6.8 9.0 %collective-permute-start.3 = (f32[32,128]{1,0:T(8,128)S(1)}, f32[32,128]{1,0:T(8,128)S(1)}, u32[]{:S(2)}, u32[]{:S(2)}) collective-permute-start(f32[32,128]{1,0:T(8,128)S(1)} %get-tuple-element.17), channel_id=1, source_target_pairs={{0,2},{2,0},{1,3},{3,1},{4,6},{6,4},{5,7},{7,5},{8,10},{10,8},{9,1... | collective-permute-start | bytes 49160 | tf_op jit(solution)/shard_map/ppermute | solution.py:568
  7.4 14.2 %collective-permute-start.1 = (f32[32,128]{1,0:T(8,128)S(1)}, f32[32,128]{1,0:T(8,128)S(1)}, u32[]{:S(2)}, u32[]{:S(2)}) collective-permute-start(f32[32,128]{1,0:T(8,128)S(1)} %get-tuple-element.17), channel_id=1, source_target_pairs={{1,6},{3,4},{4,3},{6,1},{5,10},{7,8},{8,7},{10,5},{9,14},{11,12},{... | collective-permute-start | bytes 49160 | tf_op jit(solution)/shard_map/ppermute | solution.py:568
where the time goes:
time: 38.9 us; the launch traced here: 38.7 us
  Pallas kernels  13.1 us (34%)
  blocking collectives  12.1 us (31%)
  waiting for transfers between devices  7 us (18%)
  starting transfers between devices  6.4 us (16%)
    all_to_all x1, blocking collectives, per_device(): floors = lax.all_to_all(floors, device_axes, 0, 0, tiled=True)  12.1 us
    ppermute x3, waiting for transfers between devices, swap_strips(): arrived.append(lax.ppermute(piece, device_axes, pairs) if pairs else piece)  7 us
    pallas_call x1, Pallas kernels, per_device(): pl.pallas_call(inner_kernel, out_shape=[work, work, work, pltpu.VMEM((9 *...  5.69 us
    ppermute x3, starting transfers between devices, swap_strips(): arrived.append(lax.ppermute(piece, device_axes, pairs) if pairs else piece)  3.32 us
    ppermute x1, starting transfers between devices, per_device(): far_rows = lax.ppermute(far, device_axes, far_all)  2.55 us
    pallas_call x1, Pallas kernels, per_device(): pl.pallas_call(late, out_shape=jax.ShapeDtypeStruct((height, width), f32)...  2.54 us
    pallas_call x1, Pallas kernels, per_device(): pl.pallas_call(outer, out_shape=[work, work, work, pltpu.VMEM((devices, L...  2.44 us
    pallas_call x1, Pallas kernels, per_device(): pl.pallas_call(edge_kernel, out_shape=[sent, sent, strip, strip], in_spec...  2.43 us
  transfers between devices with their start and end apart: 5, of which 2 were waited for; matrix products, arithmetic and copies ran while one was open for 0% of the time, Pallas kernels for 15%

commit v1 on v0

--- a/solution.py
+++ b/solution.py
@@ -554,11 +554,15 @@
     )(*arguments[:4])
 
     near_pairs, far_pairs = [matching(places, first) for first in range(2)]
-    col_pairs = closed(matching(cols, 0), cols)
+    stay = [(place, place) for place in range(places)]
     ends = [(place, place) for place in range(places) if place not in dict(far_pairs)]
-    same_col = [(col, col) for col in range(cols)]
-    far_all = cross(far_pairs, same_col, cols, subs) + cross(ends, col_pairs, cols, subs)
-    stay = [(place, place) for place in range(places)]
+    groups_count = lax.axis_size("groups")
+    part = places * cols
+    far_all = []
+    for group, other in closed(matching(groups_count, 0), groups_count):
+        for chosen, target in ((far_pairs, group), (ends, other)):
+            for source, arrival in cross(chosen, [(col, col) for col in range(cols)], cols, subs):
+                far_all.append((group * part + source, target * part + arrival))
     device_axes = ("rows", "cols", "sub")
 
     def swap_strips(pieces, row_pairs):
@@ -569,7 +573,7 @@
         return arrived
 
     far_strips = swap_strips((even, odd), far_pairs + ends)
-    far_rows = lax.ppermute(far, device_axes, far_all)
+    far_rows = lax.ppermute(far, ("groups",) + device_axes, far_all)
     near_rows = lax.ppermute(near, ("rows", "sub"), near_pairs)
     strips = swap_strips((even, odd), stay) + swap_strips((even, odd), near_pairs)
 

time: 38.9 us -> 32.7 us (0.84)
  waiting for transfers between devices: 7 us -> 1.72 us
  blocking collectives: 12.1 us -> 11.2 us
    ppermute x3, waiting for transfers between devices: 7 us -> 1.71 us  [swap_strips(): arrived.append(lax.ppermute(piece, device_axes, pairs) if pairs else piece)]
    all_to_all x1, blocking collectives: 12.1 us -> 11.2 us  [per_device(): floors = lax.all_to_all(floors, device_axes, 0, 0, tiled=True)]
  transfers between devices with their start and end apart: 5 -> 5, of which waited for: 2 -> 1; matrix products, arithmetic and copies ran while one was open for 0% -> 0% of each run, Pallas kernels for 15% -> 18%
where the time goes in v1:
time: 32.7 us; the launch traced here: 32.4 us
  Pallas kernels  13.1 us (40%)
  blocking collectives  11.2 us (34%)
  starting transfers between devices  6.4 us (20%)
  waiting for transfers between devices  1.72 us (5%)
    all_to_all x1, blocking collectives, per_device(): floors = lax.all_to_all(floors, device_axes, 0, 0, tiled=True)  11.2 us
    pallas_call x1, Pallas kernels, per_device(): pl.pallas_call(inner_kernel, out_shape=[work, work, work, pltpu.VMEM((9 *...  5.69 us
    ppermute x3, starting transfers between devices, swap_strips(): arrived.append(lax.ppermute(piece, device_axes, pairs) if pairs else piece)  3.29 us
    ppermute x1, starting transfers between devices, per_device(): far_rows = lax.ppermute(far, ('groups',) + device_axes, far_all)  2.58 us
    pallas_call x1, Pallas kernels, per_device(): pl.pallas_call(late, out_shape=jax.ShapeDtypeStruct((height, width), f32)...  2.54 us
    pallas_call x1, Pallas kernels, per_device(): pl.pallas_call(outer, out_shape=[work, work, work, pltpu.VMEM((devices, L...  2.44 us
    pallas_call x1, Pallas kernels, per_device(): pl.pallas_call(edge_kernel, out_shape=[sent, sent, strip, strip], in_spec...  2.43 us
    ppermute x3, waiting for transfers between devices, swap_strips(): arrived.append(lax.ppermute(piece, device_axes, pairs) if pairs else piece)  1.71 us
  transfers between devices with their start and end apart: 5, of which 1 were waited for; matrix products, arithmetic and copies ran while one was open for 0% of the time, Pallas kernels for 18%

profile of v1, /device:TPU:0, one launch (start us, length us, event | category | flops | bytes accessed | tf_op | source)
XLA Modules:
  0.0 32.4 jit_solution(4872275212310382008)
XLA Ops:
  0.0 2.4 %edge_rows.1 = (f32[1472,128]{1,0:T(8,128)S(1)}, f32[1472,128]{1,0:T(8,128)S(1)}, f32[32,128]{1,0:T(8,128)S(1)}, f32[32,128]{1,0:T(8,128)S(1)}) custom-call(f32[16,8192]{1,0:T(8,128)} %ground_hbm.3, f32[16,8192]{1,0:T(8,128)} %depth_hbm.3, s32[2,8192]{1,0:T(2,128)} %rows_hbm.3, s32[2,16]{1,0:T(2,128)} %sides_hbm.3), custom_call_target="tpu_custom_call" | custom-call | flops 1024 | bytes 1024 | tf_op jit(solution)/shard_map/edge_rows/pallas_call | solution.py:538
  2.4 0.5 %collective-permute-start.2 = (f32[1472,128]{1,0:T(8,128)S(1)}, f32[1472,128]{1,0:T(8,128)S(1)}, u32[]{:S(2)}, u32[]{:S(2)}) collective-permute-start(f32[1472,128]{1,0:T(8,128)S(1)} %get-tuple-element.19), channel_id=1, source_target_pairs={{0,1},{1,0},{4,5},{5,4},{8,9},{9,8},{12,13},{13,12},{2,3},{3,2},{6... | collective-permute-start | bytes 2261000 | tf_op jit(solution)/shard_map/ppermute | solution.py:577
  3.0 2.6 %collective-permute-start = (f32[1472,128]{1,0:T(8,128)S(1)}, f32[1472,128]{1,0:T(8,128)S(1)}, u32[]{:S(2)}, u32[]{:S(2)}) collective-permute-start(f32[1472,128]{1,0:T(8,128)S(1)} %get-tuple-element.16), channel_id=1, source_target_pairs={{1,4},{3,6},{4,1},{6,3},{5,8},{7,10},{8,5},{10,7},{9,12},{11,14},{... | collective-permute-start | bytes 2261000 | tf_op jit(solution)/shard_map/ppermute | solution.py:576
  5.6 1.3 %collective-permute-start.4 = (f32[32,128]{1,0:T(8,128)S(1)}, f32[32,128]{1,0:T(8,128)S(1)}, u32[]{:S(2)}, u32[]{:S(2)}) collective-permute-start(f32[32,128]{1,0:T(8,128)S(1)} %get-tuple-element.17), channel_id=1, source_target_pairs={{0,3},{2,1},{1,2},{3,0},{4,7},{6,5},{5,6},{7,4},{8,11},{10,9},{9,1... | collective-permute-start | bytes 49160 | tf_op jit(solution)/shard_map/ppermute | solution.py:572
  6.8 0.5 %collective-permute-start.3 = (f32[32,128]{1,0:T(8,128)S(1)}, f32[32,128]{1,0:T(8,128)S(1)}, u32[]{:S(2)}, u32[]{:S(2)}) collective-permute-start(f32[32,128]{1,0:T(8,128)S(1)} %get-tuple-element.17), channel_id=1, source_target_pairs={{0,2},{2,0},{1,3},{3,1},{4,6},{6,4},{5,7},{7,5},{8,10},{10,8},{9,1... | collective-permute-start | bytes 49160 | tf_op jit(solution)/shard_map/ppermute | solution.py:572
  7.4 1.5 %collective-permute-start.1 = (f32[32,128]{1,0:T(8,128)S(1)}, f32[32,128]{1,0:T(8,128)S(1)}, u32[]{:S(2)}, u32[]{:S(2)}) collective-permute-start(f32[32,128]{1,0:T(8,128)S(1)} %get-tuple-element.17), channel_id=1, source_target_pairs={{1,6},{3,4},{4,3},{6,1},{5,10},{7,8},{8,7},{10,5},{9,14},{11,12},{... | collective-permute-start | bytes 49160 | tf_op jit(solution)/shard_map/ppermute | solution.py:572
  8.9 0.0 collective-permute-done.4.near_even_ref
  8.9 1.7 %collective-permute-done.3.own_even_ref = f32[32,128]{1,0:T(8,128)S(1)} collective-permute-done((f32[32,128]{1,0:T(8,128)S(1)}, f32[32,128]{1,0:T(8,128)S(1)}, u32[]{:S(2)}, u32[]{:S(2)}) %collective-permute-start.3) | collective-permute-done | bytes 16416 | tf_op jit(solution)/shard_map/ppermute | solution.py:572
  10.6 0.0 collective-permute-done.2.near_ref
  10.6 5.7 %inner_passes.1 = (f32[2880,128]{1,0:T(8,128)S(1)}, f32[2880,128]{1,0:T(8,128)S(1)}, f32[2880,128]{1,0:T(8,128)S(1)}, f32[72,128]{1,0:T(8,128)S(1)}) custom-call(f32[16,8192]{1,0:T(8,128)} %ground_hbm.3, f32[16,8192]{1,0:T(8,128)} %depth_hbm.3, s32[2,8192]{1,0:T(2,128)} %rows_hbm.3, s32[2,16]{1,0:T(2,128)} %sides_hbm.3, s32[8,6]{1,0:T(8,128)} %links_hbm.1, ...), custom_call_target="tpu_custom_call" | custom-call | flops 1024 | bytes 1024 | tf_op jit(solution)/shard_map/inner_passes/pallas_call | solution.py:582
  16.3 0.0 collective-permute-done.1.refs_0_
  16.3 0.0 collective-permute-done.far_ref
  16.3 2.4 %outer_passes.1 = (f32[2880,128]{1,0:T(8,128)S(1)}, f32[2880,128]{1,0:T(8,128)S(1)}, f32[2880,128]{1,0:T(8,128)S(1)}, f32[16,128]{1,0:T(8,128)S(1)}) custom-call(f32[1472,128]{1,0:T(8,128)S(1)} %collective-permute-done.far_ref, f32[32,128]{1,0:T(8,128)S(1)} %collective-permute-done.1.refs_0_, ...), custom_call_target="tpu_custom_call", output_to_operand_aliasing={{0}: (3, {}), {1}: (4, {}), {2}: (5, {})} | custom-call | flops 1024 | bytes 1024 | tf_op jit(solution)/shard_map/outer_passes/pallas_call | solution.py:605
  18.7 11.2 %all_to_all.11 = f32[16,1,128]{2,1,0:T(1,128)S(1)} all-to-all(f32[16,1,128]{2,1,0:T(1,128)S(1)} %bitcast.5), channel_id=1, replica_groups=mesh['groups'=2,'rows'=4,'cols'=2,'sub'=2] {'rows','cols','sub'}, dimensions={0} | all-to-all | bytes 16384 | tf_op jit(solution)/shard_map/all_to_all | solution.py:616
  29.9 2.5 %final_passes.1 = f32[16,8192]{1,0:T(8,128)} custom-call(f32[2880,128]{1,0:T(8,128)S(1)} %get-tuple-element.23.refs_0_, f32[2880,128]{1,0:T(8,128)S(1)} %get-tuple-element.24.refs_1_, f32[16,128]{1,0:T(8,128)S(1)} %bitcast.4, f32[72,128]{1,0:T(8,128)S(1)} %get-tuple-element.26.refs_3_), custom_call_target="tpu_custom_call" | custom-call | flops 1024 | bytes 1024 | tf_op jit(solution)/shard_map/final_passes/pallas_call | solution.py:621
Async XLA Ops:
  2.4 8.1 %collective-permute-start.2 = (f32[1472,128]{1,0:T(8,128)S(1)}, f32[1472,128]{1,0:T(8,128)S(1)}, u32[]{:S(2)}, u32[]{:S(2)}) collective-permute-start(f32[1472,128]{1,0:T(8,128)S(1)} %get-tuple-element.19), channel_id=1, source_target_pairs={{0,1},{1,0},{4,5},{5,4},{8,9},{9,8},{12,13},{13,12},{2,3},{3,2},{6... | collective-permute-start | bytes 2261000 | tf_op jit(solution)/shard_map/ppermute | solution.py:577
  3.0 13.3 %collective-permute-start = (f32[1472,128]{1,0:T(8,128)S(1)}, f32[1472,128]{1,0:T(8,128)S(1)}, u32[]{:S(2)}, u32[]{:S(2)}) collective-permute-start(f32[1472,128]{1,0:T(8,128)S(1)} %get-tuple-element.16), channel_id=1, source_target_pairs={{1,4},{3,6},{4,1},{6,3},{5,8},{7,10},{8,5},{10,7},{9,12},{11,14},{... | collective-permute-start | bytes 2261000 | tf_op jit(solution)/shard_map/ppermute | solution.py:576
  5.6 3.3 %collective-permute-start.4 = (f32[32,128]{1,0:T(8,128)S(1)}, f32[32,128]{1,0:T(8,128)S(1)}, u32[]{:S(2)}, u32[]{:S(2)}) collective-permute-start(f32[32,128]{1,0:T(8,128)S(1)} %get-tuple-element.17), channel_id=1, source_target_pairs={{0,3},{2,1},{1,2},{3,0},{4,7},{6,5},{5,6},{7,4},{8,11},{10,9},{9,1... | collective-permute-start | bytes 49160 | tf_op jit(solution)/shard_map/ppermute | solution.py:572
  6.8 3.7 %collective-permute-start.3 = (f32[32,128]{1,0:T(8,128)S(1)}, f32[32,128]{1,0:T(8,128)S(1)}, u32[]{:S(2)}, u32[]{:S(2)}) collective-permute-start(f32[32,128]{1,0:T(8,128)S(1)} %get-tuple-element.17), channel_id=1, source_target_pairs={{0,2},{2,0},{1,3},{3,1},{4,6},{6,4},{5,7},{7,5},{8,10},{10,8},{9,1... | collective-permute-start | bytes 49160 | tf_op jit(solution)/shard_map/ppermute | solution.py:572
  7.4 8.9 %collective-permute-start.1 = (f32[32,128]{1,0:T(8,128)S(1)}, f32[32,128]{1,0:T(8,128)S(1)}, u32[]{:S(2)}, u32[]{:S(2)}) collective-permute-start(f32[32,128]{1,0:T(8,128)S(1)} %get-tuple-element.17), channel_id=1, source_target_pairs={{1,6},{3,4},{4,3},{6,1},{5,10},{7,8},{8,7},{10,5},{9,14},{11,12},{... | collective-permute-start | bytes 49160 | tf_op jit(solution)/shard_map/ppermute | solution.py:572

commit v2 on v1

--- a/solution.py
+++ b/solution.py
@@ -454,9 +454,8 @@
     ring = tiles + 1
     size = ring * SUBS
     sub, lane = position()
-    bands = lax.axis_size("sub")
-    count = floors_ref.shape[0] // bands
-    level = least(floors_ref[pl.ds(band, count, stride=bands), :] for band in range(bands))
+    level = floors_ref[...]
+    count = level.shape[0]
     raised = [level]
     for hop in range(ROUNDS):
         raised.append(raised[-1] + hop_rise)
@@ -601,10 +600,9 @@
     def outer(far_ref, *refs):
         outer_kernel(height, tiles, far_ref, *refs)
 
-    devices = lax.axis_size(device_axes)
     ground, surface, other, floors = pl.pallas_call(
         outer,
-        out_shape=[work, work, work, pltpu.VMEM((devices, LANES), f32)],
+        out_shape=[work, work, work, pltpu.VMEM((tile_count, LANES), f32)],
         in_specs=in_vmem(6),
         out_specs=in_vmem(4),
         input_output_aliases={3: 0, 4: 1, 5: 2},
@@ -613,7 +611,10 @@
         name="outer_passes",
     )(far_rows, *far_strips, ground, surface, other)
 
-    floors = lax.all_to_all(floors, device_axes, 0, 0, tiled=True)
+    for shift in range(1, subs):
+        pairs = [(sub, (sub + shift) % subs) for sub in range(subs)]
+        floors = jnp.minimum(floors, lax.ppermute(floors, "sub", pairs))
+    floors = lax.all_to_all(floors, ("rows", "cols"), 0, 0, tiled=True)
 
     def late(*refs):
         late_kernel(height, tiles, *refs)

time: 32.7 us -> 33.8 us (1.034)
  waiting for transfers between devices: 1.72 us -> 2.56 us
  starting transfers between devices: 6.4 us -> 6.75 us
    ppermute x0 -> x1, waiting for transfers between devices: none -> 0.84 us  [per_device(): floors = jnp.minimum(floors, lax.ppermute(floors, 'sub', pairs))]
    ppermute x0 -> x1, starting transfers between devices: none -> 0.34 us  [per_device(): floors = jnp.minimum(floors, lax.ppermute(floors, 'sub', pairs))]
  transfers between devices with their start and end apart: 5 -> 6, of which waited for: 1 -> 2; matrix products, arithmetic and copies ran while one was open for 0% -> 0% of each run, Pallas kernels for 18% -> 17%
where the time goes in v2:
time: 33.8 us; the launch traced here: 33.6 us
  Pallas kernels  13.1 us (39%)
  blocking collectives  11.1 us (33%)
  starting transfers between devices  6.75 us (20%)
  waiting for transfers between devices  2.56 us (8%)
    all_to_all x1, blocking collectives, per_device(): floors = lax.all_to_all(floors, ('rows', 'cols'), 0, 0, tiled=True)  11.1 us
    pallas_call x1, Pallas kernels, per_device(): pl.pallas_call(inner_kernel, out_shape=[work, work, work, pltpu.VMEM((9 *...  5.69 us
    ppermute x3, starting transfers between devices, swap_strips(): arrived.append(lax.ppermute(piece, device_axes, pairs) if pairs else piece)  3.29 us
    ppermute x1, starting transfers between devices, per_device(): far_rows = lax.ppermute(far, ('groups',) + device_axes, far_all)  2.58 us
    pallas_call x1, Pallas kernels, per_device(): pl.pallas_call(late, out_shape=jax.ShapeDtypeStruct((height, width), f32)...  2.54 us
    pallas_call x1, Pallas kernels, per_device(): pl.pallas_call(outer, out_shape=[work, work, work, pltpu.VMEM((tile_count...  2.44 us
    pallas_call x1, Pallas kernels, per_device(): pl.pallas_call(edge_kernel, out_shape=[sent, sent, strip, strip], in_spec...  2.43 us
    ppermute x3, waiting for transfers between devices, swap_strips(): arrived.append(lax.ppermute(piece, device_axes, pairs) if pairs else piece)  1.71 us
  transfers between devices with their start and end apart: 6, of which 2 were waited for; matrix products, arithmetic and copies ran while one was open for 0% of the time, Pallas kernels for 17%

profile of v2, /device:TPU:0, one launch (start us, length us, event | category | flops | bytes accessed | tf_op | source)
XLA Modules:
  0.0 33.6 jit_solution(3523765796933371320)
XLA Ops:
  0.0 2.4 %edge_rows.1 = (f32[1472,128]{1,0:T(8,128)S(1)}, f32[1472,128]{1,0:T(8,128)S(1)}, f32[32,128]{1,0:T(8,128)S(1)}, f32[32,128]{1,0:T(8,128)S(1)}) custom-call(f32[16,8192]{1,0:T(8,128)} %ground_hbm.3, f32[16,8192]{1,0:T(8,128)} %depth_hbm.3, s32[2,8192]{1,0:T(2,128)} %rows_hbm.3, s32[2,16]{1,0:T(2,128)} %sides_hbm.3), custom_call_target="tpu_custom_call" | custom-call | flops 1024 | bytes 1024 | tf_op jit(solution)/shard_map/edge_rows/pallas_call | solution.py:537
  2.4 0.5 %collective-permute-start.2 = (f32[1472,128]{1,0:T(8,128)S(1)}, f32[1472,128]{1,0:T(8,128)S(1)}, u32[]{:S(2)}, u32[]{:S(2)}) collective-permute-start(f32[1472,128]{1,0:T(8,128)S(1)} %get-tuple-element.19), channel_id=1, source_target_pairs={{0,1},{1,0},{4,5},{5,4},{8,9},{9,8},{12,13},{13,12},{2,3},{3,2},{6... | collective-permute-start | bytes 2261000 | tf_op jit(solution)/shard_map/ppermute | solution.py:576
  3.0 2.6 %collective-permute-start = (f32[1472,128]{1,0:T(8,128)S(1)}, f32[1472,128]{1,0:T(8,128)S(1)}, u32[]{:S(2)}, u32[]{:S(2)}) collective-permute-start(f32[1472,128]{1,0:T(8,128)S(1)} %get-tuple-element.16), channel_id=1, source_target_pairs={{1,4},{3,6},{4,1},{6,3},{5,8},{7,10},{8,5},{10,7},{9,12},{11,14},{... | collective-permute-start | bytes 2261000 | tf_op jit(solution)/shard_map/ppermute | solution.py:575
  5.6 1.3 %collective-permute-start.4 = (f32[32,128]{1,0:T(8,128)S(1)}, f32[32,128]{1,0:T(8,128)S(1)}, u32[]{:S(2)}, u32[]{:S(2)}) collective-permute-start(f32[32,128]{1,0:T(8,128)S(1)} %get-tuple-element.17), channel_id=1, source_target_pairs={{0,3},{2,1},{1,2},{3,0},{4,7},{6,5},{5,6},{7,4},{8,11},{10,9},{9,1... | collective-permute-start | bytes 49160 | tf_op jit(solution)/shard_map/ppermute | solution.py:571
  6.8 0.5 %collective-permute-start.3 = (f32[32,128]{1,0:T(8,128)S(1)}, f32[32,128]{1,0:T(8,128)S(1)}, u32[]{:S(2)}, u32[]{:S(2)}) collective-permute-start(f32[32,128]{1,0:T(8,128)S(1)} %get-tuple-element.17), channel_id=1, source_target_pairs={{0,2},{2,0},{1,3},{3,1},{4,6},{6,4},{5,7},{7,5},{8,10},{10,8},{9,1... | collective-permute-start | bytes 49160 | tf_op jit(solution)/shard_map/ppermute | solution.py:571
  7.4 1.5 %collective-permute-start.1 = (f32[32,128]{1,0:T(8,128)S(1)}, f32[32,128]{1,0:T(8,128)S(1)}, u32[]{:S(2)}, u32[]{:S(2)}) collective-permute-start(f32[32,128]{1,0:T(8,128)S(1)} %get-tuple-element.17), channel_id=1, source_target_pairs={{1,6},{3,4},{4,3},{6,1},{5,10},{7,8},{8,7},{10,5},{9,14},{11,12},{... | collective-permute-start | bytes 49160 | tf_op jit(solution)/shard_map/ppermute | solution.py:571
  8.9 0.0 collective-permute-done.4.near_even_ref
  8.9 1.7 %collective-permute-done.3.own_even_ref = f32[32,128]{1,0:T(8,128)S(1)} collective-permute-done((f32[32,128]{1,0:T(8,128)S(1)}, f32[32,128]{1,0:T(8,128)S(1)}, u32[]{:S(2)}, u32[]{:S(2)}) %collective-permute-start.3) | collective-permute-done | bytes 16416 | tf_op jit(solution)/shard_map/ppermute | solution.py:571
  10.6 0.0 collective-permute-done.2.near_ref
  10.6 5.7 %inner_passes.1 = (f32[2880,128]{1,0:T(8,128)S(1)}, f32[2880,128]{1,0:T(8,128)S(1)}, f32[2880,128]{1,0:T(8,128)S(1)}, f32[72,128]{1,0:T(8,128)S(1)}) custom-call(f32[16,8192]{1,0:T(8,128)} %ground_hbm.3, f32[16,8192]{1,0:T(8,128)} %depth_hbm.3, s32[2,8192]{1,0:T(2,128)} %rows_hbm.3, s32[2,16]{1,0:T(2,128)} %sides_hbm.3, s32[8,6]{1,0:T(8,128)} %links_hbm.1, ...), custom_call_target="tpu_custom_call" | custom-call | flops 1024 | bytes 1024 | tf_op jit(solution)/shard_map/inner_passes/pallas_call | solution.py:581
  16.3 0.0 collective-permute-done.1.refs_0_
  16.3 0.0 collective-permute-done.far_ref
  16.3 2.4 %outer_passes.1 = (f32[2880,128]{1,0:T(8,128)S(1)}, f32[2880,128]{1,0:T(8,128)S(1)}, f32[2880,128]{1,0:T(8,128)S(1)}, f32[8,128]{1,0:T(8,128)S(1)}) custom-call(f32[1472,128]{1,0:T(8,128)S(1)} %collective-permute-done.far_ref, f32[32,128]{1,0:T(8,128)S(1)} %collective-permute-done.1.refs_0_, ...), custom_call_target="tpu_custom_call", output_to_operand_aliasing={{0}: (3, {}), {1}: (4, {}), {2}: (5, {})} | custom-call | flops 1024 | bytes 1024 | tf_op jit(solution)/shard_map/outer_passes/pallas_call | solution.py:603
  18.7 0.3 %collective-permute-start.5 = (f32[8,128]{1,0:T(8,128)S(1)}, f32[8,128]{1,0:T(8,128)S(1)}, u32[]{:S(2)}, u32[]{:S(2)}) collective-permute-start(f32[8,128]{1,0:T(8,128)S(1)} %get-tuple-element.25), channel_id=1, source_target_pairs={{0,1},{1,0},{2,3},{3,2},{4,5},{5,4},{6,7},{7,6},{8,9},{9,8},{10,11... | collective-permute-start | bytes 12296 | tf_op jit(solution)/shard_map/ppermute | solution.py:616
  19.1 0.8 %collective-permute-done.5 = f32[8,128]{1,0:T(8,128)S(1)} collective-permute-done((f32[8,128]{1,0:T(8,128)S(1)}, f32[8,128]{1,0:T(8,128)S(1)}, u32[]{:S(2)}, u32[]{:S(2)}) %collective-permute-start.5) | collective-permute-done | bytes 4128 | tf_op jit(solution)/shard_map/ppermute | solution.py:616
  19.9 11.1 %all_to_all.11 = f32[8,1,128]{2,1,0:T(1,128)S(1)} all-to-all(f32[8,1,128]{2,1,0:T(1,128)S(1)} %bitcast.5), channel_id=1, replica_groups=mesh['groups'=2,'rows'=4,'cols'=2,'sub'=2] {'rows','cols'}, dimensions={0} | all-to-all | bytes 8192 | tf_op jit(solution)/shard_map/all_to_all | solution.py:617
  31.0 2.5 %final_passes.1 = f32[16,8192]{1,0:T(8,128)} custom-call(f32[2880,128]{1,0:T(8,128)S(1)} %get-tuple-element.23.refs_0_, f32[2880,128]{1,0:T(8,128)S(1)} %get-tuple-element.24.refs_1_, f32[8,128]{1,0:T(8,128)S(1)} %bitcast.4, f32[72,128]{1,0:T(8,128)S(1)} %get-tuple-element.26.refs_3_), custom_call_target="tpu_custom_call" | custom-call | flops 1024 | bytes 1024 | tf_op jit(solution)/shard_map/final_passes/pallas_call | solution.py:622
  (1 shorter events, 0.0 us)
Async XLA Ops:
  2.4 8.1 %collective-permute-start.2 = (f32[1472,128]{1,0:T(8,128)S(1)}, f32[1472,128]{1,0:T(8,128)S(1)}, u32[]{:S(2)}, u32[]{:S(2)}) collective-permute-start(f32[1472,128]{1,0:T(8,128)S(1)} %get-tuple-element.19), channel_id=1, source_target_pairs={{0,1},{1,0},{4,5},{5,4},{8,9},{9,8},{12,13},{13,12},{2,3},{3,2},{6... | collective-permute-start | bytes 2261000 | tf_op jit(solution)/shard_map/ppermute | solution.py:576
  3.0 13.3 %collective-permute-start = (f32[1472,128]{1,0:T(8,128)S(1)}, f32[1472,128]{1,0:T(8,128)S(1)}, u32[]{:S(2)}, u32[]{:S(2)}) collective-permute-start(f32[1472,128]{1,0:T(8,128)S(1)} %get-tuple-element.16), channel_id=1, source_target_pairs={{1,4},{3,6},{4,1},{6,3},{5,8},{7,10},{8,5},{10,7},{9,12},{11,14},{... | collective-permute-start | bytes 2261000 | tf_op jit(solution)/shard_map/ppermute | solution.py:575
  5.6 3.3 %collective-permute-start.4 = (f32[32,128]{1,0:T(8,128)S(1)}, f32[32,128]{1,0:T(8,128)S(1)}, u32[]{:S(2)}, u32[]{:S(2)}) collective-permute-start(f32[32,128]{1,0:T(8,128)S(1)} %get-tuple-element.17), channel_id=1, source_target_pairs={{0,3},{2,1},{1,2},{3,0},{4,7},{6,5},{5,6},{7,4},{8,11},{10,9},{9,1... | collective-permute-start | bytes 49160 | tf_op jit(solution)/shard_map/ppermute | solution.py:571
  6.8 3.7 %collective-permute-start.3 = (f32[32,128]{1,0:T(8,128)S(1)}, f32[32,128]{1,0:T(8,128)S(1)}, u32[]{:S(2)}, u32[]{:S(2)}) collective-permute-start(f32[32,128]{1,0:T(8,128)S(1)} %get-tuple-element.17), channel_id=1, source_target_pairs={{0,2},{2,0},{1,3},{3,1},{4,6},{6,4},{5,7},{7,5},{8,10},{10,8},{9,1... | collective-permute-start | bytes 49160 | tf_op jit(solution)/shard_map/ppermute | solution.py:571
  7.4 8.9 %collective-permute-start.1 = (f32[32,128]{1,0:T(8,128)S(1)}, f32[32,128]{1,0:T(8,128)S(1)}, u32[]{:S(2)}, u32[]{:S(2)}) collective-permute-start(f32[32,128]{1,0:T(8,128)S(1)} %get-tuple-element.17), channel_id=1, source_target_pairs={{1,6},{3,4},{4,3},{6,1},{5,10},{7,8},{8,7},{10,5},{9,14},{11,12},{... | collective-permute-start | bytes 49160 | tf_op jit(solution)/shard_map/ppermute | solution.py:571
  18.7 1.2 %collective-permute-start.5 = (f32[8,128]{1,0:T(8,128)S(1)}, f32[8,128]{1,0:T(8,128)S(1)}, u32[]{:S(2)}, u32[]{:S(2)}) collective-permute-start(f32[8,128]{1,0:T(8,128)S(1)} %get-tuple-element.25), channel_id=1, source_target_pairs={{0,1},{1,0},{2,3},{3,2},{4,5},{5,4},{6,7},{7,6},{8,9},{9,8},{10,11... | collective-permute-start | bytes 12296 | tf_op jit(solution)/shard_map/ppermute | solution.py:616

commit v3 on v1

--- a/solution.py
+++ b/solution.py
@@ -8,7 +8,7 @@
 PASSES = 8
 FINAL = 4
 ROUNDS = 4
-HALO = PASSES + FINAL
+HALO = PASSES
 SUBS = 8
 LANES = 128
 AHEAD = 5
@@ -89,73 +89,32 @@
 
 def edge_kernel(
     ground_hbm, depth_hbm, rows_hbm, sides_hbm,
-    far_ref, near_ref, even_ref, odd_ref,
-    ground_ref, depth_ref, marks_ref, sides_ref, sems, small_sems,
+    far_ref, near_ref, even_ref, odd_ref, ground_out, surface_out,
+    ground_ref, depth_ref, rows_ref, sides_ref, sems, small_sems,
 ):
     height, width = ground_hbm.shape
-    groups = height // SUBS
-    last_tile = width // LANES - 1
-    place, places = chain_place()
-    col, cols = lax.axis_index("cols"), lax.axis_size("cols")
-    small = [pltpu.make_async_copy(sides_hbm, sides_ref, small_sems.at[0])]
-    for side, tile in enumerate((0, last_tile)):
-        columns = pl.ds(tile * LANES, LANES)
-        small.append(pltpu.make_async_copy(rows_hbm.at[:, columns], marks_ref.at[side], small_sems.at[1 + side]))
+    tiles = width // (SUBS * LANES)
+    small = [
+        pltpu.make_async_copy(rows_hbm, rows_ref, small_sems.at[0]),
+        pltpu.make_async_copy(sides_hbm, sides_ref, small_sems.at[1]),
+    ]
+    start_all(small[1:])
     copies = start_own(ground_hbm, depth_hbm, ground_ref, depth_ref, sems)
-    start_all(small)
-    sub, lane = position()
+    start_all(small[:1])
     wait_all(small)
-    marks = side_marks(sides_ref)
-    at_edges = [(lane == 0) & (col == 0), (lane == LANES - 1) & (col == cols - 1)]
-    for copy in copies:
-        wait_all(copy)
-
-    def raised(group, tile):
-        rows, columns = pl.ds(group * SUBS, SUBS), pl.ds(tile * LANES, LANES)
-        ground = ground_ref[rows, columns]
-        surface = ground + depth_ref[rows, columns]
-        if tile in (0, last_tile):
-            side = 0 if tile == 0 else 1
-            chosen = marks[side][group * SUBS : (group + 1) * SUBS]
-            surface = jnp.where((chosen > 0.5) & at_edges[side], ground, surface)
-        return ground, surface
-
-    def pack(up_ref, down_ref):
-        tiles = width // (SUBS * LANES)
-        size = tiles * SUBS
-        skipped = height - HALO
-        for tile in range(last_tile + 1):
-            start = tile % tiles * SUBS + tile // tiles
-            for out_ref, ground_slot, surface_slot, shift, keep in (
-                (up_ref, 0, HALO - 1, 0, range(0, HALO)),
-                (down_ref, HALO - 1, 0, skipped, range(skipped, height)),
-            ):
-                values = [raised(group, tile) for group in range(groups)]
-                for kind, slot in enumerate((ground_slot, surface_slot)):
-                    for group in range(groups):
-                        inside = [row for row in range(group * SUBS, (group + 1) * SUBS) if row in keep]
-                        first, count = inside[0], len(inside)
-                        offset = first - group * SUBS
-                        row = slot + first - shift
-                        out_ref[pl.ds(row * size + start, count, stride=size), :] = values[group][kind][
-                            offset : offset + count
-                        ]
-
+    edges = fold_own(copies, ground_ref, depth_ref, rows_ref, sides_ref, ground_out, surface_out)
+    place, _ = chain_place()
     top = place % 2 == 0
-    pl.when(top)(lambda: pack(far_ref, near_ref))
-    pl.when(jnp.logical_not(top))(lambda: pack(near_ref, far_ref))
-    rightward = col % 2 == 0
-    for group in range(groups):
-        values = []
-        for side, tile in enumerate((0, last_tile)):
-            ground, surface = raised(group, tile)
-            if group == 0:
-                outlet = (marks_ref[side, 0:1] == 1) & (sub == 0) & (place == 0)
-                surface = jnp.where(outlet, ground, surface)
-            if group == groups - 1:
-                outlet = (marks_ref[side, 1:2] == 1) & (sub == SUBS - 1) & (place == places - 1)
-                surface = jnp.where(outlet, ground, surface)
-            values.append((ground, surface))
+    size, packed = (tiles + 1) * SUBS, tiles * SUBS
+    for out_ref, is_top in ((far_ref, top), (near_ref, jnp.logical_not(top))):
+        first = HALO + jnp.where(is_top, 0, height - HALO)
+        bases = (jnp.where(is_top, 0, HALO - 1), jnp.where(is_top, HALO - 1, 0))
+        for source, base in zip((ground_out, surface_out), bases):
+            for row in range(HALO):
+                for slot in range(tiles):
+                    out_ref[register(base + row, slot, packed), :] = source[register(first + row, slot, size), :]
+    rightward = lax.axis_index("cols") % 2 == 0
+    for group, values in enumerate(edges):
         for kind in range(2):
             rows = pl.ds(kind * height + group * SUBS, SUBS)
             even_ref[rows, :] = jnp.where(rightward, values[1][kind], values[0][kind])
@@ -195,6 +154,7 @@
     col, cols = lax.axis_index("cols"), lax.axis_size("cols")
     sub, lane = position()
     marks = side_marks(sides_ref)
+    edges = [[] for _ in range(groups)]
     for group in range(groups):
         rows = pl.ds(group * SUBS, SUBS)
         for tile in range(last_tile + 1):
@@ -226,6 +186,9 @@
             start = (HALO + group * SUBS) * size + slot * SUBS + chunk
             ground_out[pl.ds(start, SUBS, stride=size), :] = ground
             surface_out[pl.ds(start, SUBS, stride=size), :] = surface
+            if tile in (0, last_tile):
+                edges[group].append((ground, surface))
+    return edges
 
 
 def unpack_rows(rows_ref, first, is_top, present, strip_refs, strip_rows, ground_ref, surface_ref, tiles):
@@ -335,22 +298,11 @@
 
 
 def inner_kernel(
-    ground_hbm, depth_hbm, rows_hbm, sides_hbm, links_hbm,
-    near_ref, own_even_ref, own_odd_ref, near_even_ref, near_odd_ref,
-    ground_ref, surface_ref, other_ref, hops_ref,
-    raw_ground_ref, raw_depth_ref, rows_ref, sides_ref, links_ref, sems, small_sems,
+    height, tiles, links_hbm, near_ref, own_even_ref, own_odd_ref, near_even_ref, near_odd_ref, *refs
 ):
-    height, width = ground_hbm.shape
-    tiles = width // (SUBS * LANES)
-    small = start_all(
-        [
-            pltpu.make_async_copy(source, target, small_sems.at[number])
-            for number, (source, target) in enumerate(
-                ((rows_hbm, rows_ref), (sides_hbm, sides_ref), (links_hbm, links_ref))
-            )
-        ]
-    )
-    copies = start_own(ground_hbm, depth_hbm, raw_ground_ref, raw_depth_ref, sems)
+    ground_ref, surface_ref, other_ref, hops_ref, links_ref, sem = refs[2:]
+    links = pltpu.make_async_copy(links_hbm, links_ref, sem)
+    links.start()
     own_strips, near_strips = (own_even_ref, own_odd_ref), (near_even_ref, near_odd_ref)
     ring = tiles + 1
     size = ring * SUBS
@@ -368,9 +320,8 @@
         surface_ref,
         tiles,
     )
-    wait_all(small)
+    links.wait()
     hop_counts(links_ref, hops_ref, needed_tiles())
-    fold_own(copies, raw_ground_ref, raw_depth_ref, rows_ref, sides_ref, ground_ref, surface_ref)
     for kind, out_ref in enumerate((ground_ref, surface_ref)):
 
         def body(row, carry):
@@ -390,7 +341,7 @@
 
 
 def outer_kernel(height, tiles, far_ref, even_ref, odd_ref, *refs):
-    ground_ref, surface_ref, other_ref, level_ref = refs[3:7]
+    ground_ref, surface_ref, other_ref, level_ref, far_out, near_out = refs[3:9]
     ring = tiles + 1
     size = ring * SUBS
     place, places = chain_place()
@@ -411,6 +362,12 @@
     for step in range(1, PASSES + 1):
         first = jnp.where(top, step, HALO + height - step)
         relax_rows(buffers[(step + 1) % 2], buffers[step % 2], ground_ref, first, HALO, ring)
+    low, high = HALO, HALO + height - FINAL
+    for row in range(FINAL):
+        for slot in range(ring):
+            where = register(row, slot, size)
+            far_out[where, :] = surface_ref[register(jnp.where(top, low, high) + row, slot, size), :]
+            near_out[where, :] = surface_ref[register(jnp.where(top, high, low) + row, slot, size), :]
     band, bands = lax.axis_index("sub"), lax.axis_size("sub")
     sub, lane = position()
 
@@ -448,7 +405,7 @@
 
 
 def late_kernel(
-    height, tiles, ground_ref, surface_ref, floors_ref, hops_ref, out_hbm,
+    height, tiles, ground_ref, surface_ref, far_ref, near_ref, floors_ref, hops_ref, out_hbm,
     one_ref, two_ref, out_ref, sems,
 ):
     ring = tiles + 1
@@ -477,13 +434,23 @@
             jnp.where(sub == 0, left, middle),
         )
         pairs.append((middle, seam))
-    spans = ((HALO - FINAL, FINAL), (HALO, height), (HALO + height, FINAL))
-    for (first, rows), (middle, seam) in zip(spans, pairs):
+    place, _ = chain_place()
+    top = place % 2 == 0
+    low, high = HALO - FINAL, HALO + height
+    far_pair = [jnp.where(top, above, below) for above, below in zip(pairs[0], pairs[2])]
+    near_pair = [jnp.where(top, below, above) for above, below in zip(pairs[0], pairs[2])]
+    spans = (
+        (surface_ref, HALO, HALO, height, pairs[1]),
+        (near_ref, 0, jnp.where(top, high, low), FINAL, near_pair),
+        (far_ref, 0, jnp.where(top, low, high), FINAL, far_pair),
+    )
+    for source, source_first, first, rows, (middle, seam) in spans:
 
         def body(row, carry):
             for slot in range(ring):
+                value = source[register(source_first + row, slot, size), :]
+                value = jnp.minimum(value, seam if slot == tiles else middle)
                 where = register(first + row, slot, size)
-                value = jnp.minimum(surface_ref[where, :], seam if slot == tiles else middle)
                 one_ref[where, :] = jnp.maximum(ground_ref[where, :], value)
             return carry
 
@@ -535,18 +502,19 @@
     ]
     sent = pltpu.VMEM(((2 * HALO - 1) * packed, LANES), f32)
     strip = pltpu.VMEM((2 * height, LANES), f32)
-    far, near, even, odd = pl.pallas_call(
+    work = pltpu.VMEM(((height + 2 * HALO) * size, LANES), f32)
+    far, near, even, odd, ground, surface = pl.pallas_call(
         edge_kernel,
-        out_shape=[sent, sent, strip, strip],
+        out_shape=[sent, sent, strip, strip, work, work],
         in_specs=in_hbm(4),
-        out_specs=in_vmem(4),
+        out_specs=in_vmem(6),
         scratch_shapes=[
             pltpu.VMEM((height, width), f32),
             pltpu.VMEM((height, width), f32),
-            pltpu.VMEM((2, 2, LANES), jnp.int32),
+            pltpu.VMEM(edge_rows.shape, jnp.int32),
             pltpu.VMEM(edge_sides.shape, jnp.int32),
             pltpu.SemaphoreType.DMA((2, 4 * groups)),
-            pltpu.SemaphoreType.DMA((3,)),
+            pltpu.SemaphoreType.DMA((2,)),
         ],
         compiler_params=limit,
         cost_estimate=short,
@@ -577,42 +545,39 @@
     near_rows = lax.ppermute(near, ("rows", "sub"), near_pairs)
     strips = swap_strips((even, odd), stay) + swap_strips((even, odd), near_pairs)
 
-    work = pltpu.VMEM(((height + 2 * HALO) * size, LANES), f32)
-    work_scratch = pltpu.VMEM(((height + 2 * HALO) * size, LANES), f32)
+    def inner(*refs):
+        inner_kernel(height, tiles, *refs)
+
     ground, surface, other, hops = pl.pallas_call(
-        inner_kernel,
+        inner,
         out_shape=[work, work, work, pltpu.VMEM((9 * tile_count, LANES), f32)],
-        in_specs=in_hbm(5) + in_vmem(5),
+        in_specs=in_hbm(1) + in_vmem(7),
         out_specs=in_vmem(4),
-        scratch_shapes=[
-            pltpu.VMEM((height, width), f32),
-            pltpu.VMEM((height, width), f32),
-            pltpu.VMEM(edge_rows.shape, jnp.int32),
-            pltpu.VMEM(edge_sides.shape, jnp.int32),
-            pltpu.VMEM(adjacency.shape, jnp.int32),
-            pltpu.SemaphoreType.DMA((2, 4 * groups)),
-            pltpu.SemaphoreType.DMA((3,)),
-        ],
+        scratch_shapes=[pltpu.VMEM(adjacency.shape, jnp.int32), pltpu.SemaphoreType.DMA],
+        input_output_aliases={6: 0, 7: 1},
         compiler_params=limit,
         cost_estimate=short,
         name="inner_passes",
-    )(*arguments, near_rows, *strips)
+    )(arguments[4], near_rows, *strips, ground, surface)
 
     def outer(far_ref, *refs):
         outer_kernel(height, tiles, far_ref, *refs)
 
     devices = lax.axis_size(device_axes)
-    ground, surface, other, floors = pl.pallas_call(
+    again = pltpu.VMEM((FINAL * size, LANES), f32)
+    ground, surface, other, floors, far, near = pl.pallas_call(
         outer,
-        out_shape=[work, work, work, pltpu.VMEM((devices, LANES), f32)],
+        out_shape=[work, work, work, pltpu.VMEM((devices, LANES), f32), again, again],
         in_specs=in_vmem(6),
-        out_specs=in_vmem(4),
+        out_specs=in_vmem(6),
         input_output_aliases={3: 0, 4: 1, 5: 2},
         compiler_params=limit,
         cost_estimate=short,
         name="outer_passes",
     )(far_rows, *far_strips, ground, surface, other)
 
+    far_rows = lax.ppermute(far, ("groups",) + device_axes, far_all)
+    near_rows = lax.ppermute(near, ("rows", "sub"), near_pairs)
     floors = lax.all_to_all(floors, device_axes, 0, 0, tiled=True)
 
     def late(*refs):
@@ -621,18 +586,18 @@
     return pl.pallas_call(
         late,
         out_shape=jax.ShapeDtypeStruct((height, width), f32),
-        in_specs=in_vmem(4),
+        in_specs=in_vmem(6),
         out_specs=pl.BlockSpec(memory_space=pltpu.HBM),
         scratch_shapes=[
-            work_scratch,
-            work_scratch,
+            work,
+            work,
             pltpu.VMEM((height, width), f32),
             pltpu.SemaphoreType.DMA((groups,)),
         ],
         compiler_params=limit,
         cost_estimate=short,
         name="final_passes",
-    )(ground, surface, floors, hops)
+    )(ground, surface, far_rows, near_rows, floors, hops)
 
 
 def solution(mesh):

time: 32.7 us -> 30.6 us (0.936)
  Pallas kernels: 13.1 us -> 10.4 us
  starting transfers between devices: 6.4 us -> 8.14 us
  blocking collectives: 11.2 us -> 10.1 us
    pallas_call x2, Pallas kernels: 8.13 us -> 5.94 us  [the longest x1 4.07 us: per_device(): pl.pallas_call(inner, out_shape=[work, work, work, pltpu.VMEM((9 * tile_c...]
    ppermute x1 -> x2, starting transfers between devices: 2.58 us -> 4.15 us  [per_device(): far_rows = lax.ppermute(far, ('groups',) + device_axes, far_all)]
    all_to_all x1, blocking collectives: 11.2 us -> 10.1 us  [per_device(): floors = lax.all_to_all(floors, device_axes, 0, 0, tiled=True)]
    pallas_call x1, Pallas kernels: 2.44 us -> 1.83 us  [per_device(): pl.pallas_call(outer, out_shape=[work, work, work, pltpu.VMEM((devices, L...]
    ppermute x1 -> x2, starting transfers between devices: 0.53 us -> 0.69 us  [per_device(): near_rows = lax.ppermute(near, ('rows', 'sub'), near_pairs)]
  transfers between devices with their start and end apart: 5 -> 7, of which waited for: 1 -> 1; matrix products, arithmetic and copies ran while one was open for 0% -> 0% of each run, Pallas kernels for 18% -> 13%
where the time goes in v3:
time: 30.6 us; the launch traced here: 30.4 us
  Pallas kernels  10.4 us (34%)
  blocking collectives  10.1 us (33%)
  starting transfers between devices  8.14 us (27%)
  waiting for transfers between devices  1.72 us (6%)
    all_to_all x1, blocking collectives, per_device(): floors = lax.all_to_all(floors, device_axes, 0, 0, tiled=True)  10.1 us
    ppermute x2, starting transfers between devices, per_device(): far_rows = lax.ppermute(far, ('groups',) + device_axes, far_all)  4.15 us
    pallas_call x1, Pallas kernels, per_device(): pl.pallas_call(inner, out_shape=[work, work, work, pltpu.VMEM((9 * tile_c...  4.07 us
    ppermute x3, starting transfers between devices, swap_strips(): arrived.append(lax.ppermute(piece, device_axes, pairs) if pairs else piece)  3.29 us
    pallas_call x1, Pallas kernels, per_device(): pl.pallas_call(late, out_shape=jax.ShapeDtypeStruct((height, width), f32)...  2.59 us
    pallas_call x1, Pallas kernels, per_device(): pl.pallas_call(edge_kernel, out_shape=[sent, sent, strip, strip, work, wo...  1.87 us
    pallas_call x1, Pallas kernels, per_device(): pl.pallas_call(outer, out_shape=[work, work, work, pltpu.VMEM((devices, L...  1.83 us
    ppermute x3, waiting for transfers between devices, swap_strips(): arrived.append(lax.ppermute(piece, device_axes, pairs) if pairs else piece)  1.71 us
  transfers between devices with their start and end apart: 7, of which 1 were waited for; matrix products, arithmetic and copies ran while one was open for 0% of the time, Pallas kernels for 13%

profile of v3, /device:TPU:0, one launch (start us, length us, event | category | flops | bytes accessed | tf_op | source)
XLA Modules:
  0.0 30.4 jit_solution(8229847918838422054)
XLA Ops:
  0.0 1.9 %edge_rows.1 = (f32[960,128]{1,0:T(8,128)S(1)}, f32[960,128]{1,0:T(8,128)S(1)}, f32[32,128]{1,0:T(8,128)S(1)}, f32[32,128]{1,0:T(8,128)S(1)}, f32[2304,128]{1,0:T(8,128)S(1)}, /*index=5*/f32[2304,128]{1,0:T(8,128)S(1)}) custom-call(f32[16,8192]{1,0:T(8,128)} %ground_hbm.1, f32[16,8192]{1,0:T(8,128)} %depth_hbm.1, s32[2,8192]{1,0:T(2,128)} %rows_hbm.1, ...), custom_call_target="tpu_custom_call" | custom-call | flops 1024 | bytes 1024 | tf_op jit(solution)/shard_map/edge_rows/pallas_call | solution.py:506
  1.9 0.5 %collective-permute-start.2 = (f32[960,128]{1,0:T(8,128)S(1)}, f32[960,128]{1,0:T(8,128)S(1)}, u32[]{:S(2)}, u32[]{:S(2)}) collective-permute-start(f32[960,128]{1,0:T(8,128)S(1)} %get-tuple-element.23), channel_id=1, source_target_pairs={{0,1},{1,0},{4,5},{5,4},{8,9},{9,8},{12,13},{13,12},{2,3},{3,2},{6... | collective-permute-start | bytes 1474568 | tf_op jit(solution)/shard_map/ppermute | solution.py:545
  2.4 2.6 %collective-permute-start = (f32[960,128]{1,0:T(8,128)S(1)}, f32[960,128]{1,0:T(8,128)S(1)}, u32[]{:S(2)}, u32[]{:S(2)}) collective-permute-start(f32[960,128]{1,0:T(8,128)S(1)} %get-tuple-element.20), channel_id=1, source_target_pairs={{1,4},{3,6},{4,1},{6,3},{5,8},{7,10},{8,5},{10,7},{9,12},{11,14},{... | collective-permute-start | bytes 1474568 | tf_op jit(solution)/shard_map/ppermute | solution.py:544
  5.0 1.3 %collective-permute-start.4 = (f32[32,128]{1,0:T(8,128)S(1)}, f32[32,128]{1,0:T(8,128)S(1)}, u32[]{:S(2)}, u32[]{:S(2)}) collective-permute-start(f32[32,128]{1,0:T(8,128)S(1)} %get-tuple-element.21), channel_id=1, source_target_pairs={{0,3},{2,1},{1,2},{3,0},{4,7},{6,5},{5,6},{7,4},{8,11},{10,9},{9,1... | collective-permute-start | bytes 49160 | tf_op jit(solution)/shard_map/ppermute | solution.py:540
  6.3 0.5 %collective-permute-start.3 = (f32[32,128]{1,0:T(8,128)S(1)}, f32[32,128]{1,0:T(8,128)S(1)}, u32[]{:S(2)}, u32[]{:S(2)}) collective-permute-start(f32[32,128]{1,0:T(8,128)S(1)} %get-tuple-element.21), channel_id=1, source_target_pairs={{0,2},{2,0},{1,3},{3,1},{4,6},{6,4},{5,7},{7,5},{8,10},{10,8},{9,1... | collective-permute-start | bytes 49160 | tf_op jit(solution)/shard_map/ppermute | solution.py:540
  6.8 1.5 %collective-permute-start.1 = (f32[32,128]{1,0:T(8,128)S(1)}, f32[32,128]{1,0:T(8,128)S(1)}, u32[]{:S(2)}, u32[]{:S(2)}) collective-permute-start(f32[32,128]{1,0:T(8,128)S(1)} %get-tuple-element.21), channel_id=1, source_target_pairs={{1,6},{3,4},{4,3},{6,1},{5,10},{7,8},{8,7},{10,5},{9,14},{11,12},{... | collective-permute-start | bytes 49160 | tf_op jit(solution)/shard_map/ppermute | solution.py:540
  8.3 0.0 collective-permute-done.4.refs_4_
  8.3 1.7 %collective-permute-done.3.refs_2_ = f32[32,128]{1,0:T(8,128)S(1)} collective-permute-done((f32[32,128]{1,0:T(8,128)S(1)}, f32[32,128]{1,0:T(8,128)S(1)}, u32[]{:S(2)}, u32[]{:S(2)}) %collective-permute-start.3) | collective-permute-done | bytes 16416 | tf_op jit(solution)/shard_map/ppermute | solution.py:540
  10.0 0.0 collective-permute-done.2.refs_1_
  10.0 4.1 %inner_passes.1 = (f32[2304,128]{1,0:T(8,128)S(1)}, f32[2304,128]{1,0:T(8,128)S(1)}, f32[2304,128]{1,0:T(8,128)S(1)}, f32[72,128]{1,0:T(8,128)S(1)}) custom-call(s32[8,6]{1,0:T(8,128)} %refs_0_.1, f32[960,128]{1,0:T(8,128)S(1)} %collective-permute-done.2.refs_1_, ...), custom_call_target="tpu_custom_call", output_to_operand_aliasing={{0}: (6, {}), {1}: (7, {})} | custom-call | flops 1024 | bytes 1024 | tf_op jit(solution)/shard_map/inner_passes/pallas_call | solution.py:551
  14.1 0.0 collective-permute-done.1.refs_0_
  14.1 0.0 collective-permute-done.far_ref
  14.1 1.8 %outer_passes.1 = (f32[2304,128]{1,0:T(8,128)S(1)}, f32[2304,128]{1,0:T(8,128)S(1)}, f32[2304,128]{1,0:T(8,128)S(1)}, f32[16,128]{1,0:T(8,128)S(1)}, f32[288,128]{1,0:T(8,128)S(1)}, /*index=5*/f32[288,128]{1,0:T(8,128)S(1)}) custom-call(f32[960,128]{1,0:T(8,128)S(1)} %collective-permute-done.far_ref, ...), custom_call_target="tpu_custom_call", output_to_operand_aliasing={{0}: (3, {}), {1}: (4, {}), {2}: (5, {})} | custom-call | flops 1024 | bytes 1024 | tf_op jit(solution)/shard_map/outer_passes/pallas_call | solution.py:568
  15.9 1.6 %collective-permute-start.5 = (f32[288,128]{1,0:T(8,128)S(1)}, f32[288,128]{1,0:T(8,128)S(1)}, u32[]{:S(2)}, u32[]{:S(2)}) collective-permute-start(f32[288,128]{1,0:T(8,128)S(1)} %get-tuple-element.31), channel_id=1, source_target_pairs={{1,4},{3,6},{4,1},{6,3},{5,8},{7,10},{8,5},{10,7},{9,12},{11,14},{... | collective-permute-start | bytes 442376 | tf_op jit(solution)/shard_map/ppermute | solution.py:579
  17.5 0.2 collective-permute-start.6
  17.7 10.1 %all_to_all.11 = f32[16,1,128]{2,1,0:T(1,128)S(1)} all-to-all(f32[16,1,128]{2,1,0:T(1,128)S(1)} %bitcast.5), channel_id=1, replica_groups=mesh['groups'=2,'rows'=4,'cols'=2,'sub'=2] {'rows','cols','sub'}, dimensions={0} | all-to-all | bytes 16384 | tf_op jit(solution)/shard_map/all_to_all | solution.py:581
  27.8 0.0 collective-permute-done.5.refs_2_
  27.8 0.0 collective-permute-done.6.refs_3_
  27.8 2.6 %final_passes.1 = f32[16,8192]{1,0:T(8,128)} custom-call(f32[2304,128]{1,0:T(8,128)S(1)} %get-tuple-element.29.refs_0_, f32[2304,128]{1,0:T(8,128)S(1)} %get-tuple-element.30.refs_1_, f32[288,128]{1,0:T(8,128)S(1)} %collective-permute-done.5.refs_2_, f32[288,128]{1,0:T(8,128)S(1)} %collective-permute-done.6.refs_3_, f32[16,128]{1,0:T(8,128)S(1)} %bitcast.4, ...), custom_call_target="tpu_custom_call" | custom-call | flops 1024 | bytes 1024 | tf_op jit(solution)/shard_map/final_passes/pallas_call | solution.py:586
Async XLA Ops:
  1.9 8.1 %collective-permute-start.2 = (f32[960,128]{1,0:T(8,128)S(1)}, f32[960,128]{1,0:T(8,128)S(1)}, u32[]{:S(2)}, u32[]{:S(2)}) collective-permute-start(f32[960,128]{1,0:T(8,128)S(1)} %get-tuple-element.23), channel_id=1, source_target_pairs={{0,1},{1,0},{4,5},{5,4},{8,9},{9,8},{12,13},{13,12},{2,3},{3,2},{6... | collective-permute-start | bytes 1474568 | tf_op jit(solution)/shard_map/ppermute | solution.py:545
  2.4 11.7 %collective-permute-start = (f32[960,128]{1,0:T(8,128)S(1)}, f32[960,128]{1,0:T(8,128)S(1)}, u32[]{:S(2)}, u32[]{:S(2)}) collective-permute-start(f32[960,128]{1,0:T(8,128)S(1)} %get-tuple-element.20), channel_id=1, source_target_pairs={{1,4},{3,6},{4,1},{6,3},{5,8},{7,10},{8,5},{10,7},{9,12},{11,14},{... | collective-permute-start | bytes 1474568 | tf_op jit(solution)/shard_map/ppermute | solution.py:544
  5.0 3.3 %collective-permute-start.4 = (f32[32,128]{1,0:T(8,128)S(1)}, f32[32,128]{1,0:T(8,128)S(1)}, u32[]{:S(2)}, u32[]{:S(2)}) collective-permute-start(f32[32,128]{1,0:T(8,128)S(1)} %get-tuple-element.21), channel_id=1, source_target_pairs={{0,3},{2,1},{1,2},{3,0},{4,7},{6,5},{5,6},{7,4},{8,11},{10,9},{9,1... | collective-permute-start | bytes 49160 | tf_op jit(solution)/shard_map/ppermute | solution.py:540
  6.3 3.7 %collective-permute-start.3 = (f32[32,128]{1,0:T(8,128)S(1)}, f32[32,128]{1,0:T(8,128)S(1)}, u32[]{:S(2)}, u32[]{:S(2)}) collective-permute-start(f32[32,128]{1,0:T(8,128)S(1)} %get-tuple-element.21), channel_id=1, source_target_pairs={{0,2},{2,0},{1,3},{3,1},{4,6},{6,4},{5,7},{7,5},{8,10},{10,8},{9,1... | collective-permute-start | bytes 49160 | tf_op jit(solution)/shard_map/ppermute | solution.py:540
  6.8 7.3 %collective-permute-start.1 = (f32[32,128]{1,0:T(8,128)S(1)}, f32[32,128]{1,0:T(8,128)S(1)}, u32[]{:S(2)}, u32[]{:S(2)}) collective-permute-start(f32[32,128]{1,0:T(8,128)S(1)} %get-tuple-element.21), channel_id=1, source_target_pairs={{1,6},{3,4},{4,3},{6,1},{5,10},{7,8},{8,7},{10,5},{9,14},{11,12},{... | collective-permute-start | bytes 49160 | tf_op jit(solution)/shard_map/ppermute | solution.py:540
  15.9 11.9 %collective-permute-start.5 = (f32[288,128]{1,0:T(8,128)S(1)}, f32[288,128]{1,0:T(8,128)S(1)}, u32[]{:S(2)}, u32[]{:S(2)}) collective-permute-start(f32[288,128]{1,0:T(8,128)S(1)} %get-tuple-element.31), channel_id=1, source_target_pairs={{1,4},{3,6},{4,1},{6,3},{5,8},{7,10},{8,5},{10,7},{9,12},{11,14},{... | collective-permute-start | bytes 442376 | tf_op jit(solution)/shard_map/ppermute | solution.py:579
  17.5 10.3 %collective-permute-start.6 = (f32[288,128]{1,0:T(8,128)S(1)}, f32[288,128]{1,0:T(8,128)S(1)}, u32[]{:S(2)}, u32[]{:S(2)}) collective-permute-start(f32[288,128]{1,0:T(8,128)S(1)} %get-tuple-element.32), channel_id=1, source_target_pairs={{0,1},{1,0},{4,5},{5,4},{8,9},{9,8},{12,13},{13,12},{2,3},{3,2},{6... | collective-permute-start | bytes 442376 | tf_op jit(solution)/shard_map/ppermute | solution.py:580

commit v4 on v3

--- a/solution.py
+++ b/solution.py
@@ -191,11 +191,28 @@
     return edges
 
 
-def unpack_rows(rows_ref, first, is_top, present, strip_refs, strip_rows, ground_ref, surface_ref, tiles):
+def strips_of(rows_ref, tiles):
+    start = (2 * HALO - 1) * tiles * SUBS
+    return [[(rows_ref, start + (2 * parity + kind) * HALO) for parity in range(2)] for kind in range(2)]
+
+
+def append_kernel(even_ref, odd_ref, *refs):
+    height = even_ref.shape[0] // 2
+    place, _ = chain_place()
+    top = place % 2 == 0
+    for out_ref, is_top in zip(refs[2:], (top, jnp.logical_not(top))):
+        tiles = (out_ref.shape[0] - 4 * HALO) // ((2 * HALO - 1) * SUBS)
+        for kind, starts in enumerate(strips_of(out_ref, tiles)):
+            rows = pl.ds(aligned(kind * height + jnp.where(is_top, 0, height - HALO)), HALO)
+            for source, (_, start) in zip((even_ref, odd_ref), starts):
+                out_ref[pl.ds(start, HALO), :] = source[rows, :]
+
+
+def unpack_rows(rows_ref, first, is_top, present, ground_ref, surface_ref, tiles):
     packed = tiles * SUBS
     size = packed + SUBS
     bases = (jnp.where(is_top, HALO - 1, 0), jnp.where(is_top, 0, HALO - 1))
-    for base, out_ref, strip_row in zip(bases, (ground_ref, surface_ref), strip_rows):
+    for base, out_ref, strips in zip(bases, (ground_ref, surface_ref), strips_of(rows_ref, tiles)):
 
         def body(row, carry):
             values = [
@@ -204,17 +221,17 @@
             ]
             for slot in range(tiles):
                 out_ref[register(first + row, slot, size), :] = values[slot]
-            fill_seam(out_ref, first + row, values[0], values[-1], strip_refs, strip_row + row, present, tiles)
+            fill_seam(out_ref, first + row, values[0], values[-1], strips, row, present, tiles)
             return carry
 
         lax.fori_loop(0, HALO, body, 0, unroll=4)
 
 
-def fill_seam(out_ref, row, first_tile, last_tile, strip_refs, strip_row, present, tiles):
+def fill_seam(out_ref, row, first_tile, last_tile, strips, strip_row, present, tiles):
     col, cols = lax.axis_index("cols"), lax.axis_size("cols")
     sub, lane = position()
     rightward = col % 2 == 0
-    even, odd = [ref[pl.ds(strip_row, 1), :] for ref in strip_refs]
+    even, odd = [ref[pl.ds(start + strip_row, 1), :] for ref, start in strips]
     after = jnp.where(present & (col < cols - 1), jnp.where(rightward, even, odd), unreached)
     before = jnp.where(present & (col > 0), jnp.where(rightward, odd, even), unreached)
     after = jnp.where(sub == SUBS - 1, after, pltpu.roll(first_tile, SUBS - 1, 0))
@@ -297,13 +314,15 @@
     return [r * cols + c for r in (above, row, below) for c in (left, col, right)]
 
 
-def inner_kernel(
-    height, tiles, links_hbm, near_ref, own_even_ref, own_odd_ref, near_even_ref, near_odd_ref, *refs
-):
-    ground_ref, surface_ref, other_ref, hops_ref, links_ref, sem = refs[2:]
+def hops_kernel(links_hbm, after_ref, hops_ref, links_ref, sem):
     links = pltpu.make_async_copy(links_hbm, links_ref, sem)
     links.start()
-    own_strips, near_strips = (own_even_ref, own_odd_ref), (near_even_ref, near_odd_ref)
+    links.wait()
+    hop_counts(links_ref, hops_ref, needed_tiles())
+
+
+def inner_kernel(height, tiles, near_ref, even_ref, odd_ref, *refs):
+    ground_ref, surface_ref, other_ref = refs[3:]
     ring = tiles + 1
     size = ring * SUBS
     place, places = chain_place()
@@ -314,21 +333,18 @@
         jnp.where(top, HALO + height, 0),
         jnp.logical_not(top),
         has_near,
-        near_strips,
-        [kind * height + jnp.where(top, 0, height - HALO) for kind in range(2)],
         ground_ref,
         surface_ref,
         tiles,
     )
-    links.wait()
-    hop_counts(links_ref, hops_ref, needed_tiles())
     for kind, out_ref in enumerate((ground_ref, surface_ref)):
-
-        def body(row, carry):
+        strips = [(ref, kind * height) for ref in (even_ref, odd_ref)]
+
+        def body(row, carry, out_ref=out_ref, strips=strips):
             first_tile = out_ref[register(HALO + row, 0, size), :]
             last_tile = out_ref[register(HALO + row, tiles - 1, size), :]
             fill_seam(
-                out_ref, HALO + row, first_tile, last_tile, own_strips, kind * height + row, place >= 0, tiles
+                out_ref, HALO + row, first_tile, last_tile, strips, row, place >= 0, tiles
             )
             return carry
 
@@ -340,7 +356,7 @@
         relax_rows(buffers[(step + 1) % 2], buffers[step % 2], ground_ref, first, count, ring)
 
 
-def outer_kernel(height, tiles, far_ref, even_ref, odd_ref, *refs):
+def outer_kernel(height, tiles, far_ref, *refs):
     ground_ref, surface_ref, other_ref, level_ref, far_out, near_out = refs[3:9]
     ring = tiles + 1
     size = ring * SUBS
@@ -352,8 +368,6 @@
         jnp.where(top, 0, HALO + height),
         top,
         has_far,
-        (even_ref, odd_ref),
-        [kind * height + jnp.where(top, height - HALO, 0) for kind in range(2)],
         ground_ref,
         surface_ref,
         tiles,
@@ -500,7 +514,7 @@
         pltpu.with_memory_space_constraint(value, pltpu.HBM)
         for value in (elevation, fill_depth, edge_rows, edge_sides, adjacency)
     ]
-    sent = pltpu.VMEM(((2 * HALO - 1) * packed, LANES), f32)
+    sent = pltpu.VMEM(((2 * HALO - 1) * packed + 4 * HALO, LANES), f32)
     strip = pltpu.VMEM((2 * height, LANES), f32)
     work = pltpu.VMEM(((height + 2 * HALO) * size, LANES), f32)
     far, near, even, odd, ground, surface = pl.pallas_call(
@@ -522,7 +536,6 @@
     )(*arguments[:4])
 
     near_pairs, far_pairs = [matching(places, first) for first in range(2)]
-    stay = [(place, place) for place in range(places)]
     ends = [(place, place) for place in range(places) if place not in dict(far_pairs)]
     groups_count = lax.axis_size("groups")
     part = places * cols
@@ -533,32 +546,46 @@
                 far_all.append((group * part + source, target * part + arrival))
     device_axes = ("rows", "cols", "sub")
 
-    def swap_strips(pieces, row_pairs):
-        arrived = []
-        for first, piece in enumerate(pieces):
-            pairs = cross(row_pairs, matching(cols, first), cols, subs)
-            arrived.append(lax.ppermute(piece, device_axes, pairs) if pairs else piece)
-        return arrived
-
-    far_strips = swap_strips((even, odd), far_pairs + ends)
+    strips = []
+    for first, piece in enumerate((even, odd)):
+        pairs = matching(cols, first)
+        strips.append(lax.ppermute(piece, "cols", pairs) if pairs else piece)
+    far, near = pl.pallas_call(
+        append_kernel,
+        out_shape=[sent, sent],
+        in_specs=in_vmem(4),
+        out_specs=in_vmem(2),
+        input_output_aliases={2: 0, 3: 1},
+        compiler_params=limit,
+        cost_estimate=short,
+        name="append_strips",
+    )(*strips, far, near)
     far_rows = lax.ppermute(far, ("groups",) + device_axes, far_all)
     near_rows = lax.ppermute(near, ("rows", "sub"), near_pairs)
-    strips = swap_strips((even, odd), stay) + swap_strips((even, odd), near_pairs)
+    hops = pl.pallas_call(
+        hops_kernel,
+        out_shape=pltpu.VMEM((9 * tile_count, LANES), f32),
+        in_specs=in_hbm(1) + in_vmem(1),
+        out_specs=pl.BlockSpec(memory_space=pltpu.VMEM),
+        scratch_shapes=[pltpu.VMEM(adjacency.shape, jnp.int32), pltpu.SemaphoreType.DMA],
+        compiler_params=limit,
+        cost_estimate=short,
+        name="tile_hops",
+    )(arguments[4], even)
 
     def inner(*refs):
         inner_kernel(height, tiles, *refs)
 
-    ground, surface, other, hops = pl.pallas_call(
+    ground, surface, other = pl.pallas_call(
         inner,
-        out_shape=[work, work, work, pltpu.VMEM((9 * tile_count, LANES), f32)],
-        in_specs=in_hbm(1) + in_vmem(7),
-        out_specs=in_vmem(4),
-        scratch_shapes=[pltpu.VMEM(adjacency.shape, jnp.int32), pltpu.SemaphoreType.DMA],
-        input_output_aliases={6: 0, 7: 1},
+        out_shape=[work, work, work],
+        in_specs=in_vmem(6),
+        out_specs=in_vmem(3),
+        input_output_aliases={3: 0, 4: 1},
         compiler_params=limit,
         cost_estimate=short,
         name="inner_passes",
-    )(arguments[4], near_rows, *strips, ground, surface)
+    )(near_rows, *strips, ground, surface, hops)
 
     def outer(far_ref, *refs):
         outer_kernel(height, tiles, far_ref, *refs)
@@ -568,13 +595,13 @@
     ground, surface, other, floors, far, near = pl.pallas_call(
         outer,
         out_shape=[work, work, work, pltpu.VMEM((devices, LANES), f32), again, again],
-        in_specs=in_vmem(6),
+        in_specs=in_vmem(4),
         out_specs=in_vmem(6),
-        input_output_aliases={3: 0, 4: 1, 5: 2},
+        input_output_aliases={1: 0, 2: 1, 3: 2},
         compiler_params=limit,
         cost_estimate=short,
         name="outer_passes",
-    )(far_rows, *far_strips, ground, surface, other)
+    )(far_rows, ground, surface, other)
 
     far_rows = lax.ppermute(far, ("groups",) + device_axes, far_all)
     near_rows = lax.ppermute(near, ("rows", "sub"), near_pairs)

time: 30.6 us -> 33.7 us (1.10)
  waiting for transfers between devices: 1.72 us -> 4.49 us
  blocking collectives: 10.1 us -> 11.3 us
  starting transfers between devices: 8.14 us -> 7.12 us
    ppermute x2, waiting for transfers between devices: 0.01 us -> 2.77 us  [per_device(): far_rows = lax.ppermute(far, ('groups',) + device_axes, far_all)]
    all_to_all x1, blocking collectives: 10.1 us -> 11.3 us  [per_device(): floors = lax.all_to_all(floors, device_axes, 0, 0, tiled=True)]
    ppermute x2, starting transfers between devices: 0.69 us -> 0.01 us  [per_device(): near_rows = lax.ppermute(near, ('rows', 'sub'), near_pairs)]
    ppermute x3 -> x1, starting transfers between devices: 3.29 us -> 3 us  [per_device(): strips.append(lax.ppermute(piece, 'cols', pairs) if pairs else piece)]
    pallas_call x1 -> x3, Pallas kernels: 4.07 us -> 4.19 us  [the longest x1 2.81 us: per_device(): pl.pallas_call(inner, out_shape=[work, work, work], in_specs=in_vmem(6),...]
    ppermute x3 -> x1, waiting for transfers between devices: 1.71 us -> 1.72 us  [per_device(): strips.append(lax.ppermute(piece, 'cols', pairs) if pairs else piece)]
  transfers between devices with their start and end apart: 7 -> 5, of which waited for: 1 -> 2; matrix products, arithmetic and copies ran while one was open for 0% -> 0% of each run, Pallas kernels for 13% -> 13%
where the time goes in v4:
time: 33.7 us; the launch traced here: 33.4 us
  blocking collectives  11.3 us (34%)
  Pallas kernels  10.5 us (31%)
  starting transfers between devices  7.12 us (21%)
  waiting for transfers between devices  4.49 us (13%)
    all_to_all x1, blocking collectives, per_device(): floors = lax.all_to_all(floors, device_axes, 0, 0, tiled=True)  11.3 us
    ppermute x2, starting transfers between devices, per_device(): far_rows = lax.ppermute(far, ('groups',) + device_axes, far_all)  4.11 us
    ppermute x1, starting transfers between devices, per_device(): strips.append(lax.ppermute(piece, 'cols', pairs) if pairs else piece)  3 us
    pallas_call x1, Pallas kernels, per_device(): pl.pallas_call(inner, out_shape=[work, work, work], in_specs=in_vmem(6),...  2.81 us
    ppermute x2, waiting for transfers between devices, per_device(): far_rows = lax.ppermute(far, ('groups',) + device_axes, far_all)  2.77 us
    pallas_call x1, Pallas kernels, per_device(): pl.pallas_call(late, out_shape=jax.ShapeDtypeStruct((height, width), f32)...  2.59 us
    pallas_call x1, Pallas kernels, per_device(): pl.pallas_call(edge_kernel, out_shape=[sent, sent, strip, strip, work, wo...  1.87 us
    pallas_call x1, Pallas kernels, per_device(): pl.pallas_call(outer, out_shape=[work, work, work, pltpu.VMEM((devices, L...  1.8 us
  transfers between devices with their start and end apart: 5, of which 2 were waited for; matrix products, arithmetic and copies ran while one was open for 0% of the time, Pallas kernels for 13%

profile of v4, /device:TPU:0, one launch (start us, length us, event | category | flops | bytes accessed | tf_op | source)
XLA Modules:
  0.0 33.4 jit_solution(11998952277142693695)
XLA Ops:
  0.0 1.9 %edge_rows.1 = (f32[992,128]{1,0:T(8,128)S(1)}, f32[992,128]{1,0:T(8,128)S(1)}, f32[32,128]{1,0:T(8,128)S(1)}, f32[32,128]{1,0:T(8,128)S(1)}, f32[2304,128]{1,0:T(8,128)S(1)}, /*index=5*/f32[2304,128]{1,0:T(8,128)S(1)}) custom-call(f32[16,8192]{1,0:T(8,128)} %ground_hbm.1, f32[16,8192]{1,0:T(8,128)} %depth_hbm.1, s32[2,8192]{1,0:T(2,128)} %rows_hbm.1, ...), custom_call_target="tpu_custom_call" | custom-call | flops 1024 | bytes 1024 | tf_op jit(solution)/shard_map/edge_rows/pallas_call | solution.py:520
  1.9 3.0 %collective-permute-start = (f32[32,128]{1,0:T(8,128)S(1)}, f32[32,128]{1,0:T(8,128)S(1)}, u32[]{:S(2)}, u32[]{:S(2)}) collective-permute-start(f32[32,128]{1,0:T(8,128)S(1)} %get-tuple-element.21.after_ref), channel_id=1, source_target_pairs={{0,2},{2,0},{1,3},{3,1},{4,6},{6,4},{5,7},{7,5},{8,10},{10,8},{9,1... | collective-permute-start | bytes 49160 | tf_op jit(solution)/shard_map/ppermute | solution.py:552
  4.9 1.7 %collective-permute-done.even_ref.refs_1_ = f32[32,128]{1,0:T(8,128)S(1)} collective-permute-done((f32[32,128]{1,0:T(8,128)S(1)}, f32[32,128]{1,0:T(8,128)S(1)}, u32[]{:S(2)}, u32[]{:S(2)}) %collective-permute-start) | collective-permute-done | bytes 16416 | tf_op jit(solution)/shard_map/ppermute | solution.py:552
  6.6 0.0 collective-permute-start.2
  6.6 2.0 %collective-permute-start.1 = (f32[992,128]{1,0:T(8,128)S(1)}, f32[992,128]{1,0:T(8,128)S(1)}, u32[]{:S(2)}, u32[]{:S(2)}) collective-permute-start(f32[992,128]{1,0:T(8,128)S(1)} %get-tuple-element.25), channel_id=1, source_target_pairs={{1,4},{3,6},{4,1},{6,3},{5,8},{7,10},{8,5},{10,7},{9,12},{11,14},{... | collective-permute-start | bytes 1523720 | tf_op jit(solution)/shard_map/ppermute | solution.py:563
  8.7 1.4 %tile_hops.1.refs_5_ = f32[72,128]{1,0:T(8,128)S(1)} custom-call(s32[8,6]{1,0:T(8,128)} %links_hbm.1, f32[32,128]{1,0:T(8,128)S(1)} %get-tuple-element.21.after_ref), custom_call_target="tpu_custom_call" | custom-call | flops 1024 | bytes 1024 | tf_op jit(solution)/shard_map/tile_hops/pallas_call | solution.py:565
  10.0 0.0 collective-permute-done.2.refs_0_
  10.1 2.8 %inner_passes.1 = (f32[2304,128]{1,0:T(8,128)S(1)}, f32[2304,128]{1,0:T(8,128)S(1)}, f32[2304,128]{1,0:T(8,128)S(1)}) custom-call(f32[992,128]{1,0:T(8,128)S(1)} %collective-permute-done.2.refs_0_, f32[32,128]{1,0:T(8,128)S(1)} %collective-permute-done.even_ref.refs_1_, ...), custom_call_target="tpu_custom_call", output_to_operand_aliasing={{0}: (3, {}), {1}: (4, {})} | custom-call | flops 1024 | bytes 1024 | tf_op jit(solution)/shard_map/inner_passes/pallas_call | solution.py:579
  12.9 2.8 %collective-permute-done.1.far_ref = f32[992,128]{1,0:T(8,128)S(1)} collective-permute-done((f32[992,128]{1,0:T(8,128)S(1)}, f32[992,128]{1,0:T(8,128)S(1)}, u32[]{:S(2)}, u32[]{:S(2)}) %collective-permute-start.1) | collective-permute-done | bytes 507936 | tf_op jit(solution)/shard_map/ppermute | solution.py:563
  15.6 1.8 %outer_passes.1 = (f32[2304,128]{1,0:T(8,128)S(1)}, f32[2304,128]{1,0:T(8,128)S(1)}, f32[2304,128]{1,0:T(8,128)S(1)}, f32[16,128]{1,0:T(8,128)S(1)}, f32[288,128]{1,0:T(8,128)S(1)}, /*index=5*/f32[288,128]{1,0:T(8,128)S(1)}) custom-call(f32[992,128]{1,0:T(8,128)S(1)} %collective-permute-done.1.far_ref, ...), custom_call_target="tpu_custom_call", output_to_operand_aliasing={{0}: (1, {}), {1}: (2, {}), {2}: (3, {})} | custom-call | flops 1024 | bytes 1024 | tf_op jit(solution)/shard_map/outer_passes/pallas_call | solution.py:595
  17.4 2.1 %collective-permute-start.3 = (f32[288,128]{1,0:T(8,128)S(1)}, f32[288,128]{1,0:T(8,128)S(1)}, u32[]{:S(2)}, u32[]{:S(2)}) collective-permute-start(f32[288,128]{1,0:T(8,128)S(1)} %get-tuple-element.34), channel_id=1, source_target_pairs={{1,4},{3,6},{4,1},{6,3},{5,8},{7,10},{8,5},{10,7},{9,12},{11,14},{... | collective-permute-start | bytes 442376 | tf_op jit(solution)/shard_map/ppermute | solution.py:606
  19.5 0.0 collective-permute-start.4
  19.5 11.3 %all_to_all.11 = f32[16,1,128]{2,1,0:T(1,128)S(1)} all-to-all(f32[16,1,128]{2,1,0:T(1,128)S(1)} %bitcast.5), channel_id=1, replica_groups=mesh['groups'=2,'rows'=4,'cols'=2,'sub'=2] {'rows','cols','sub'}, dimensions={0} | all-to-all | bytes 16384 | tf_op jit(solution)/shard_map/all_to_all | solution.py:608
  30.9 0.0 collective-permute-done.3.refs_2_
  30.9 0.0 collective-permute-done.4.refs_3_
  30.9 2.6 %final_passes.1 = f32[16,8192]{1,0:T(8,128)} custom-call(f32[2304,128]{1,0:T(8,128)S(1)} %get-tuple-element.32.refs_0_, f32[2304,128]{1,0:T(8,128)S(1)} %get-tuple-element.33.refs_1_, f32[288,128]{1,0:T(8,128)S(1)} %collective-permute-done.3.refs_2_, f32[288,128]{1,0:T(8,128)S(1)} %collective-permute-done.4.refs_3_, f32[16,128]{1,0:T(8,128)S(1)} %bitcast.4, ...), custom_call_target="tpu_custom_call" | custom-call | flops 1024 | bytes 1024 | tf_op jit(solution)/shard_map/final_passes/pallas_call | solution.py:613
  (1 shorter events, 0.0 us)
Async XLA Ops:
  1.9 4.7 %collective-permute-start = (f32[32,128]{1,0:T(8,128)S(1)}, f32[32,128]{1,0:T(8,128)S(1)}, u32[]{:S(2)}, u32[]{:S(2)}) collective-permute-start(f32[32,128]{1,0:T(8,128)S(1)} %get-tuple-element.21.after_ref), channel_id=1, source_target_pairs={{0,2},{2,0},{1,3},{3,1},{4,6},{6,4},{5,7},{7,5},{8,10},{10,8},{9,1... | collective-permute-start | bytes 49160 | tf_op jit(solution)/shard_map/ppermute | solution.py:552
  6.6 3.4 %collective-permute-start.2 = (f32[992,128]{1,0:T(8,128)S(1)}, f32[992,128]{1,0:T(8,128)S(1)}, u32[]{:S(2)}, u32[]{:S(2)}) collective-permute-start(f32[992,128]{1,0:T(8,128)S(1)} %get-tuple-element.26), channel_id=1, source_target_pairs={{0,1},{1,0},{4,5},{5,4},{8,9},{9,8},{12,13},{13,12},{2,3},{3,2},{6... | collective-permute-start | bytes 1523720 | tf_op jit(solution)/shard_map/ppermute | solution.py:564
  6.6 9.0 %collective-permute-start.1 = (f32[992,128]{1,0:T(8,128)S(1)}, f32[992,128]{1,0:T(8,128)S(1)}, u32[]{:S(2)}, u32[]{:S(2)}) collective-permute-start(f32[992,128]{1,0:T(8,128)S(1)} %get-tuple-element.25), channel_id=1, source_target_pairs={{1,4},{3,6},{4,1},{6,3},{5,8},{7,10},{8,5},{10,7},{9,12},{11,14},{... | collective-permute-start | bytes 1523720 | tf_op jit(solution)/shard_map/ppermute | solution.py:563
  17.4 13.4 %collective-permute-start.3 = (f32[288,128]{1,0:T(8,128)S(1)}, f32[288,128]{1,0:T(8,128)S(1)}, u32[]{:S(2)}, u32[]{:S(2)}) collective-permute-start(f32[288,128]{1,0:T(8,128)S(1)} %get-tuple-element.34), channel_id=1, source_target_pairs={{1,4},{3,6},{4,1},{6,3},{5,8},{7,10},{8,5},{10,7},{9,12},{11,14},{... | collective-permute-start | bytes 442376 | tf_op jit(solution)/shard_map/ppermute | solution.py:606
  19.5 11.4 %collective-permute-start.4 = (f32[288,128]{1,0:T(8,128)S(1)}, f32[288,128]{1,0:T(8,128)S(1)}, u32[]{:S(2)}, u32[]{:S(2)}) collective-permute-start(f32[288,128]{1,0:T(8,128)S(1)} %get-tuple-element.35), channel_id=1, source_target_pairs={{0,1},{1,0},{4,5},{5,4},{8,9},{9,8},{12,13},{13,12},{2,3},{3,2},{6... | collective-permute-start | bytes 442376 | tf_op jit(solution)/shard_map/ppermute | solution.py:607

commit v5 on v3

--- a/solution.py
+++ b/solution.py
@@ -1,3 +1,5 @@
+import functools
+
 import jax
 import jax.numpy as jnp
 from jax import lax
@@ -88,8 +90,8 @@
 
 
 def edge_kernel(
-    ground_hbm, depth_hbm, rows_hbm, sides_hbm,
-    far_ref, near_ref, even_ref, odd_ref, ground_out, surface_out,
+    ground_hbm, depth_hbm, rows_hbm, sides_hbm, links_hbm,
+    far_ref, near_ref, even_ref, odd_ref, ground_out, surface_out, links_ref,
     ground_ref, depth_ref, rows_ref, sides_ref, sems, small_sems,
 ):
     height, width = ground_hbm.shape
@@ -97,6 +99,7 @@
     small = [
         pltpu.make_async_copy(rows_hbm, rows_ref, small_sems.at[0]),
         pltpu.make_async_copy(sides_hbm, sides_ref, small_sems.at[1]),
+        pltpu.make_async_copy(links_hbm, links_ref, small_sems.at[2]),
     ]
     start_all(small[1:])
     copies = start_own(ground_hbm, depth_hbm, ground_ref, depth_ref, sems)
@@ -222,7 +225,7 @@
     out_ref[register(row, tiles, (tiles + 1) * SUBS), :] = jnp.where(lane < LANES // 2, after, before)
 
 
-def relax_rows(source, target, ground, first, count, ring):
+def relax_passes(passes, ground, ring):
     size = ring * SUBS
     _, lane = position()
     at_first = lane == 0
@@ -230,17 +233,20 @@
     order = [ring - 1] + list(range(ring - 1))
     made = {}
 
-    def make(pair, slot):
+    def make(number, pair, slot):
+        source, _, first, _, _ = passes[number]
         row = first + 2 * pair
         values = [source[register(row + step, slot, size), :] for step in range(-1, 3)]
         both = jnp.minimum(values[1], values[2])
         for one, column in enumerate((jnp.minimum(values[0], both), jnp.minimum(both, values[3]))):
-            made[pair, one, slot] = (column, pltpu.roll(column, 1, 1), pltpu.roll(column, LANES - 1, 1))
-
-    def finish(pair, slot):
+            rolled = pltpu.roll(column, 1, 1), pltpu.roll(column, LANES - 1, 1)
+            made[number, pair, one, slot] = (column, *rolled)
+
+    def finish(number, pair, slot):
+        source, target, first, _, _ = passes[number]
         for one in range(2):
             row = first + 2 * pair + one
-            before, here, after = [made[pair, one, (slot + step) % ring] for step in (-1, 0, 1)]
+            before, here, after = [made[number, pair, one, (slot + step) % ring] for step in (-1, 0, 1)]
             from_left = jnp.where(at_first, before[1], here[1])
             from_right = jnp.where(at_last, after[2], here[2])
             lowest = jnp.minimum(jnp.minimum(from_left, from_right), here[0])
@@ -248,16 +254,24 @@
             raised = jnp.minimum(source[where, :], lowest + rise_step)
             target[where, :] = jnp.maximum(ground[where, :], raised)
 
-    makes = [(pair, slot) for pair in range(count // 2) for slot in order]
-    finishes = [(pair, slot) for pair in range(count // 2) for slot in range(ring)]
-    done = 0
-    for number, item in enumerate(makes):
-        make(*item)
+    def items(slots):
+        return [
+            (number, pair, slot)
+            for number, (_, _, _, count, _) in enumerate(passes)
+            for pair in range(count // 2)
+            for slot in slots
+        ]
+
+    makes, finishes = items(order), items(range(ring))
+    for number in range(len(makes) + AHEAD):
+        if number < len(makes):
+            make(*makes[number])
         if number >= AHEAD:
-            finish(*finishes[done])
-            done += 1
-    for item in finishes[done:]:
-        finish(*item)
+            done = finishes[number - AHEAD]
+            finish(*done)
+            _, _, _, count, then = passes[done[0]]
+            if then is not None and done[1:] == (count // 2 - 1, ring - 1):
+                then()
 
 
 def hop_counts(links_ref, hops_ref, needed):
@@ -297,12 +311,12 @@
     return [r * cols + c for r in (above, row, below) for c in (left, col, right)]
 
 
-def inner_kernel(
-    height, tiles, links_hbm, near_ref, own_even_ref, own_odd_ref, near_even_ref, near_odd_ref, *refs
-):
-    ground_ref, surface_ref, other_ref, hops_ref, links_ref, sem = refs[2:]
-    links = pltpu.make_async_copy(links_hbm, links_ref, sem)
-    links.start()
+def hops_kernel(links_ref, hops_ref):
+    hop_counts(links_ref, hops_ref, needed_tiles())
+
+
+def inner_kernel(height, tiles, near_ref, own_even_ref, own_odd_ref, near_even_ref, near_odd_ref, *refs):
+    ground_ref, surface_ref, other_ref = refs[3:]
     own_strips, near_strips = (own_even_ref, own_odd_ref), (near_even_ref, near_odd_ref)
     ring = tiles + 1
     size = ring * SUBS
@@ -320,8 +334,6 @@
         surface_ref,
         tiles,
     )
-    links.wait()
-    hop_counts(links_ref, hops_ref, needed_tiles())
     for kind, out_ref in enumerate((ground_ref, surface_ref)):
 
         def body(row, carry):
@@ -334,10 +346,11 @@
 
         lax.fori_loop(0, height, body, 0, unroll=4)
     buffers = (surface_ref, other_ref)
+    passes = []
     for step in range(1, PASSES + 1):
         first = step + jnp.where(top, HALO, 0)
-        count = height + HALO - 2 * step
-        relax_rows(buffers[(step + 1) % 2], buffers[step % 2], ground_ref, first, count, ring)
+        passes.append((buffers[(step + 1) % 2], buffers[step % 2], first, height + HALO - 2 * step, None))
+    relax_passes(passes, ground_ref, ring)
 
 
 def outer_kernel(height, tiles, far_ref, even_ref, odd_ref, *refs):
@@ -359,9 +372,11 @@
         tiles,
     )
     buffers = (surface_ref, other_ref)
+    passes = []
     for step in range(1, PASSES + 1):
         first = jnp.where(top, step, HALO + height - step)
-        relax_rows(buffers[(step + 1) % 2], buffers[step % 2], ground_ref, first, HALO, ring)
+        passes.append((buffers[(step + 1) % 2], buffers[step % 2], first, HALO, None))
+    relax_passes(passes, ground_ref, ring)
     low, high = HALO, HALO + height - FINAL
     for row in range(FINAL):
         for slot in range(ring):
@@ -456,23 +471,28 @@
 
         lax.fori_loop(0, rows, body, 0, unroll=4)
     buffers = (one_ref, two_ref)
+    passes = []
     for step in range(1, FINAL):
         first = HALO - FINAL + step
-        relax_rows(
-            buffers[(step + 1) % 2], buffers[step % 2], ground_ref, first, 2 * HALO + height - 2 * first, ring
-        )
+        count = 2 * HALO + height - 2 * first
+        passes.append((buffers[(step + 1) % 2], buffers[step % 2], first, count, None))
     source, target = buffers[(FINAL + 1) % 2], buffers[FINAL % 2]
     copies = []
-    for group in range(height // SUBS):
+
+    def unfold(group):
         first = HALO + group * SUBS
-        relax_rows(source, target, ground_ref, first, SUBS, ring)
         for tile in range(tiles * SUBS):
             chunk, slot = tile // tiles, tile % tiles
             out_ref[pl.ds(group * SUBS, SUBS), pl.ds(tile * LANES, LANES)] = target[
                 pl.ds(first * size + slot * SUBS + chunk, SUBS, stride=size), :
             ]
         where = (pl.ds(group * SUBS, SUBS), slice(None))
-        copies += start_all([pltpu.make_async_copy(out_ref.at[where], out_hbm.at[where], sems.at[group])])
+        copies.extend(start_all([pltpu.make_async_copy(out_ref.at[where], out_hbm.at[where], sems.at[group])]))
+
+    for group in range(height // SUBS):
+        first = HALO + group * SUBS
+        passes.append((source, target, first, SUBS, functools.partial(unfold, group)))
+    relax_passes(passes, ground_ref, ring)
     wait_all(copies)
 
 
@@ -503,23 +523,23 @@
     sent = pltpu.VMEM(((2 * HALO - 1) * packed, LANES), f32)
     strip = pltpu.VMEM((2 * height, LANES), f32)
     work = pltpu.VMEM(((height + 2 * HALO) * size, LANES), f32)
-    far, near, even, odd, ground, surface = pl.pallas_call(
+    far, near, even, odd, ground, surface, links = pl.pallas_call(
         edge_kernel,
-        out_shape=[sent, sent, strip, strip, work, work],
-        in_specs=in_hbm(4),
-        out_specs=in_vmem(6),
+        out_shape=[sent, sent, strip, strip, work, work, pltpu.VMEM(adjacency.shape, jnp.int32)],
+        in_specs=in_hbm(5),
+        out_specs=in_vmem(7),
         scratch_shapes=[
             pltpu.VMEM((height, width), f32),
             pltpu.VMEM((height, width), f32),
             pltpu.VMEM(edge_rows.shape, jnp.int32),
             pltpu.VMEM(edge_sides.shape, jnp.int32),
             pltpu.SemaphoreType.DMA((2, 4 * groups)),
-            pltpu.SemaphoreType.DMA((2,)),
+            pltpu.SemaphoreType.DMA((3,)),
         ],
         compiler_params=limit,
         cost_estimate=short,
         name="edge_rows",
-    )(*arguments[:4])
+    )(*arguments)
 
     near_pairs, far_pairs = [matching(places, first) for first in range(2)]
     stay = [(place, place) for place in range(places)]
@@ -545,20 +565,29 @@
     near_rows = lax.ppermute(near, ("rows", "sub"), near_pairs)
     strips = swap_strips((even, odd), stay) + swap_strips((even, odd), near_pairs)
 
+    hops = pl.pallas_call(
+        hops_kernel,
+        out_shape=pltpu.VMEM((9 * tile_count, LANES), f32),
+        in_specs=in_vmem(1),
+        out_specs=pl.BlockSpec(memory_space=pltpu.VMEM),
+        compiler_params=limit,
+        cost_estimate=short,
+        name="tile_hops",
+    )(links)
+
     def inner(*refs):
         inner_kernel(height, tiles, *refs)
 
-    ground, surface, other, hops = pl.pallas_call(
+    ground, surface, other = pl.pallas_call(
         inner,
-        out_shape=[work, work, work, pltpu.VMEM((9 * tile_count, LANES), f32)],
-        in_specs=in_hbm(1) + in_vmem(7),
-        out_specs=in_vmem(4),
-        scratch_shapes=[pltpu.VMEM(adjacency.shape, jnp.int32), pltpu.SemaphoreType.DMA],
-        input_output_aliases={6: 0, 7: 1},
+        out_shape=[work, work, work],
+        in_specs=in_vmem(8),
+        out_specs=in_vmem(3),
+        input_output_aliases={5: 0, 6: 1},
         compiler_params=limit,
         cost_estimate=short,
         name="inner_passes",
-    )(arguments[4], near_rows, *strips, ground, surface)
+    )(near_rows, *strips, ground, surface, hops)
 
     def outer(far_ref, *refs):
         outer_kernel(height, tiles, far_ref, *refs)

time: 30.6 us -> 29.9 us (0.977)
  Pallas kernels: 10.4 us -> 9.72 us
  waiting for transfers between devices: 1.72 us -> 1.05 us
  blocking collectives: 10.1 us -> 10.7 us
    ppermute x3, waiting for transfers between devices: 1.71 us -> 1.04 us  [swap_strips(): arrived.append(lax.ppermute(piece, device_axes, pairs) if pairs else piece)]
    pallas_call x1 -> x2, Pallas kernels: 4.07 us -> 3.42 us  [the longest x1 2.75 us: per_device(): pl.pallas_call(inner, out_shape=[work, work, work], in_specs=in_vmem(8),...]
    all_to_all x1, blocking collectives: 10.1 us -> 10.7 us  [per_device(): floors = lax.all_to_all(floors, device_axes, 0, 0, tiled=True)]
  transfers between devices with their start and end apart: 7 -> 7, of which waited for: 1 -> 1; matrix products, arithmetic and copies ran while one was open for 0% -> 0% of each run, Pallas kernels for 13% -> 12%
where the time goes in v5:
time: 29.9 us; the launch traced here: 29.7 us
  blocking collectives  10.7 us (36%)
  Pallas kernels  9.72 us (33%)
  starting transfers between devices  8.16 us (27%)
  waiting for transfers between devices  1.05 us (4%)
    all_to_all x1, blocking collectives, per_device(): floors = lax.all_to_all(floors, device_axes, 0, 0, tiled=True)  10.7 us
    ppermute x2, starting transfers between devices, per_device(): far_rows = lax.ppermute(far, ('groups',) + device_axes, far_all)  4.15 us
    ppermute x3, starting transfers between devices, swap_strips(): arrived.append(lax.ppermute(piece, device_axes, pairs) if pairs else piece)  3.29 us
    pallas_call x1, Pallas kernels, per_device(): pl.pallas_call(inner, out_shape=[work, work, work], in_specs=in_vmem(8),...  2.75 us
    pallas_call x1, Pallas kernels, per_device(): pl.pallas_call(late, out_shape=jax.ShapeDtypeStruct((height, width), f32)...  2.59 us
    pallas_call x1, Pallas kernels, per_device(): pl.pallas_call(edge_kernel, out_shape=[sent, sent, strip, strip, work, wo...  1.88 us
    pallas_call x1, Pallas kernels, per_device(): pl.pallas_call(outer, out_shape=[work, work, work, pltpu.VMEM((devices, L...  1.83 us
    ppermute x3, waiting for transfers between devices, swap_strips(): arrived.append(lax.ppermute(piece, device_axes, pairs) if pairs else piece)  1.04 us
  transfers between devices with their start and end apart: 7, of which 1 were waited for; matrix products, arithmetic and copies ran while one was open for 0% of the time, Pallas kernels for 12%

profile of v5, /device:TPU:0, one launch (start us, length us, event | category | flops | bytes accessed | tf_op | source)
XLA Modules:
  0.0 29.7 jit_solution(8500831300679016993)
XLA Ops:
  0.0 1.9 %edge_rows.1 = (f32[960,128]{1,0:T(8,128)S(1)}, f32[960,128]{1,0:T(8,128)S(1)}, f32[32,128]{1,0:T(8,128)S(1)}, f32[32,128]{1,0:T(8,128)S(1)}, f32[2304,128]{1,0:...) custom-call(f32[16,8192]{1,0:T(8,128)} %ground_hbm.1, f32[16,8192]{1,0:T(8,128)} %depth_hbm.1, ...), custom_call_target="tpu_custom_call" | custom-call | flops 1024 | bytes 1024 | tf_op jit(solution)/shard_map/edge_rows/pallas_call | solution.py:526
  1.9 0.5 %collective-permute-start.2 = (f32[960,128]{1,0:T(8,128)S(1)}, f32[960,128]{1,0:T(8,128)S(1)}, u32[]{:S(2)}, u32[]{:S(2)}) collective-permute-start(f32[960,128]{1,0:T(8,128)S(1)} %get-tuple-element.23), channel_id=1, source_target_pairs={{0,1},{1,0},{4,5},{5,4},{8,9},{9,8},{12,13},{13,12},{2,3},{3,2},{6... | collective-permute-start | bytes 1474568 | tf_op jit(solution)/shard_map/ppermute | solution.py:565
  2.4 2.6 %collective-permute-start = (f32[960,128]{1,0:T(8,128)S(1)}, f32[960,128]{1,0:T(8,128)S(1)}, u32[]{:S(2)}, u32[]{:S(2)}) collective-permute-start(f32[960,128]{1,0:T(8,128)S(1)} %get-tuple-element.20), channel_id=1, source_target_pairs={{1,4},{3,6},{4,1},{6,3},{5,8},{7,10},{8,5},{10,7},{9,12},{11,14},{... | collective-permute-start | bytes 1474568 | tf_op jit(solution)/shard_map/ppermute | solution.py:564
  5.0 1.3 %collective-permute-start.4 = (f32[32,128]{1,0:T(8,128)S(1)}, f32[32,128]{1,0:T(8,128)S(1)}, u32[]{:S(2)}, u32[]{:S(2)}) collective-permute-start(f32[32,128]{1,0:T(8,128)S(1)} %get-tuple-element.21), channel_id=1, source_target_pairs={{0,3},{2,1},{1,2},{3,0},{4,7},{6,5},{5,6},{7,4},{8,11},{10,9},{9,1... | collective-permute-start | bytes 49160 | tf_op jit(solution)/shard_map/ppermute | solution.py:560
  6.3 0.5 %collective-permute-start.3 = (f32[32,128]{1,0:T(8,128)S(1)}, f32[32,128]{1,0:T(8,128)S(1)}, u32[]{:S(2)}, u32[]{:S(2)}) collective-permute-start(f32[32,128]{1,0:T(8,128)S(1)} %get-tuple-element.21), channel_id=1, source_target_pairs={{0,2},{2,0},{1,3},{3,1},{4,6},{6,4},{5,7},{7,5},{8,10},{10,8},{9,1... | collective-permute-start | bytes 49160 | tf_op jit(solution)/shard_map/ppermute | solution.py:560
  6.8 1.5 %collective-permute-start.1 = (f32[32,128]{1,0:T(8,128)S(1)}, f32[32,128]{1,0:T(8,128)S(1)}, u32[]{:S(2)}, u32[]{:S(2)}) collective-permute-start(f32[32,128]{1,0:T(8,128)S(1)} %get-tuple-element.21), channel_id=1, source_target_pairs={{1,6},{3,4},{4,3},{6,1},{5,10},{7,8},{8,7},{10,5},{9,14},{11,12},{... | collective-permute-start | bytes 49160 | tf_op jit(solution)/shard_map/ppermute | solution.py:560
  8.3 0.7 %tile_hops.1.refs_7_.refs_5_ = f32[72,128]{1,0:T(8,128)S(1)} custom-call(s32[8,6]{1,0:T(8,128)S(1)} %get-tuple-element.26.links_ref), custom_call_target="tpu_custom_call" | custom-call | flops 1024 | bytes 1024 | tf_op jit(solution)/shard_map/tile_hops/pallas_call | solution.py:568
  9.0 0.0 collective-permute-done.4.refs_3_
  9.0 1.0 %collective-permute-done.3.refs_1_ = f32[32,128]{1,0:T(8,128)S(1)} collective-permute-done((f32[32,128]{1,0:T(8,128)S(1)}, f32[32,128]{1,0:T(8,128)S(1)}, u32[]{:S(2)}, u32[]{:S(2)}) %collective-permute-start.3) | collective-permute-done | bytes 16416 | tf_op jit(solution)/shard_map/ppermute | solution.py:560
  10.0 0.0 collective-permute-done.2.refs_0_
  10.0 2.8 %inner_passes.1 = (f32[2304,128]{1,0:T(8,128)S(1)}, f32[2304,128]{1,0:T(8,128)S(1)}, f32[2304,128]{1,0:T(8,128)S(1)}) custom-call(f32[960,128]{1,0:T(8,128)S(1)} %collective-permute-done.2.refs_0_, f32[32,128]{1,0:T(8,128)S(1)} %collective-permute-done.3.refs_1_, ...), custom_call_target="tpu_custom_call", output_to_operand_aliasing={{0}: (5, {}), {1}: (6, {})} | custom-call | flops 1024 | bytes 1024 | tf_op jit(solution)/shard_map/inner_passes/pallas_call | solution.py:581
  12.8 0.0 collective-permute-done.1.refs_0_
  12.8 0.0 collective-permute-done.far_ref
  12.8 1.8 %outer_passes.1 = (f32[2304,128]{1,0:T(8,128)S(1)}, f32[2304,128]{1,0:T(8,128)S(1)}, f32[2304,128]{1,0:T(8,128)S(1)}, f32[16,128]{1,0:T(8,128)S(1)}, f32[288,128]{1,0:T(8,128)S(1)}, /*index=5*/f32[288,128]{1,0:T(8,128)S(1)}) custom-call(f32[960,128]{1,0:T(8,128)S(1)} %collective-permute-done.far_ref, ...), custom_call_target="tpu_custom_call", output_to_operand_aliasing={{0}: (3, {}), {1}: (4, {}), {2}: (5, {})} | custom-call | flops 1024 | bytes 1024 | tf_op jit(solution)/shard_map/outer_passes/pallas_call | solution.py:597
  14.6 1.6 %collective-permute-start.5 = (f32[288,128]{1,0:T(8,128)S(1)}, f32[288,128]{1,0:T(8,128)S(1)}, u32[]{:S(2)}, u32[]{:S(2)}) collective-permute-start(f32[288,128]{1,0:T(8,128)S(1)} %get-tuple-element.32), channel_id=1, source_target_pairs={{1,4},{3,6},{4,1},{6,3},{5,8},{7,10},{8,5},{10,7},{9,12},{11,14},{... | collective-permute-start | bytes 442376 | tf_op jit(solution)/shard_map/ppermute | solution.py:608
  16.2 0.2 collective-permute-start.6
  16.4 10.7 %all_to_all.11 = f32[16,1,128]{2,1,0:T(1,128)S(1)} all-to-all(f32[16,1,128]{2,1,0:T(1,128)S(1)} %bitcast.5), channel_id=1, replica_groups=mesh['groups'=2,'rows'=4,'cols'=2,'sub'=2] {'rows','cols','sub'}, dimensions={0} | all-to-all | bytes 16384 | tf_op jit(solution)/shard_map/all_to_all | solution.py:610
  27.1 0.0 collective-permute-done.5.refs_2_
  27.1 0.0 collective-permute-done.6.refs_3_
  27.1 2.6 %final_passes.1 = f32[16,8192]{1,0:T(8,128)} custom-call(f32[2304,128]{1,0:T(8,128)S(1)} %get-tuple-element.30.refs_0_, f32[2304,128]{1,0:T(8,128)S(1)} %get-tuple-element.31.refs_1_, f32[288,128]{1,0:T(8,128)S(1)} %collective-permute-done.5.refs_2_, f32[288,128]{1,0:T(8,128)S(1)} %collective-permute-done.6.refs_3_, f32[16,128]{1,0:T(8,128)S(1)} %bitcast.4, ...), custom_call_target="tpu_custom_call" | custom-call | flops 1024 | bytes 1024 | tf_op jit(solution)/shard_map/final_passes/pallas_call | solution.py:615
Async XLA Ops:
  1.9 8.1 %collective-permute-start.2 = (f32[960,128]{1,0:T(8,128)S(1)}, f32[960,128]{1,0:T(8,128)S(1)}, u32[]{:S(2)}, u32[]{:S(2)}) collective-permute-start(f32[960,128]{1,0:T(8,128)S(1)} %get-tuple-element.23), channel_id=1, source_target_pairs={{0,1},{1,0},{4,5},{5,4},{8,9},{9,8},{12,13},{13,12},{2,3},{3,2},{6... | collective-permute-start | bytes 1474568 | tf_op jit(solution)/shard_map/ppermute | solution.py:565
  2.4 10.4 %collective-permute-start = (f32[960,128]{1,0:T(8,128)S(1)}, f32[960,128]{1,0:T(8,128)S(1)}, u32[]{:S(2)}, u32[]{:S(2)}) collective-permute-start(f32[960,128]{1,0:T(8,128)S(1)} %get-tuple-element.20), channel_id=1, source_target_pairs={{1,4},{3,6},{4,1},{6,3},{5,8},{7,10},{8,5},{10,7},{9,12},{11,14},{... | collective-permute-start | bytes 1474568 | tf_op jit(solution)/shard_map/ppermute | solution.py:564
  5.0 4.0 %collective-permute-start.4 = (f32[32,128]{1,0:T(8,128)S(1)}, f32[32,128]{1,0:T(8,128)S(1)}, u32[]{:S(2)}, u32[]{:S(2)}) collective-permute-start(f32[32,128]{1,0:T(8,128)S(1)} %get-tuple-element.21), channel_id=1, source_target_pairs={{0,3},{2,1},{1,2},{3,0},{4,7},{6,5},{5,6},{7,4},{8,11},{10,9},{9,1... | collective-permute-start | bytes 49160 | tf_op jit(solution)/shard_map/ppermute | solution.py:560
  6.3 3.7 %collective-permute-start.3 = (f32[32,128]{1,0:T(8,128)S(1)}, f32[32,128]{1,0:T(8,128)S(1)}, u32[]{:S(2)}, u32[]{:S(2)}) collective-permute-start(f32[32,128]{1,0:T(8,128)S(1)} %get-tuple-element.21), channel_id=1, source_target_pairs={{0,2},{2,0},{1,3},{3,1},{4,6},{6,4},{5,7},{7,5},{8,10},{10,8},{9,1... | collective-permute-start | bytes 49160 | tf_op jit(solution)/shard_map/ppermute | solution.py:560
  6.8 6.0 %collective-permute-start.1 = (f32[32,128]{1,0:T(8,128)S(1)}, f32[32,128]{1,0:T(8,128)S(1)}, u32[]{:S(2)}, u32[]{:S(2)}) collective-permute-start(f32[32,128]{1,0:T(8,128)S(1)} %get-tuple-element.21), channel_id=1, source_target_pairs={{1,6},{3,4},{4,3},{6,1},{5,10},{7,8},{8,7},{10,5},{9,14},{11,12},{... | collective-permute-start | bytes 49160 | tf_op jit(solution)/shard_map/ppermute | solution.py:560
  14.6 12.4 %collective-permute-start.5 = (f32[288,128]{1,0:T(8,128)S(1)}, f32[288,128]{1,0:T(8,128)S(1)}, u32[]{:S(2)}, u32[]{:S(2)}) collective-permute-start(f32[288,128]{1,0:T(8,128)S(1)} %get-tuple-element.32), channel_id=1, source_target_pairs={{1,4},{3,6},{4,1},{6,3},{5,8},{7,10},{8,5},{10,7},{9,12},{11,14},{... | collective-permute-start | bytes 442376 | tf_op jit(solution)/shard_map/ppermute | solution.py:608
  16.2 10.9 %collective-permute-start.6 = (f32[288,128]{1,0:T(8,128)S(1)}, f32[288,128]{1,0:T(8,128)S(1)}, u32[]{:S(2)}, u32[]{:S(2)}) collective-permute-start(f32[288,128]{1,0:T(8,128)S(1)} %get-tuple-element.33), channel_id=1, source_target_pairs={{0,1},{1,0},{4,5},{5,4},{8,9},{9,8},{12,13},{13,12},{2,3},{3,2},{6... | collective-permute-start | bytes 442376 | tf_op jit(solution)/shard_map/ppermute | solution.py:609

commit v6 on v5

--- a/solution.py
+++ b/solution.py
@@ -199,8 +199,7 @@
     size = packed + SUBS
     bases = (jnp.where(is_top, HALO - 1, 0), jnp.where(is_top, 0, HALO - 1))
     for base, out_ref, strip_row in zip(bases, (ground_ref, surface_ref), strip_rows):
-
-        def body(row, carry):
+        for row in range(HALO):
             values = [
                 jnp.where(present, rows_ref[register(base + row, slot, packed), :], unreached)
                 for slot in range(tiles)
@@ -208,9 +207,6 @@
             for slot in range(tiles):
                 out_ref[register(first + row, slot, size), :] = values[slot]
             fill_seam(out_ref, first + row, values[0], values[-1], strip_refs, strip_row + row, present, tiles)
-            return carry
-
-        lax.fori_loop(0, HALO, body, 0, unroll=4)
 
 
 def fill_seam(out_ref, row, first_tile, last_tile, strip_refs, strip_row, present, tiles):
@@ -335,16 +331,12 @@
         tiles,
     )
     for kind, out_ref in enumerate((ground_ref, surface_ref)):
-
-        def body(row, carry):
+        for row in range(height):
             first_tile = out_ref[register(HALO + row, 0, size), :]
             last_tile = out_ref[register(HALO + row, tiles - 1, size), :]
             fill_seam(
                 out_ref, HALO + row, first_tile, last_tile, own_strips, kind * height + row, place >= 0, tiles
             )
-            return carry
-
-        lax.fori_loop(0, height, body, 0, unroll=4)
     buffers = (surface_ref, other_ref)
     passes = []
     for step in range(1, PASSES + 1):
@@ -460,16 +452,12 @@
         (far_ref, 0, jnp.where(top, low, high), FINAL, far_pair),
     )
     for source, source_first, first, rows, (middle, seam) in spans:
-
-        def body(row, carry):
+        for row in range(rows):
             for slot in range(ring):
                 value = source[register(source_first + row, slot, size), :]
                 value = jnp.minimum(value, seam if slot == tiles else middle)
                 where = register(first + row, slot, size)
                 one_ref[where, :] = jnp.maximum(ground_ref[where, :], value)
-            return carry
-
-        lax.fori_loop(0, rows, body, 0, unroll=4)
     buffers = (one_ref, two_ref)
     passes = []
     for step in range(1, FINAL):

time: 29.9 us -> 29.7 us (level)
  transfers between devices with their start and end apart: 7 -> 7, of which waited for: 1 -> 1; matrix products, arithmetic and copies ran while one was open for 0% -> 0% of each run, Pallas kernels for 12% -> 11%
where the time goes in v6:
time: 29.7 us; the launch traced here: 29.5 us
  blocking collectives  10.7 us (36%)
  Pallas kernels  9.49 us (32%)
  starting transfers between devices  8.25 us (28%)
  waiting for transfers between devices  1.05 us (4%)
    all_to_all x1, blocking collectives, per_device(): floors = lax.all_to_all(floors, device_axes, 0, 0, tiled=True)  10.7 us
    ppermute x2, starting transfers between devices, per_device(): far_rows = lax.ppermute(far, ('groups',) + device_axes, far_all)  4.15 us
    ppermute x3, starting transfers between devices, swap_strips(): arrived.append(lax.ppermute(piece, device_axes, pairs) if pairs else piece)  3.29 us
    pallas_call x1, Pallas kernels, per_device(): pl.pallas_call(inner, out_shape=[work, work, work], in_specs=in_vmem(8),...  2.67 us
    pallas_call x1, Pallas kernels, per_device(): pl.pallas_call(late, out_shape=jax.ShapeDtypeStruct((height, width), f32)...  2.49 us
    pallas_call x1, Pallas kernels, per_device(): pl.pallas_call(edge_kernel, out_shape=[sent, sent, strip, strip, work, wo...  1.88 us
    pallas_call x1, Pallas kernels, per_device(): pl.pallas_call(outer, out_shape=[work, work, work, pltpu.VMEM((devices, L...  1.78 us
    ppermute x3, waiting for transfers between devices, swap_strips(): arrived.append(lax.ppermute(piece, device_axes, pairs) if pairs else piece)  1.04 us
  transfers between devices with their start and end apart: 7, of which 1 were waited for; matrix products, arithmetic and copies ran while one was open for 0% of the time, Pallas kernels for 11%

profile of v6, /device:TPU:0, one launch (start us, length us, event | category | flops | bytes accessed | tf_op | source)
XLA Modules:
  0.0 29.5 jit_solution(14409886500599551427)
XLA Ops:
  0.0 1.9 %edge_rows.1 = (f32[960,128]{1,0:T(8,128)S(1)}, f32[960,128]{1,0:T(8,128)S(1)}, f32[32,128]{1,0:T(8,128)S(1)}, f32[32,128]{1,0:T(8,128)S(1)}, f32[2304,128]{1,0:...) custom-call(f32[16,8192]{1,0:T(8,128)} %ground_hbm.1, f32[16,8192]{1,0:T(8,128)} %depth_hbm.1, ...), custom_call_target="tpu_custom_call" | custom-call | flops 1024 | bytes 1024 | tf_op jit(solution)/shard_map/edge_rows/pallas_call | solution.py:514
  1.9 0.5 %collective-permute-start.2 = (f32[960,128]{1,0:T(8,128)S(1)}, f32[960,128]{1,0:T(8,128)S(1)}, u32[]{:S(2)}, u32[]{:S(2)}) collective-permute-start(f32[960,128]{1,0:T(8,128)S(1)} %get-tuple-element.23), channel_id=1, source_target_pairs={{0,1},{1,0},{4,5},{5,4},{8,9},{9,8},{12,13},{13,12},{2,3},{3,2},{6... | collective-permute-start | bytes 1474568 | tf_op jit(solution)/shard_map/ppermute | solution.py:553
  2.4 2.6 %collective-permute-start = (f32[960,128]{1,0:T(8,128)S(1)}, f32[960,128]{1,0:T(8,128)S(1)}, u32[]{:S(2)}, u32[]{:S(2)}) collective-permute-start(f32[960,128]{1,0:T(8,128)S(1)} %get-tuple-element.20), channel_id=1, source_target_pairs={{1,4},{3,6},{4,1},{6,3},{5,8},{7,10},{8,5},{10,7},{9,12},{11,14},{... | collective-permute-start | bytes 1474568 | tf_op jit(solution)/shard_map/ppermute | solution.py:552
  5.0 1.3 %collective-permute-start.4 = (f32[32,128]{1,0:T(8,128)S(1)}, f32[32,128]{1,0:T(8,128)S(1)}, u32[]{:S(2)}, u32[]{:S(2)}) collective-permute-start(f32[32,128]{1,0:T(8,128)S(1)} %get-tuple-element.21), channel_id=1, source_target_pairs={{0,3},{2,1},{1,2},{3,0},{4,7},{6,5},{5,6},{7,4},{8,11},{10,9},{9,1... | collective-permute-start | bytes 49160 | tf_op jit(solution)/shard_map/ppermute | solution.py:548
  6.3 0.5 %collective-permute-start.3 = (f32[32,128]{1,0:T(8,128)S(1)}, f32[32,128]{1,0:T(8,128)S(1)}, u32[]{:S(2)}, u32[]{:S(2)}) collective-permute-start(f32[32,128]{1,0:T(8,128)S(1)} %get-tuple-element.21), channel_id=1, source_target_pairs={{0,2},{2,0},{1,3},{3,1},{4,6},{6,4},{5,7},{7,5},{8,10},{10,8},{9,1... | collective-permute-start | bytes 49160 | tf_op jit(solution)/shard_map/ppermute | solution.py:548
  6.8 1.5 %collective-permute-start.1 = (f32[32,128]{1,0:T(8,128)S(1)}, f32[32,128]{1,0:T(8,128)S(1)}, u32[]{:S(2)}, u32[]{:S(2)}) collective-permute-start(f32[32,128]{1,0:T(8,128)S(1)} %get-tuple-element.21), channel_id=1, source_target_pairs={{1,6},{3,4},{4,3},{6,1},{5,10},{7,8},{8,7},{10,5},{9,14},{11,12},{... | collective-permute-start | bytes 49160 | tf_op jit(solution)/shard_map/ppermute | solution.py:548
  8.3 0.7 %tile_hops.1.refs_7_.refs_5_ = f32[72,128]{1,0:T(8,128)S(1)} custom-call(s32[8,6]{1,0:T(8,128)S(1)} %get-tuple-element.26.links_ref), custom_call_target="tpu_custom_call" | custom-call | flops 1024 | bytes 1024 | tf_op jit(solution)/shard_map/tile_hops/pallas_call | solution.py:556
  9.0 0.0 collective-permute-done.4.refs_3_
  9.0 1.0 %collective-permute-done.3.refs_1_ = f32[32,128]{1,0:T(8,128)S(1)} collective-permute-done((f32[32,128]{1,0:T(8,128)S(1)}, f32[32,128]{1,0:T(8,128)S(1)}, u32[]{:S(2)}, u32[]{:S(2)}) %collective-permute-start.3) | collective-permute-done | bytes 16416 | tf_op jit(solution)/shard_map/ppermute | solution.py:548
  10.0 0.0 collective-permute-done.2.refs_0_
  10.0 2.7 %inner_passes.1 = (f32[2304,128]{1,0:T(8,128)S(1)}, f32[2304,128]{1,0:T(8,128)S(1)}, f32[2304,128]{1,0:T(8,128)S(1)}) custom-call(f32[960,128]{1,0:T(8,128)S(1)} %collective-permute-done.2.refs_0_, f32[32,128]{1,0:T(8,128)S(1)} %collective-permute-done.3.refs_1_, ...), custom_call_target="tpu_custom_call", output_to_operand_aliasing={{0}: (5, {}), {1}: (6, {})} | custom-call | flops 1024 | bytes 1024 | tf_op jit(solution)/shard_map/inner_passes/pallas_call | solution.py:569
  12.7 0.0 collective-permute-done.1.refs_0_
  12.7 0.0 collective-permute-done.far_ref
  12.7 1.8 %outer_passes.1 = (f32[2304,128]{1,0:T(8,128)S(1)}, f32[2304,128]{1,0:T(8,128)S(1)}, f32[2304,128]{1,0:T(8,128)S(1)}, f32[16,128]{1,0:T(8,128)S(1)}, f32[288,128]{1,0:T(8,128)S(1)}, /*index=5*/f32[288,128]{1,0:T(8,128)S(1)}) custom-call(f32[960,128]{1,0:T(8,128)S(1)} %collective-permute-done.far_ref, ...), custom_call_target="tpu_custom_call", output_to_operand_aliasing={{0}: (3, {}), {1}: (4, {}), {2}: (5, {})} | custom-call | flops 1024 | bytes 1024 | tf_op jit(solution)/shard_map/outer_passes/pallas_call | solution.py:585
  14.5 1.6 %collective-permute-start.5 = (f32[288,128]{1,0:T(8,128)S(1)}, f32[288,128]{1,0:T(8,128)S(1)}, u32[]{:S(2)}, u32[]{:S(2)}) collective-permute-start(f32[288,128]{1,0:T(8,128)S(1)} %get-tuple-element.32), channel_id=1, source_target_pairs={{1,4},{3,6},{4,1},{6,3},{5,8},{7,10},{8,5},{10,7},{9,12},{11,14},{... | collective-permute-start | bytes 442376 | tf_op jit(solution)/shard_map/ppermute | solution.py:596
  16.0 0.3 collective-permute-start.6
  16.3 10.7 %all_to_all.11 = f32[16,1,128]{2,1,0:T(1,128)S(1)} all-to-all(f32[16,1,128]{2,1,0:T(1,128)S(1)} %bitcast.5), channel_id=1, replica_groups=mesh['groups'=2,'rows'=4,'cols'=2,'sub'=2] {'rows','cols','sub'}, dimensions={0} | all-to-all | bytes 16384 | tf_op jit(solution)/shard_map/all_to_all | solution.py:598
  27.0 0.0 collective-permute-done.5.refs_2_
  27.0 0.0 collective-permute-done.6.refs_3_
  27.0 2.5 %final_passes.1 = f32[16,8192]{1,0:T(8,128)} custom-call(f32[2304,128]{1,0:T(8,128)S(1)} %get-tuple-element.30.refs_0_, f32[2304,128]{1,0:T(8,128)S(1)} %get-tuple-element.31.refs_1_, f32[288,128]{1,0:T(8,128)S(1)} %collective-permute-done.5.refs_2_, f32[288,128]{1,0:T(8,128)S(1)} %collective-permute-done.6.refs_3_, f32[16,128]{1,0:T(8,128)S(1)} %bitcast.4, ...), custom_call_target="tpu_custom_call" | custom-call | flops 1024 | bytes 1024 | tf_op jit(solution)/shard_map/final_passes/pallas_call | solution.py:603
Async XLA Ops:
  1.9 8.1 %collective-permute-start.2 = (f32[960,128]{1,0:T(8,128)S(1)}, f32[960,128]{1,0:T(8,128)S(1)}, u32[]{:S(2)}, u32[]{:S(2)}) collective-permute-start(f32[960,128]{1,0:T(8,128)S(1)} %get-tuple-element.23), channel_id=1, source_target_pairs={{0,1},{1,0},{4,5},{5,4},{8,9},{9,8},{12,13},{13,12},{2,3},{3,2},{6... | collective-permute-start | bytes 1474568 | tf_op jit(solution)/shard_map/ppermute | solution.py:553
  2.4 10.3 %collective-permute-start = (f32[960,128]{1,0:T(8,128)S(1)}, f32[960,128]{1,0:T(8,128)S(1)}, u32[]{:S(2)}, u32[]{:S(2)}) collective-permute-start(f32[960,128]{1,0:T(8,128)S(1)} %get-tuple-element.20), channel_id=1, source_target_pairs={{1,4},{3,6},{4,1},{6,3},{5,8},{7,10},{8,5},{10,7},{9,12},{11,14},{... | collective-permute-start | bytes 1474568 | tf_op jit(solution)/shard_map/ppermute | solution.py:552
  5.0 4.0 %collective-permute-start.4 = (f32[32,128]{1,0:T(8,128)S(1)}, f32[32,128]{1,0:T(8,128)S(1)}, u32[]{:S(2)}, u32[]{:S(2)}) collective-permute-start(f32[32,128]{1,0:T(8,128)S(1)} %get-tuple-element.21), channel_id=1, source_target_pairs={{0,3},{2,1},{1,2},{3,0},{4,7},{6,5},{5,6},{7,4},{8,11},{10,9},{9,1... | collective-permute-start | bytes 49160 | tf_op jit(solution)/shard_map/ppermute | solution.py:548
  6.3 3.7 %collective-permute-start.3 = (f32[32,128]{1,0:T(8,128)S(1)}, f32[32,128]{1,0:T(8,128)S(1)}, u32[]{:S(2)}, u32[]{:S(2)}) collective-permute-start(f32[32,128]{1,0:T(8,128)S(1)} %get-tuple-element.21), channel_id=1, source_target_pairs={{0,2},{2,0},{1,3},{3,1},{4,6},{6,4},{5,7},{7,5},{8,10},{10,8},{9,1... | collective-permute-start | bytes 49160 | tf_op jit(solution)/shard_map/ppermute | solution.py:548
  6.8 5.9 %collective-permute-start.1 = (f32[32,128]{1,0:T(8,128)S(1)}, f32[32,128]{1,0:T(8,128)S(1)}, u32[]{:S(2)}, u32[]{:S(2)}) collective-permute-start(f32[32,128]{1,0:T(8,128)S(1)} %get-tuple-element.21), channel_id=1, source_target_pairs={{1,6},{3,4},{4,3},{6,1},{5,10},{7,8},{8,7},{10,5},{9,14},{11,12},{... | collective-permute-start | bytes 49160 | tf_op jit(solution)/shard_map/ppermute | solution.py:548
  14.5 12.5 %collective-permute-start.5 = (f32[288,128]{1,0:T(8,128)S(1)}, f32[288,128]{1,0:T(8,128)S(1)}, u32[]{:S(2)}, u32[]{:S(2)}) collective-permute-start(f32[288,128]{1,0:T(8,128)S(1)} %get-tuple-element.32), channel_id=1, source_target_pairs={{1,4},{3,6},{4,1},{6,3},{5,8},{7,10},{8,5},{10,7},{9,12},{11,14},{... | collective-permute-start | bytes 442376 | tf_op jit(solution)/shard_map/ppermute | solution.py:596
  16.0 11.0 %collective-permute-start.6 = (f32[288,128]{1,0:T(8,128)S(1)}, f32[288,128]{1,0:T(8,128)S(1)}, u32[]{:S(2)}, u32[]{:S(2)}) collective-permute-start(f32[288,128]{1,0:T(8,128)S(1)} %get-tuple-element.33), channel_id=1, source_target_pairs={{0,1},{1,0},{4,5},{5,4},{8,9},{9,8},{12,13},{13,12},{2,3},{3,2},{6... | collective-permute-start | bytes 442376 | tf_op jit(solution)/shard_map/ppermute | solution.py:597

commit v7 on v6

--- a/solution.py
+++ b/solution.py
@@ -125,23 +125,19 @@
 
 
 def start_own(ground_hbm, depth_hbm, ground_ref, depth_ref, sems):
-    height, width = ground_hbm.shape
-    groups = height // SUBS
-    pieces = sems.shape[1] // groups
-    part = width // pieces
+    pieces = sems.shape[1]
+    part = ground_hbm.shape[1] // pieces
     copies = []
-    for group in range(groups):
-        for piece in range(pieces):
-            where = (pl.ds(group * SUBS, SUBS), pl.ds(piece * part, part))
-            number = group * pieces + piece
-            copies.append(
-                start_all(
-                    [
-                        pltpu.make_async_copy(ground_hbm.at[where], ground_ref.at[where], sems.at[0, number]),
-                        pltpu.make_async_copy(depth_hbm.at[where], depth_ref.at[where], sems.at[1, number]),
-                    ]
-                )
+    for piece in range(pieces):
+        where = (slice(None), pl.ds(piece * part, part))
+        copies.append(
+            start_all(
+                [
+                    pltpu.make_async_copy(ground_hbm.at[where], ground_ref.at[where], sems.at[0, piece]),
+                    pltpu.make_async_copy(depth_hbm.at[where], depth_ref.at[where], sems.at[1, piece]),
+                ]
             )
+        )
     return copies
 
 
@@ -150,20 +146,19 @@
     groups = height // SUBS
     tiles = width // (SUBS * LANES)
     last_tile = width // LANES - 1
-    pieces = len(copies) // groups
-    part = width // pieces
+    part = width // len(copies)
     size = (tiles + 1) * SUBS
     place, places = chain_place()
     col, cols = lax.axis_index("cols"), lax.axis_size("cols")
     sub, lane = position()
     marks = side_marks(sides_ref)
     edges = [[] for _ in range(groups)]
-    for group in range(groups):
-        rows = pl.ds(group * SUBS, SUBS)
-        for tile in range(last_tile + 1):
-            if tile * LANES % part == 0:
-                wait_all(copies[group * pieces + tile * LANES // part])
-            columns = pl.ds(tile * LANES, LANES)
+    for tile in range(last_tile + 1):
+        if tile * LANES % part == 0:
+            wait_all(copies[tile * LANES // part])
+        columns = pl.ds(tile * LANES, LANES)
+        for group in range(groups):
+            rows = pl.ds(group * SUBS, SUBS)
             ground = ground_ref[rows, columns]
             surface = ground + depth_ref[rows, columns]
             outlets = []
@@ -221,7 +216,7 @@
     out_ref[register(row, tiles, (tiles + 1) * SUBS), :] = jnp.where(lane < LANES // 2, after, before)
 
 
-def relax_passes(passes, ground, ring):
+def relax_passes(passes, ground, ring, ahead=AHEAD):
     size = ring * SUBS
     _, lane = position()
     at_first = lane == 0
@@ -259,11 +254,11 @@
         ]
 
     makes, finishes = items(order), items(range(ring))
-    for number in range(len(makes) + AHEAD):
+    for number in range(len(makes) + ahead):
         if number < len(makes):
             make(*makes[number])
-        if number >= AHEAD:
-            done = finishes[number - AHEAD]
+        if number >= ahead:
+            done = finishes[number - ahead]
             finish(*done)
             _, _, _, count, then = passes[done[0]]
             if then is not None and done[1:] == (count // 2 - 1, ring - 1):
@@ -364,11 +359,16 @@
         tiles,
     )
     buffers = (surface_ref, other_ref)
-    passes = []
-    for step in range(1, PASSES + 1):
-        first = jnp.where(top, step, HALO + height - step)
-        passes.append((buffers[(step + 1) % 2], buffers[step % 2], first, HALO, None))
-    relax_passes(passes, ground_ref, ring)
+
+    def two_passes(pair, carry):
+        passes = []
+        for step in range(1, 3):
+            first = jnp.where(top, step + 2 * pair, HALO + height - step - 2 * pair)
+            passes.append((buffers[(step + 1) % 2], buffers[step % 2], first, HALO, None))
+        relax_passes(passes, ground_ref, ring)
+        return carry
+
+    lax.fori_loop(0, PASSES // 2, two_passes, 0)
     low, high = HALO, HALO + height - FINAL
     for row in range(FINAL):
         for slot in range(ring):
@@ -480,7 +480,7 @@
     for group in range(height // SUBS):
         first = HALO + group * SUBS
         passes.append((source, target, first, SUBS, functools.partial(unfold, group)))
-    relax_passes(passes, ground_ref, ring)
+    relax_passes(passes, ground_ref, ring, 9)
     wait_all(copies)
 
 
@@ -521,7 +521,7 @@
             pltpu.VMEM((height, width), f32),
             pltpu.VMEM(edge_rows.shape, jnp.int32),
             pltpu.VMEM(edge_sides.shape, jnp.int32),
-            pltpu.SemaphoreType.DMA((2, 4 * groups)),
+            pltpu.SemaphoreType.DMA((2, 4)),
             pltpu.SemaphoreType.DMA((3,)),
         ],
         compiler_params=limit,

time: 29.7 us -> 29.9 us (level)
  no operation moved by 1% of the time
where the time goes in v7:
time: 29.9 us; the launch traced here: 29.7 us
  blocking collectives  10.7 us (36%)
  Pallas kernels  9.67 us (32%)
  starting transfers between devices  8.21 us (27%)
  waiting for transfers between devices  1.05 us (4%)
    all_to_all x1, blocking collectives, per_device(): floors = lax.all_to_all(floors, device_axes, 0, 0, tiled=True)  10.7 us
    ppermute x2, starting transfers between devices, per_device(): far_rows = lax.ppermute(far, ('groups',) + device_axes, far_all)  4.11 us
    ppermute x3, starting transfers between devices, swap_strips(): arrived.append(lax.ppermute(piece, device_axes, pairs) if pairs else piece)  3.29 us
    pallas_call x1, Pallas kernels, per_device(): pl.pallas_call(inner, out_shape=[work, work, work], in_specs=in_vmem(8),...  2.67 us
    pallas_call x1, Pallas kernels, per_device(): pl.pallas_call(late, out_shape=jax.ShapeDtypeStruct((height, width), f32)...  2.49 us
    pallas_call x1, Pallas kernels, per_device(): pl.pallas_call(outer, out_shape=[work, work, work, pltpu.VMEM((devices, L...  2.02 us
    pallas_call x1, Pallas kernels, per_device(): pl.pallas_call(edge_kernel, out_shape=[sent, sent, strip, strip, work, wo...  1.82 us
    ppermute x3, waiting for transfers between devices, swap_strips(): arrived.append(lax.ppermute(piece, device_axes, pairs) if pairs else piece)  1.04 us
  transfers between devices with their start and end apart: 7, of which 1 were waited for; matrix products, arithmetic and copies ran while one was open for 0% of the time, Pallas kernels for 11%

profile of v7, /device:TPU:0, one launch (start us, length us, event | category | flops | bytes accessed | tf_op | source)
XLA Modules:
  0.0 29.7 jit_solution(10011377166226775148)
XLA Ops:
  0.0 1.8 %edge_rows.1 = (f32[960,128]{1,0:T(8,128)S(1)}, f32[960,128]{1,0:T(8,128)S(1)}, f32[32,128]{1,0:T(8,128)S(1)}, f32[32,128]{1,0:T(8,128)S(1)}, f32[2304,128]{1,0:...) custom-call(f32[16,8192]{1,0:T(8,128)} %ground_hbm.1, f32[16,8192]{1,0:T(8,128)} %depth_hbm.1, ...), custom_call_target="tpu_custom_call" | custom-call | flops 1024 | bytes 1024 | tf_op jit(solution)/shard_map/edge_rows/pallas_call | solution.py:514
  1.8 0.5 %collective-permute-start.2 = (f32[960,128]{1,0:T(8,128)S(1)}, f32[960,128]{1,0:T(8,128)S(1)}, u32[]{:S(2)}, u32[]{:S(2)}) collective-permute-start(f32[960,128]{1,0:T(8,128)S(1)} %get-tuple-element.23), channel_id=1, source_target_pairs={{0,1},{1,0},{4,5},{5,4},{8,9},{9,8},{12,13},{13,12},{2,3},{3,2},{6... | collective-permute-start | bytes 1474568 | tf_op jit(solution)/shard_map/ppermute | solution.py:553
  2.4 2.6 %collective-permute-start = (f32[960,128]{1,0:T(8,128)S(1)}, f32[960,128]{1,0:T(8,128)S(1)}, u32[]{:S(2)}, u32[]{:S(2)}) collective-permute-start(f32[960,128]{1,0:T(8,128)S(1)} %get-tuple-element.20), channel_id=1, source_target_pairs={{1,4},{3,6},{4,1},{6,3},{5,8},{7,10},{8,5},{10,7},{9,12},{11,14},{... | collective-permute-start | bytes 1474568 | tf_op jit(solution)/shard_map/ppermute | solution.py:552
  4.9 1.3 %collective-permute-start.4 = (f32[32,128]{1,0:T(8,128)S(1)}, f32[32,128]{1,0:T(8,128)S(1)}, u32[]{:S(2)}, u32[]{:S(2)}) collective-permute-start(f32[32,128]{1,0:T(8,128)S(1)} %get-tuple-element.21), channel_id=1, source_target_pairs={{0,3},{2,1},{1,2},{3,0},{4,7},{6,5},{5,6},{7,4},{8,11},{10,9},{9,1... | collective-permute-start | bytes 49160 | tf_op jit(solution)/shard_map/ppermute | solution.py:548
  6.2 0.5 %collective-permute-start.3 = (f32[32,128]{1,0:T(8,128)S(1)}, f32[32,128]{1,0:T(8,128)S(1)}, u32[]{:S(2)}, u32[]{:S(2)}) collective-permute-start(f32[32,128]{1,0:T(8,128)S(1)} %get-tuple-element.21), channel_id=1, source_target_pairs={{0,2},{2,0},{1,3},{3,1},{4,6},{6,4},{5,7},{7,5},{8,10},{10,8},{9,1... | collective-permute-start | bytes 49160 | tf_op jit(solution)/shard_map/ppermute | solution.py:548
  6.7 1.5 %collective-permute-start.1 = (f32[32,128]{1,0:T(8,128)S(1)}, f32[32,128]{1,0:T(8,128)S(1)}, u32[]{:S(2)}, u32[]{:S(2)}) collective-permute-start(f32[32,128]{1,0:T(8,128)S(1)} %get-tuple-element.21), channel_id=1, source_target_pairs={{1,6},{3,4},{4,3},{6,1},{5,10},{7,8},{8,7},{10,5},{9,14},{11,12},{... | collective-permute-start | bytes 49160 | tf_op jit(solution)/shard_map/ppermute | solution.py:548
  8.2 0.7 %tile_hops.1.refs_7_.refs_5_ = f32[72,128]{1,0:T(8,128)S(1)} custom-call(s32[8,6]{1,0:T(8,128)S(1)} %get-tuple-element.26.links_ref), custom_call_target="tpu_custom_call" | custom-call | flops 1024 | bytes 1024 | tf_op jit(solution)/shard_map/tile_hops/pallas_call | solution.py:556
  8.9 0.0 collective-permute-done.4.refs_3_
  8.9 1.0 %collective-permute-done.3.refs_1_ = f32[32,128]{1,0:T(8,128)S(1)} collective-permute-done((f32[32,128]{1,0:T(8,128)S(1)}, f32[32,128]{1,0:T(8,128)S(1)}, u32[]{:S(2)}, u32[]{:S(2)}) %collective-permute-start.3) | collective-permute-done | bytes 16416 | tf_op jit(solution)/shard_map/ppermute | solution.py:548
  10.0 0.0 collective-permute-done.2.refs_0_
  10.0 2.7 %inner_passes.1 = (f32[2304,128]{1,0:T(8,128)S(1)}, f32[2304,128]{1,0:T(8,128)S(1)}, f32[2304,128]{1,0:T(8,128)S(1)}) custom-call(f32[960,128]{1,0:T(8,128)S(1)} %collective-permute-done.2.refs_0_, f32[32,128]{1,0:T(8,128)S(1)} %collective-permute-done.3.refs_1_, ...), custom_call_target="tpu_custom_call", output_to_operand_aliasing={{0}: (5, {}), {1}: (6, {})} | custom-call | flops 1024 | bytes 1024 | tf_op jit(solution)/shard_map/inner_passes/pallas_call | solution.py:569
  12.6 0.0 collective-permute-done.1.refs_0_
  12.6 0.0 collective-permute-done.far_ref
  12.7 2.0 %outer_passes.1 = (f32[2304,128]{1,0:T(8,128)S(1)}, f32[2304,128]{1,0:T(8,128)S(1)}, f32[2304,128]{1,0:T(8,128)S(1)}, f32[16,128]{1,0:T(8,128)S(1)}, f32[288,128]{1,0:T(8,128)S(1)}, /*index=5*/f32[288,128]{1,0:T(8,128)S(1)}) custom-call(f32[960,128]{1,0:T(8,128)S(1)} %collective-permute-done.far_ref, ...), custom_call_target="tpu_custom_call", output_to_operand_aliasing={{0}: (3, {}), {1}: (4, {}), {2}: (5, {})} | custom-call | flops 1024 | bytes 1024 | tf_op jit(solution)/shard_map/outer_passes/pallas_call | solution.py:585
  14.7 1.5 %collective-permute-start.5 = (f32[288,128]{1,0:T(8,128)S(1)}, f32[288,128]{1,0:T(8,128)S(1)}, u32[]{:S(2)}, u32[]{:S(2)}) collective-permute-start(f32[288,128]{1,0:T(8,128)S(1)} %get-tuple-element.32), channel_id=1, source_target_pairs={{1,4},{3,6},{4,1},{6,3},{5,8},{7,10},{8,5},{10,7},{9,12},{11,14},{... | collective-permute-start | bytes 442376 | tf_op jit(solution)/shard_map/ppermute | solution.py:596
  16.2 0.3 collective-permute-start.6
  16.5 10.7 %all_to_all.11 = f32[16,1,128]{2,1,0:T(1,128)S(1)} all-to-all(f32[16,1,128]{2,1,0:T(1,128)S(1)} %bitcast.5), channel_id=1, replica_groups=mesh['groups'=2,'rows'=4,'cols'=2,'sub'=2] {'rows','cols','sub'}, dimensions={0} | all-to-all | bytes 16384 | tf_op jit(solution)/shard_map/all_to_all | solution.py:598
  27.2 0.0 collective-permute-done.5.refs_2_
  27.2 0.0 collective-permute-done.6.refs_3_
  27.2 2.5 %final_passes.1 = f32[16,8192]{1,0:T(8,128)} custom-call(f32[2304,128]{1,0:T(8,128)S(1)} %get-tuple-element.30.refs_0_, f32[2304,128]{1,0:T(8,128)S(1)} %get-tuple-element.31.refs_1_, f32[288,128]{1,0:T(8,128)S(1)} %collective-permute-done.5.refs_2_, f32[288,128]{1,0:T(8,128)S(1)} %collective-permute-done.6.refs_3_, f32[16,128]{1,0:T(8,128)S(1)} %bitcast.4, ...), custom_call_target="tpu_custom_call" | custom-call | flops 1024 | bytes 1024 | tf_op jit(solution)/shard_map/final_passes/pallas_call | solution.py:603
Async XLA Ops:
  1.8 8.1 %collective-permute-start.2 = (f32[960,128]{1,0:T(8,128)S(1)}, f32[960,128]{1,0:T(8,128)S(1)}, u32[]{:S(2)}, u32[]{:S(2)}) collective-permute-start(f32[960,128]{1,0:T(8,128)S(1)} %get-tuple-element.23), channel_id=1, source_target_pairs={{0,1},{1,0},{4,5},{5,4},{8,9},{9,8},{12,13},{13,12},{2,3},{3,2},{6... | collective-permute-start | bytes 1474568 | tf_op jit(solution)/shard_map/ppermute | solution.py:553
  2.4 10.3 %collective-permute-start = (f32[960,128]{1,0:T(8,128)S(1)}, f32[960,128]{1,0:T(8,128)S(1)}, u32[]{:S(2)}, u32[]{:S(2)}) collective-permute-start(f32[960,128]{1,0:T(8,128)S(1)} %get-tuple-element.20), channel_id=1, source_target_pairs={{1,4},{3,6},{4,1},{6,3},{5,8},{7,10},{8,5},{10,7},{9,12},{11,14},{... | collective-permute-start | bytes 1474568 | tf_op jit(solution)/shard_map/ppermute | solution.py:552
  4.9 4.0 %collective-permute-start.4 = (f32[32,128]{1,0:T(8,128)S(1)}, f32[32,128]{1,0:T(8,128)S(1)}, u32[]{:S(2)}, u32[]{:S(2)}) collective-permute-start(f32[32,128]{1,0:T(8,128)S(1)} %get-tuple-element.21), channel_id=1, source_target_pairs={{0,3},{2,1},{1,2},{3,0},{4,7},{6,5},{5,6},{7,4},{8,11},{10,9},{9,1... | collective-permute-start | bytes 49160 | tf_op jit(solution)/shard_map/ppermute | solution.py:548
  6.2 3.7 %collective-permute-start.3 = (f32[32,128]{1,0:T(8,128)S(1)}, f32[32,128]{1,0:T(8,128)S(1)}, u32[]{:S(2)}, u32[]{:S(2)}) collective-permute-start(f32[32,128]{1,0:T(8,128)S(1)} %get-tuple-element.21), channel_id=1, source_target_pairs={{0,2},{2,0},{1,3},{3,1},{4,6},{6,4},{5,7},{7,5},{8,10},{10,8},{9,1... | collective-permute-start | bytes 49160 | tf_op jit(solution)/shard_map/ppermute | solution.py:548
  6.7 5.9 %collective-permute-start.1 = (f32[32,128]{1,0:T(8,128)S(1)}, f32[32,128]{1,0:T(8,128)S(1)}, u32[]{:S(2)}, u32[]{:S(2)}) collective-permute-start(f32[32,128]{1,0:T(8,128)S(1)} %get-tuple-element.21), channel_id=1, source_target_pairs={{1,6},{3,4},{4,3},{6,1},{5,10},{7,8},{8,7},{10,5},{9,14},{11,12},{... | collective-permute-start | bytes 49160 | tf_op jit(solution)/shard_map/ppermute | solution.py:548
  14.7 12.5 %collective-permute-start.5 = (f32[288,128]{1,0:T(8,128)S(1)}, f32[288,128]{1,0:T(8,128)S(1)}, u32[]{:S(2)}, u32[]{:S(2)}) collective-permute-start(f32[288,128]{1,0:T(8,128)S(1)} %get-tuple-element.32), channel_id=1, source_target_pairs={{1,4},{3,6},{4,1},{6,3},{5,8},{7,10},{8,5},{10,7},{9,12},{11,14},{... | collective-permute-start | bytes 442376 | tf_op jit(solution)/shard_map/ppermute | solution.py:596
  16.2 11.0 %collective-permute-start.6 = (f32[288,128]{1,0:T(8,128)S(1)}, f32[288,128]{1,0:T(8,128)S(1)}, u32[]{:S(2)}, u32[]{:S(2)}) collective-permute-start(f32[288,128]{1,0:T(8,128)S(1)} %get-tuple-element.33), channel_id=1, source_target_pairs={{0,1},{1,0},{4,5},{5,4},{8,9},{9,8},{12,13},{13,12},{2,3},{3,2},{6... | collective-permute-start | bytes 442376 | tf_op jit(solution)/shard_map/ppermute | solution.py:597

commit v8 on v7

--- a/solution.py
+++ b/solution.py
@@ -216,7 +216,7 @@
     out_ref[register(row, tiles, (tiles + 1) * SUBS), :] = jnp.where(lane < LANES // 2, after, before)
 
 
-def relax_passes(passes, ground, ring, ahead=AHEAD):
+def relax_passes(passes, ground, ring):
     size = ring * SUBS
     _, lane = position()
     at_first = lane == 0
@@ -231,10 +231,10 @@
         both = jnp.minimum(values[1], values[2])
         for one, column in enumerate((jnp.minimum(values[0], both), jnp.minimum(both, values[3]))):
             rolled = pltpu.roll(column, 1, 1), pltpu.roll(column, LANES - 1, 1)
-            made[number, pair, one, slot] = (column, *rolled)
+            made[number, pair, one, slot] = (column, *rolled, values[1 + one])
 
     def finish(number, pair, slot):
-        source, target, first, _, _ = passes[number]
+        _, target, first, _, _ = passes[number]
         for one in range(2):
             row = first + 2 * pair + one
             before, here, after = [made[number, pair, one, (slot + step) % ring] for step in (-1, 0, 1)]
@@ -242,7 +242,7 @@
             from_right = jnp.where(at_last, after[2], here[2])
             lowest = jnp.minimum(jnp.minimum(from_left, from_right), here[0])
             where = register(row, slot, size)
-            raised = jnp.minimum(source[where, :], lowest + rise_step)
+            raised = jnp.minimum(here[3], lowest + rise_step)
             target[where, :] = jnp.maximum(ground[where, :], raised)
 
     def items(slots):
@@ -254,11 +254,11 @@
         ]
 
     makes, finishes = items(order), items(range(ring))
-    for number in range(len(makes) + ahead):
+    for number in range(len(makes) + AHEAD):
         if number < len(makes):
             make(*makes[number])
-        if number >= ahead:
-            done = finishes[number - ahead]
+        if number >= AHEAD:
+            done = finishes[number - AHEAD]
             finish(*done)
             _, _, _, count, then = passes[done[0]]
             if then is not None and done[1:] == (count // 2 - 1, ring - 1):
@@ -359,16 +359,11 @@
         tiles,
     )
     buffers = (surface_ref, other_ref)
-
-    def two_passes(pair, carry):
-        passes = []
-        for step in range(1, 3):
-            first = jnp.where(top, step + 2 * pair, HALO + height - step - 2 * pair)
-            passes.append((buffers[(step + 1) % 2], buffers[step % 2], first, HALO, None))
-        relax_passes(passes, ground_ref, ring)
-        return carry
-
-    lax.fori_loop(0, PASSES // 2, two_passes, 0)
+    passes = []
+    for step in range(1, PASSES + 1):
+        first = jnp.where(top, step, HALO + height - step)
+        passes.append((buffers[(step + 1) % 2], buffers[step % 2], first, HALO, None))
+    relax_passes(passes, ground_ref, ring)
     low, high = HALO, HALO + height - FINAL
     for row in range(FINAL):
         for slot in range(ring):
@@ -480,7 +475,7 @@
     for group in range(height // SUBS):
         first = HALO + group * SUBS
         passes.append((source, target, first, SUBS, functools.partial(unfold, group)))
-    relax_passes(passes, ground_ref, ring, 9)
+    relax_passes(passes, ground_ref, ring)
     wait_all(copies)
 
 

time: 29.9 us -> 29.6 us (0.990)
  no operation moved by 1% of the time
where the time goes in v8:
time: 29.6 us; the launch traced here: 29.5 us
  blocking collectives  10.7 us (36%)
  Pallas kernels  9.46 us (32%)
  starting transfers between devices  8.24 us (28%)
  waiting for transfers between devices  1.05 us (4%)
    all_to_all x1, blocking collectives, per_device(): floors = lax.all_to_all(floors, device_axes, 0, 0, tiled=True)  10.7 us
    ppermute x2, starting transfers between devices, per_device(): far_rows = lax.ppermute(far, ('groups',) + device_axes, far_all)  4.15 us
    ppermute x3, starting transfers between devices, swap_strips(): arrived.append(lax.ppermute(piece, device_axes, pairs) if pairs else piece)  3.29 us
    pallas_call x1, Pallas kernels, per_device(): pl.pallas_call(inner, out_shape=[work, work, work], in_specs=in_vmem(8),...  2.68 us
    pallas_call x1, Pallas kernels, per_device(): pl.pallas_call(late, out_shape=jax.ShapeDtypeStruct((height, width), f32)...  2.52 us
    pallas_call x1, Pallas kernels, per_device(): pl.pallas_call(edge_kernel, out_shape=[sent, sent, strip, strip, work, wo...  1.82 us
    pallas_call x1, Pallas kernels, per_device(): pl.pallas_call(outer, out_shape=[work, work, work, pltpu.VMEM((devices, L...  1.78 us
    ppermute x3, waiting for transfers between devices, swap_strips(): arrived.append(lax.ppermute(piece, device_axes, pairs) if pairs else piece)  1.04 us
  transfers between devices with their start and end apart: 7, of which 1 were waited for; matrix products, arithmetic and copies ran while one was open for 0% of the time, Pallas kernels for 11%

profile of v8, /device:TPU:0, one launch (start us, length us, event | category | flops | bytes accessed | tf_op | source)
XLA Modules:
  0.0 29.5 jit_solution(17950075599325585710)
XLA Ops:
  0.0 1.8 %edge_rows.1 = (f32[960,128]{1,0:T(8,128)S(1)}, f32[960,128]{1,0:T(8,128)S(1)}, f32[32,128]{1,0:T(8,128)S(1)}, f32[32,128]{1,0:T(8,128)S(1)}, f32[2304,128]{1,0:...) custom-call(f32[16,8192]{1,0:T(8,128)} %ground_hbm.1, f32[16,8192]{1,0:T(8,128)} %depth_hbm.1, ...), custom_call_target="tpu_custom_call" | custom-call | flops 1024 | bytes 1024 | tf_op jit(solution)/shard_map/edge_rows/pallas_call | solution.py:509
  1.8 0.5 %collective-permute-start.2 = (f32[960,128]{1,0:T(8,128)S(1)}, f32[960,128]{1,0:T(8,128)S(1)}, u32[]{:S(2)}, u32[]{:S(2)}) collective-permute-start(f32[960,128]{1,0:T(8,128)S(1)} %get-tuple-element.23), channel_id=1, source_target_pairs={{0,1},{1,0},{4,5},{5,4},{8,9},{9,8},{12,13},{13,12},{2,3},{3,2},{6... | collective-permute-start | bytes 1474568 | tf_op jit(solution)/shard_map/ppermute | solution.py:548
  2.4 2.6 %collective-permute-start = (f32[960,128]{1,0:T(8,128)S(1)}, f32[960,128]{1,0:T(8,128)S(1)}, u32[]{:S(2)}, u32[]{:S(2)}) collective-permute-start(f32[960,128]{1,0:T(8,128)S(1)} %get-tuple-element.20), channel_id=1, source_target_pairs={{1,4},{3,6},{4,1},{6,3},{5,8},{7,10},{8,5},{10,7},{9,12},{11,14},{... | collective-permute-start | bytes 1474568 | tf_op jit(solution)/shard_map/ppermute | solution.py:547
  4.9 1.3 %collective-permute-start.4 = (f32[32,128]{1,0:T(8,128)S(1)}, f32[32,128]{1,0:T(8,128)S(1)}, u32[]{:S(2)}, u32[]{:S(2)}) collective-permute-start(f32[32,128]{1,0:T(8,128)S(1)} %get-tuple-element.21), channel_id=1, source_target_pairs={{0,3},{2,1},{1,2},{3,0},{4,7},{6,5},{5,6},{7,4},{8,11},{10,9},{9,1... | collective-permute-start | bytes 49160 | tf_op jit(solution)/shard_map/ppermute | solution.py:543
  6.2 0.5 %collective-permute-start.3 = (f32[32,128]{1,0:T(8,128)S(1)}, f32[32,128]{1,0:T(8,128)S(1)}, u32[]{:S(2)}, u32[]{:S(2)}) collective-permute-start(f32[32,128]{1,0:T(8,128)S(1)} %get-tuple-element.21), channel_id=1, source_target_pairs={{0,2},{2,0},{1,3},{3,1},{4,6},{6,4},{5,7},{7,5},{8,10},{10,8},{9,1... | collective-permute-start | bytes 49160 | tf_op jit(solution)/shard_map/ppermute | solution.py:543
  6.7 1.5 %collective-permute-start.1 = (f32[32,128]{1,0:T(8,128)S(1)}, f32[32,128]{1,0:T(8,128)S(1)}, u32[]{:S(2)}, u32[]{:S(2)}) collective-permute-start(f32[32,128]{1,0:T(8,128)S(1)} %get-tuple-element.21), channel_id=1, source_target_pairs={{1,6},{3,4},{4,3},{6,1},{5,10},{7,8},{8,7},{10,5},{9,14},{11,12},{... | collective-permute-start | bytes 49160 | tf_op jit(solution)/shard_map/ppermute | solution.py:543
  8.2 0.7 %tile_hops.1.refs_7_.refs_5_ = f32[72,128]{1,0:T(8,128)S(1)} custom-call(s32[8,6]{1,0:T(8,128)S(1)} %get-tuple-element.26.links_ref), custom_call_target="tpu_custom_call" | custom-call | flops 1024 | bytes 1024 | tf_op jit(solution)/shard_map/tile_hops/pallas_call | solution.py:551
  8.9 0.0 collective-permute-done.4.refs_3_
  8.9 1.0 %collective-permute-done.3.refs_1_ = f32[32,128]{1,0:T(8,128)S(1)} collective-permute-done((f32[32,128]{1,0:T(8,128)S(1)}, f32[32,128]{1,0:T(8,128)S(1)}, u32[]{:S(2)}, u32[]{:S(2)}) %collective-permute-start.3) | collective-permute-done | bytes 16416 | tf_op jit(solution)/shard_map/ppermute | solution.py:543
  10.0 0.0 collective-permute-done.2.refs_0_
  10.0 2.7 %inner_passes.1 = (f32[2304,128]{1,0:T(8,128)S(1)}, f32[2304,128]{1,0:T(8,128)S(1)}, f32[2304,128]{1,0:T(8,128)S(1)}) custom-call(f32[960,128]{1,0:T(8,128)S(1)} %collective-permute-done.2.refs_0_, f32[32,128]{1,0:T(8,128)S(1)} %collective-permute-done.3.refs_1_, ...), custom_call_target="tpu_custom_call", output_to_operand_aliasing={{0}: (5, {}), {1}: (6, {})} | custom-call | flops 1024 | bytes 1024 | tf_op jit(solution)/shard_map/inner_passes/pallas_call | solution.py:564
  12.6 0.0 collective-permute-done.1.refs_0_
  12.6 0.0 collective-permute-done.far_ref
  12.7 1.8 %outer_passes.1 = (f32[2304,128]{1,0:T(8,128)S(1)}, f32[2304,128]{1,0:T(8,128)S(1)}, f32[2304,128]{1,0:T(8,128)S(1)}, f32[16,128]{1,0:T(8,128)S(1)}, f32[288,128]{1,0:T(8,128)S(1)}, /*index=5*/f32[288,128]{1,0:T(8,128)S(1)}) custom-call(f32[960,128]{1,0:T(8,128)S(1)} %collective-permute-done.far_ref, ...), custom_call_target="tpu_custom_call", output_to_operand_aliasing={{0}: (3, {}), {1}: (4, {}), {2}: (5, {})} | custom-call | flops 1024 | bytes 1024 | tf_op jit(solution)/shard_map/outer_passes/pallas_call | solution.py:580
  14.4 1.6 %collective-permute-start.5 = (f32[288,128]{1,0:T(8,128)S(1)}, f32[288,128]{1,0:T(8,128)S(1)}, u32[]{:S(2)}, u32[]{:S(2)}) collective-permute-start(f32[288,128]{1,0:T(8,128)S(1)} %get-tuple-element.32), channel_id=1, source_target_pairs={{1,4},{3,6},{4,1},{6,3},{5,8},{7,10},{8,5},{10,7},{9,12},{11,14},{... | collective-permute-start | bytes 442376 | tf_op jit(solution)/shard_map/ppermute | solution.py:591
  16.0 0.3 collective-permute-start.6
  16.3 10.7 %all_to_all.11 = f32[16,1,128]{2,1,0:T(1,128)S(1)} all-to-all(f32[16,1,128]{2,1,0:T(1,128)S(1)} %bitcast.5), channel_id=1, replica_groups=mesh['groups'=2,'rows'=4,'cols'=2,'sub'=2] {'rows','cols','sub'}, dimensions={0} | all-to-all | bytes 16384 | tf_op jit(solution)/shard_map/all_to_all | solution.py:593
  26.9 0.0 collective-permute-done.5.refs_2_
  27.0 0.0 collective-permute-done.6.refs_3_
  27.0 2.5 %final_passes.1 = f32[16,8192]{1,0:T(8,128)} custom-call(f32[2304,128]{1,0:T(8,128)S(1)} %get-tuple-element.30.refs_0_, f32[2304,128]{1,0:T(8,128)S(1)} %get-tuple-element.31.refs_1_, f32[288,128]{1,0:T(8,128)S(1)} %collective-permute-done.5.refs_2_, f32[288,128]{1,0:T(8,128)S(1)} %collective-permute-done.6.refs_3_, f32[16,128]{1,0:T(8,128)S(1)} %bitcast.4, ...), custom_call_target="tpu_custom_call" | custom-call | flops 1024 | bytes 1024 | tf_op jit(solution)/shard_map/final_passes/pallas_call | solution.py:598
Async XLA Ops:
  1.8 8.1 %collective-permute-start.2 = (f32[960,128]{1,0:T(8,128)S(1)}, f32[960,128]{1,0:T(8,128)S(1)}, u32[]{:S(2)}, u32[]{:S(2)}) collective-permute-start(f32[960,128]{1,0:T(8,128)S(1)} %get-tuple-element.23), channel_id=1, source_target_pairs={{0,1},{1,0},{4,5},{5,4},{8,9},{9,8},{12,13},{13,12},{2,3},{3,2},{6... | collective-permute-start | bytes 1474568 | tf_op jit(solution)/shard_map/ppermute | solution.py:548
  2.4 10.3 %collective-permute-start = (f32[960,128]{1,0:T(8,128)S(1)}, f32[960,128]{1,0:T(8,128)S(1)}, u32[]{:S(2)}, u32[]{:S(2)}) collective-permute-start(f32[960,128]{1,0:T(8,128)S(1)} %get-tuple-element.20), channel_id=1, source_target_pairs={{1,4},{3,6},{4,1},{6,3},{5,8},{7,10},{8,5},{10,7},{9,12},{11,14},{... | collective-permute-start | bytes 1474568 | tf_op jit(solution)/shard_map/ppermute | solution.py:547
  4.9 4.0 %collective-permute-start.4 = (f32[32,128]{1,0:T(8,128)S(1)}, f32[32,128]{1,0:T(8,128)S(1)}, u32[]{:S(2)}, u32[]{:S(2)}) collective-permute-start(f32[32,128]{1,0:T(8,128)S(1)} %get-tuple-element.21), channel_id=1, source_target_pairs={{0,3},{2,1},{1,2},{3,0},{4,7},{6,5},{5,6},{7,4},{8,11},{10,9},{9,1... | collective-permute-start | bytes 49160 | tf_op jit(solution)/shard_map/ppermute | solution.py:543
  6.2 3.7 %collective-permute-start.3 = (f32[32,128]{1,0:T(8,128)S(1)}, f32[32,128]{1,0:T(8,128)S(1)}, u32[]{:S(2)}, u32[]{:S(2)}) collective-permute-start(f32[32,128]{1,0:T(8,128)S(1)} %get-tuple-element.21), channel_id=1, source_target_pairs={{0,2},{2,0},{1,3},{3,1},{4,6},{6,4},{5,7},{7,5},{8,10},{10,8},{9,1... | collective-permute-start | bytes 49160 | tf_op jit(solution)/shard_map/ppermute | solution.py:543
  6.7 5.9 %collective-permute-start.1 = (f32[32,128]{1,0:T(8,128)S(1)}, f32[32,128]{1,0:T(8,128)S(1)}, u32[]{:S(2)}, u32[]{:S(2)}) collective-permute-start(f32[32,128]{1,0:T(8,128)S(1)} %get-tuple-element.21), channel_id=1, source_target_pairs={{1,6},{3,4},{4,3},{6,1},{5,10},{7,8},{8,7},{10,5},{9,14},{11,12},{... | collective-permute-start | bytes 49160 | tf_op jit(solution)/shard_map/ppermute | solution.py:543
  14.4 12.5 %collective-permute-start.5 = (f32[288,128]{1,0:T(8,128)S(1)}, f32[288,128]{1,0:T(8,128)S(1)}, u32[]{:S(2)}, u32[]{:S(2)}) collective-permute-start(f32[288,128]{1,0:T(8,128)S(1)} %get-tuple-element.32), channel_id=1, source_target_pairs={{1,4},{3,6},{4,1},{6,3},{5,8},{7,10},{8,5},{10,7},{9,12},{11,14},{... | collective-permute-start | bytes 442376 | tf_op jit(solution)/shard_map/ppermute | solution.py:591
  16.0 11.0 %collective-permute-start.6 = (f32[288,128]{1,0:T(8,128)S(1)}, f32[288,128]{1,0:T(8,128)S(1)}, u32[]{:S(2)}, u32[]{:S(2)}) collective-permute-start(f32[288,128]{1,0:T(8,128)S(1)} %get-tuple-element.33), channel_id=1, source_target_pairs={{0,1},{1,0},{4,5},{5,4},{8,9},{9,8},{12,13},{13,12},{2,3},{3,2},{6... | collective-permute-start | bytes 442376 | tf_op jit(solution)/shard_map/ppermute | solution.py:592

commit v9 on v8

--- a/solution.py
+++ b/solution.py
@@ -13,6 +13,7 @@
 HALO = PASSES
 SUBS = 8
 LANES = 128
+WANTED = 16
 AHEAD = 5
 
 unreached = 1000000000.0
@@ -273,21 +274,19 @@
     for edge in range(1, degree):
         linked = linked | (links[:, edge : edge + 1] == number)
     linked = linked.astype(jnp.float32)
-    tile = lax.broadcasted_iota(jnp.int32, (tiles, LANES), 0)
-    lane = lax.broadcasted_iota(jnp.int32, (tiles, LANES), 1)
-    reached = jnp.zeros((tiles, LANES), jnp.float32)
-    for index, wanted in enumerate(needed):
-        reached = jnp.where((lane == index) & (tile == wanted), 1.0, reached)
+    index = lax.broadcasted_iota(jnp.int32, (WANTED, tiles), 0)
+    tile = lax.broadcasted_iota(jnp.int32, (WANTED, tiles), 1)
+    reached = jnp.zeros((WANTED, tiles), jnp.float32)
+    for number, wanted in enumerate(needed):
+        reached = jnp.where((index == number) & (tile == wanted), 1.0, reached)
     hops = jnp.where(reached > 0.5, 0.0, float(ROUNDS + 1))
     for hop in range(1, ROUNDS + 1):
-        reached = lax.dot_general(
-            linked, reached, (((0,), (0,)), ((), ())), preferred_element_type=jnp.float32
-        )
+        reached = jnp.dot(reached, linked, preferred_element_type=jnp.float32)
         reached = jnp.where(reached > 0.5, 1.0, 0.0)
         hops = jnp.minimum(hops, jnp.where(reached > 0.5, float(hop), float(ROUNDS + 1)))
-    for index in range(len(needed)):
-        hops_ref[pl.ds(index * tiles, tiles), :] = jnp.broadcast_to(
-            hops[:, index : index + 1], (tiles, LANES)
+    for number in range(tiles):
+        hops_ref[pl.ds(number * WANTED, WANTED), :] = jnp.broadcast_to(
+            hops[:, number : number + 1], (WANTED, LANES)
         )
 
 
@@ -306,8 +305,14 @@
     hop_counts(links_ref, hops_ref, needed_tiles())
 
 
+def copy_rows(source, first, target, ring):
+    for row in range(FINAL):
+        for slot in range(ring):
+            target[register(row, slot, ring * SUBS), :] = source[register(first + row, slot, ring * SUBS), :]
+
+
 def inner_kernel(height, tiles, near_ref, own_even_ref, own_odd_ref, near_even_ref, near_odd_ref, *refs):
-    ground_ref, surface_ref, other_ref = refs[3:]
+    ground_ref, surface_ref, other_ref, near_out = refs[3:]
     own_strips, near_strips = (own_even_ref, own_odd_ref), (near_even_ref, near_odd_ref)
     ring = tiles + 1
     size = ring * SUBS
@@ -338,10 +343,11 @@
         first = step + jnp.where(top, HALO, 0)
         passes.append((buffers[(step + 1) % 2], buffers[step % 2], first, height + HALO - 2 * step, None))
     relax_passes(passes, ground_ref, ring)
+    copy_rows(surface_ref, jnp.where(top, HALO + height - FINAL, HALO), near_out, ring)
 
 
 def outer_kernel(height, tiles, far_ref, even_ref, odd_ref, *refs):
-    ground_ref, surface_ref, other_ref, level_ref, far_out, near_out = refs[3:9]
+    ground_ref, surface_ref, other_ref, level_ref, far_out = refs[3:8]
     ring = tiles + 1
     size = ring * SUBS
     place, places = chain_place()
@@ -364,12 +370,7 @@
         first = jnp.where(top, step, HALO + height - step)
         passes.append((buffers[(step + 1) % 2], buffers[step % 2], first, HALO, None))
     relax_passes(passes, ground_ref, ring)
-    low, high = HALO, HALO + height - FINAL
-    for row in range(FINAL):
-        for slot in range(ring):
-            where = register(row, slot, size)
-            far_out[where, :] = surface_ref[register(jnp.where(top, low, high) + row, slot, size), :]
-            near_out[where, :] = surface_ref[register(jnp.where(top, high, low) + row, slot, size), :]
+    copy_rows(surface_ref, jnp.where(top, HALO, HALO + height - FINAL), far_out, ring)
     band, bands = lax.axis_index("sub"), lax.axis_size("sub")
     sub, lane = position()
 
@@ -408,25 +409,24 @@
 
 def late_kernel(
     height, tiles, ground_ref, surface_ref, far_ref, near_ref, floors_ref, hops_ref, out_hbm,
-    one_ref, two_ref, out_ref, sems,
+    one_ref, two_ref, out_ref, ceilings_ref, sems,
 ):
     ring = tiles + 1
     size = ring * SUBS
     sub, lane = position()
     bands = lax.axis_size("sub")
-    count = floors_ref.shape[0] // bands
-    level = least(floors_ref[pl.ds(band, count, stride=bands), :] for band in range(bands))
-    raised = [level]
-    for hop in range(ROUNDS):
-        raised.append(raised[-1] + hop_rise)
-    ceilings = []
-    for index in range(9):
-        hops = hops_ref[pl.ds(index * count, count), :]
-        lowest = jnp.full((count, LANES), unreached, jnp.float32)
+    offers = []
+    for tile in range(floors_ref.shape[0] // bands):
+        raised = [least(floors_ref[pl.ds(tile * bands + band, 1), :] for band in range(bands))]
+        for hop in range(ROUNDS):
+            raised.append(raised[-1] + hop_rise)
+        hops = hops_ref[pl.ds(tile * WANTED, WANTED), :]
+        offer = jnp.full((WANTED, LANES), unreached, jnp.float32)
         for hop in range(ROUNDS + 1):
-            lowest = jnp.where(hops == float(hop), raised[hop], lowest)
-        lowest = jnp.min(lowest, axis=0, keepdims=True) + spill_lift
-        ceilings.append(jnp.broadcast_to(lowest, (SUBS, LANES)))
+            offer = jnp.where(hops == float(hop), raised[hop], offer)
+        offers.append(offer)
+    ceilings_ref[...] = least(offers) + spill_lift
+    ceilings = [jnp.broadcast_to(ceilings_ref[pl.ds(index, 1), :], (SUBS, LANES)) for index in range(9)]
     pairs = []
     for region in range(3):
         left, middle, right = ceilings[3 * region : 3 * region + 3]
@@ -464,13 +464,17 @@
 
     def unfold(group):
         first = HALO + group * SUBS
+        half = tiles * SUBS // 2
         for tile in range(tiles * SUBS):
             chunk, slot = tile // tiles, tile % tiles
             out_ref[pl.ds(group * SUBS, SUBS), pl.ds(tile * LANES, LANES)] = target[
                 pl.ds(first * size + slot * SUBS + chunk, SUBS, stride=size), :
             ]
-        where = (pl.ds(group * SUBS, SUBS), slice(None))
-        copies.extend(start_all([pltpu.make_async_copy(out_ref.at[where], out_hbm.at[where], sems.at[group])]))
+            if tile % half == half - 1:
+                side = tile // half
+                where = (pl.ds(group * SUBS, SUBS), pl.ds(side * half * LANES, half * LANES))
+                copy = pltpu.make_async_copy(out_ref.at[where], out_hbm.at[where], sems.at[group, side])
+                copies.extend(start_all([copy]))
 
     for group in range(height // SUBS):
         first = HALO + group * SUBS
@@ -550,7 +554,7 @@
 
     hops = pl.pallas_call(
         hops_kernel,
-        out_shape=pltpu.VMEM((9 * tile_count, LANES), f32),
+        out_shape=pltpu.VMEM((WANTED * tile_count, LANES), f32),
         in_specs=in_vmem(1),
         out_specs=pl.BlockSpec(memory_space=pltpu.VMEM),
         compiler_params=limit,
@@ -561,11 +565,12 @@
     def inner(*refs):
         inner_kernel(height, tiles, *refs)
 
-    ground, surface, other = pl.pallas_call(
+    again = pltpu.VMEM((FINAL * size, LANES), f32)
+    ground, surface, other, near = pl.pallas_call(
         inner,
-        out_shape=[work, work, work],
+        out_shape=[work, work, work, again],
         in_specs=in_vmem(8),
-        out_specs=in_vmem(3),
+        out_specs=in_vmem(4),
         input_output_aliases={5: 0, 6: 1},
         compiler_params=limit,
         cost_estimate=short,
@@ -576,12 +581,11 @@
         outer_kernel(height, tiles, far_ref, *refs)
 
     devices = lax.axis_size(device_axes)
-    again = pltpu.VMEM((FINAL * size, LANES), f32)
-    ground, surface, other, floors, far, near = pl.pallas_call(
+    ground, surface, other, floors, far = pl.pallas_call(
         outer,
-        out_shape=[work, work, work, pltpu.VMEM((devices, LANES), f32), again, again],
+        out_shape=[work, work, work, pltpu.VMEM((devices, LANES), f32), again],
         in_specs=in_vmem(6),
-        out_specs=in_vmem(6),
+        out_specs=in_vmem(5),
         input_output_aliases={3: 0, 4: 1, 5: 2},
         compiler_params=limit,
         cost_estimate=short,
@@ -604,7 +608,8 @@
             work,
             work,
             pltpu.VMEM((height, width), f32),
-            pltpu.SemaphoreType.DMA((groups,)),
+            pltpu.VMEM((WANTED, LANES), f32),
+            pltpu.SemaphoreType.DMA((groups, 2)),
         ],
         compiler_params=limit,
         cost_estimate=short,

time: 29.6 us -> 29.5 us (level)
  no operation moved by 1% of the time
where the time goes in v9:
time: 29.5 us; the launch traced here: 29.4 us
  blocking collectives  10.7 us (36%)
  Pallas kernels  9.26 us (31%)
  starting transfers between devices  8.3 us (28%)
  waiting for transfers between devices  1.1 us (4%)
    all_to_all x1, blocking collectives, per_device(): floors = lax.all_to_all(floors, device_axes, 0, 0, tiled=True)  10.7 us
    ppermute x2, starting transfers between devices, per_device(): far_rows = lax.ppermute(far, ('groups',) + device_axes, far_all)  4.14 us
    ppermute x3, starting transfers between devices, swap_strips(): arrived.append(lax.ppermute(piece, device_axes, pairs) if pairs else piece)  3.29 us
    pallas_call x1, Pallas kernels, per_device(): pl.pallas_call(inner, out_shape=[work, work, work, again], in_specs=in_vm...  2.62 us
    pallas_call x1, Pallas kernels, per_device(): pl.pallas_call(late, out_shape=jax.ShapeDtypeStruct((height, width), f32)...  2.44 us
    pallas_call x1, Pallas kernels, per_device(): pl.pallas_call(edge_kernel, out_shape=[sent, sent, strip, strip, work, wo...  1.82 us
    pallas_call x1, Pallas kernels, per_device(): pl.pallas_call(outer, out_shape=[work, work, work, pltpu.VMEM((devices, L...  1.76 us
    ppermute x3, waiting for transfers between devices, swap_strips(): arrived.append(lax.ppermute(piece, device_axes, pairs) if pairs else piece)  1.09 us
  transfers between devices with their start and end apart: 7, of which 1 were waited for; matrix products, arithmetic and copies ran while one was open for 0% of the time, Pallas kernels for 11%

profile of v9, /device:TPU:0, one launch (start us, length us, event | category | flops | bytes accessed | tf_op | source)
XLA Modules:
  0.0 29.4 jit_solution(7117493536698155050)
XLA Ops:
  0.0 1.8 %edge_rows.1 = (f32[960,128]{1,0:T(8,128)S(1)}, f32[960,128]{1,0:T(8,128)S(1)}, f32[32,128]{1,0:T(8,128)S(1)}, f32[32,128]{1,0:T(8,128)S(1)}, f32[2304,128]{1,0:...) custom-call(f32[16,8192]{1,0:T(8,128)} %ground_hbm.1, f32[16,8192]{1,0:T(8,128)} %depth_hbm.1, ...), custom_call_target="tpu_custom_call" | custom-call | flops 1024 | bytes 1024 | tf_op jit(solution)/shard_map/edge_rows/pallas_call | solution.py:513
  1.8 0.5 %collective-permute-start.2 = (f32[960,128]{1,0:T(8,128)S(1)}, f32[960,128]{1,0:T(8,128)S(1)}, u32[]{:S(2)}, u32[]{:S(2)}) collective-permute-start(f32[960,128]{1,0:T(8,128)S(1)} %get-tuple-element.23), channel_id=1, source_target_pairs={{0,1},{1,0},{4,5},{5,4},{8,9},{9,8},{12,13},{13,12},{2,3},{3,2},{6... | collective-permute-start | bytes 1474568 | tf_op jit(solution)/shard_map/ppermute | solution.py:552
  2.3 2.6 %collective-permute-start = (f32[960,128]{1,0:T(8,128)S(1)}, f32[960,128]{1,0:T(8,128)S(1)}, u32[]{:S(2)}, u32[]{:S(2)}) collective-permute-start(f32[960,128]{1,0:T(8,128)S(1)} %get-tuple-element.20), channel_id=1, source_target_pairs={{1,4},{3,6},{4,1},{6,3},{5,8},{7,10},{8,5},{10,7},{9,12},{11,14},{... | collective-permute-start | bytes 1474568 | tf_op jit(solution)/shard_map/ppermute | solution.py:551
  4.9 1.3 %collective-permute-start.4 = (f32[32,128]{1,0:T(8,128)S(1)}, f32[32,128]{1,0:T(8,128)S(1)}, u32[]{:S(2)}, u32[]{:S(2)}) collective-permute-start(f32[32,128]{1,0:T(8,128)S(1)} %get-tuple-element.21), channel_id=1, source_target_pairs={{0,3},{2,1},{1,2},{3,0},{4,7},{6,5},{5,6},{7,4},{8,11},{10,9},{9,1... | collective-permute-start | bytes 49160 | tf_op jit(solution)/shard_map/ppermute | solution.py:547
  6.2 0.5 %collective-permute-start.3 = (f32[32,128]{1,0:T(8,128)S(1)}, f32[32,128]{1,0:T(8,128)S(1)}, u32[]{:S(2)}, u32[]{:S(2)}) collective-permute-start(f32[32,128]{1,0:T(8,128)S(1)} %get-tuple-element.21), channel_id=1, source_target_pairs={{0,2},{2,0},{1,3},{3,1},{4,6},{6,4},{5,7},{7,5},{8,10},{10,8},{9,1... | collective-permute-start | bytes 49160 | tf_op jit(solution)/shard_map/ppermute | solution.py:547
  6.7 1.5 %collective-permute-start.1 = (f32[32,128]{1,0:T(8,128)S(1)}, f32[32,128]{1,0:T(8,128)S(1)}, u32[]{:S(2)}, u32[]{:S(2)}) collective-permute-start(f32[32,128]{1,0:T(8,128)S(1)} %get-tuple-element.21), channel_id=1, source_target_pairs={{1,6},{3,4},{4,3},{6,1},{5,10},{7,8},{8,7},{10,5},{9,14},{11,12},{... | collective-permute-start | bytes 49160 | tf_op jit(solution)/shard_map/ppermute | solution.py:547
  8.2 0.6 %tile_hops.1.refs_7_.refs_5_ = f32[128,128]{1,0:T(8,128)S(1)} custom-call(s32[8,6]{1,0:T(8,128)S(1)} %get-tuple-element.26.links_ref), custom_call_target="tpu_custom_call" | custom-call | flops 1024 | bytes 1024 | tf_op jit(solution)/shard_map/tile_hops/pallas_call | solution.py:555
  8.9 0.0 collective-permute-done.4.refs_3_
  8.9 1.1 %collective-permute-done.3.refs_1_ = f32[32,128]{1,0:T(8,128)S(1)} collective-permute-done((f32[32,128]{1,0:T(8,128)S(1)}, f32[32,128]{1,0:T(8,128)S(1)}, u32[]{:S(2)}, u32[]{:S(2)}) %collective-permute-start.3) | collective-permute-done | bytes 16416 | tf_op jit(solution)/shard_map/ppermute | solution.py:547
  9.9 0.0 collective-permute-done.2.refs_0_
  10.0 2.6 %inner_passes.1 = (f32[2304,128]{1,0:T(8,128)S(1)}, f32[2304,128]{1,0:T(8,128)S(1)}, f32[2304,128]{1,0:T(8,128)S(1)}, f32[288,128]{1,0:T(8,128)S(1)}) custom-call(f32[960,128]{1,0:T(8,128)S(1)} %collective-permute-done.2.refs_0_, f32[32,128]{1,0:T(8,128)S(1)} %collective-permute-done.3.refs_1_, ...), custom_call_target="tpu_custom_call", output_to_operand_aliasing={{0}: (5, {}), {1}: (6, {})} | custom-call | flops 1024 | bytes 1024 | tf_op jit(solution)/shard_map/inner_passes/pallas_call | solution.py:569
  12.6 0.0 collective-permute-done.1.refs_0_
  12.6 0.0 collective-permute-done.far_ref
  12.6 1.8 %outer_passes.1 = (f32[2304,128]{1,0:T(8,128)S(1)}, f32[2304,128]{1,0:T(8,128)S(1)}, f32[2304,128]{1,0:T(8,128)S(1)}, f32[16,128]{1,0:T(8,128)S(1)}, f32[288,128]{1,0:T(8,128)S(1)}) custom-call(f32[960,128]{1,0:T(8,128)S(1)} %collective-permute-done.far_ref, ...), custom_call_target="tpu_custom_call", output_to_operand_aliasing={{0}: (3, {}), {1}: (4, {}), {2}: (5, {})} | custom-call | flops 1024 | bytes 1024 | tf_op jit(solution)/shard_map/outer_passes/pallas_call | solution.py:584
  14.4 1.6 %collective-permute-start.5 = (f32[288,128]{1,0:T(8,128)S(1)}, f32[288,128]{1,0:T(8,128)S(1)}, u32[]{:S(2)}, u32[]{:S(2)}) collective-permute-start(f32[288,128]{1,0:T(8,128)S(1)} %get-tuple-element.32), channel_id=1, source_target_pairs={{1,4},{3,6},{4,1},{6,3},{5,8},{7,10},{8,5},{10,7},{9,12},{11,14},{... | collective-permute-start | bytes 442376 | tf_op jit(solution)/shard_map/ppermute | solution.py:595
  15.9 0.3 %collective-permute-start.6 = (f32[288,128]{1,0:T(8,128)S(1)}, f32[288,128]{1,0:T(8,128)S(1)}, u32[]{:S(2)}, u32[]{:S(2)}) collective-permute-start(f32[288,128]{1,0:T(8,128)S(1)} %get-tuple-element.33), channel_id=1, source_target_pairs={{0,1},{1,0},{4,5},{5,4},{8,9},{9,8},{12,13},{13,12},{2,3},{3,2},{6... | collective-permute-start | bytes 442376 | tf_op jit(solution)/shard_map/ppermute | solution.py:596
  16.2 10.7 %all_to_all.11 = f32[16,1,128]{2,1,0:T(1,128)S(1)} all-to-all(f32[16,1,128]{2,1,0:T(1,128)S(1)} %bitcast.5), channel_id=1, replica_groups=mesh['groups'=2,'rows'=4,'cols'=2,'sub'=2] {'rows','cols','sub'}, dimensions={0} | all-to-all | bytes 16384 | tf_op jit(solution)/shard_map/all_to_all | solution.py:597
  26.9 0.0 collective-permute-done.5.refs_2_
  26.9 0.0 collective-permute-done.6.refs_3_
  26.9 2.4 %final_passes.1 = f32[16,8192]{1,0:T(8,128)} custom-call(f32[2304,128]{1,0:T(8,128)S(1)} %get-tuple-element.30.refs_0_, f32[2304,128]{1,0:T(8,128)S(1)} %get-tuple-element.31.refs_1_, f32[288,128]{1,0:T(8,128)S(1)} %collective-permute-done.5.refs_2_, f32[288,128]{1,0:T(8,128)S(1)} %collective-permute-done.6.refs_3_, f32[16,128]{1,0:T(8,128)S(1)} %bitcast.4, ...), custom_call_target="tpu_custom_call" | custom-call | flops 1024 | bytes 1024 | tf_op jit(solution)/shard_map/final_passes/pallas_call | solution.py:602
Async XLA Ops:
  1.8 8.1 %collective-permute-start.2 = (f32[960,128]{1,0:T(8,128)S(1)}, f32[960,128]{1,0:T(8,128)S(1)}, u32[]{:S(2)}, u32[]{:S(2)}) collective-permute-start(f32[960,128]{1,0:T(8,128)S(1)} %get-tuple-element.23), channel_id=1, source_target_pairs={{0,1},{1,0},{4,5},{5,4},{8,9},{9,8},{12,13},{13,12},{2,3},{3,2},{6... | collective-permute-start | bytes 1474568 | tf_op jit(solution)/shard_map/ppermute | solution.py:552
  2.3 10.2 %collective-permute-start = (f32[960,128]{1,0:T(8,128)S(1)}, f32[960,128]{1,0:T(8,128)S(1)}, u32[]{:S(2)}, u32[]{:S(2)}) collective-permute-start(f32[960,128]{1,0:T(8,128)S(1)} %get-tuple-element.20), channel_id=1, source_target_pairs={{1,4},{3,6},{4,1},{6,3},{5,8},{7,10},{8,5},{10,7},{9,12},{11,14},{... | collective-permute-start | bytes 1474568 | tf_op jit(solution)/shard_map/ppermute | solution.py:551
  4.9 3.9 %collective-permute-start.4 = (f32[32,128]{1,0:T(8,128)S(1)}, f32[32,128]{1,0:T(8,128)S(1)}, u32[]{:S(2)}, u32[]{:S(2)}) collective-permute-start(f32[32,128]{1,0:T(8,128)S(1)} %get-tuple-element.21), channel_id=1, source_target_pairs={{0,3},{2,1},{1,2},{3,0},{4,7},{6,5},{5,6},{7,4},{8,11},{10,9},{9,1... | collective-permute-start | bytes 49160 | tf_op jit(solution)/shard_map/ppermute | solution.py:547
  6.2 3.7 %collective-permute-start.3 = (f32[32,128]{1,0:T(8,128)S(1)}, f32[32,128]{1,0:T(8,128)S(1)}, u32[]{:S(2)}, u32[]{:S(2)}) collective-permute-start(f32[32,128]{1,0:T(8,128)S(1)} %get-tuple-element.21), channel_id=1, source_target_pairs={{0,2},{2,0},{1,3},{3,1},{4,6},{6,4},{5,7},{7,5},{8,10},{10,8},{9,1... | collective-permute-start | bytes 49160 | tf_op jit(solution)/shard_map/ppermute | solution.py:547
  6.7 5.8 %collective-permute-start.1 = (f32[32,128]{1,0:T(8,128)S(1)}, f32[32,128]{1,0:T(8,128)S(1)}, u32[]{:S(2)}, u32[]{:S(2)}) collective-permute-start(f32[32,128]{1,0:T(8,128)S(1)} %get-tuple-element.21), channel_id=1, source_target_pairs={{1,6},{3,4},{4,3},{6,1},{5,10},{7,8},{8,7},{10,5},{9,14},{11,12},{... | collective-permute-start | bytes 49160 | tf_op jit(solution)/shard_map/ppermute | solution.py:547
  14.4 12.6 %collective-permute-start.5 = (f32[288,128]{1,0:T(8,128)S(1)}, f32[288,128]{1,0:T(8,128)S(1)}, u32[]{:S(2)}, u32[]{:S(2)}) collective-permute-start(f32[288,128]{1,0:T(8,128)S(1)} %get-tuple-element.32), channel_id=1, source_target_pairs={{1,4},{3,6},{4,1},{6,3},{5,8},{7,10},{8,5},{10,7},{9,12},{11,14},{... | collective-permute-start | bytes 442376 | tf_op jit(solution)/shard_map/ppermute | solution.py:595
  15.9 11.0 %collective-permute-start.6 = (f32[288,128]{1,0:T(8,128)S(1)}, f32[288,128]{1,0:T(8,128)S(1)}, u32[]{:S(2)}, u32[]{:S(2)}) collective-permute-start(f32[288,128]{1,0:T(8,128)S(1)} %get-tuple-element.33), channel_id=1, source_target_pairs={{0,1},{1,0},{4,5},{5,4},{8,9},{9,8},{12,13},{13,12},{2,3},{3,2},{6... | collective-permute-start | bytes 442376 | tf_op jit(solution)/shard_map/ppermute | solution.py:596

commit v10 on v9

--- a/solution.py
+++ b/solution.py
@@ -14,6 +14,7 @@
 SUBS = 8
 LANES = 128
 WANTED = 16
+SKEW = SUBS + 1
 AHEAD = 5
 
 unreached = 1000000000.0
@@ -93,7 +94,7 @@
 def edge_kernel(
     ground_hbm, depth_hbm, rows_hbm, sides_hbm, links_hbm,
     far_ref, near_ref, even_ref, odd_ref, ground_out, surface_out, links_ref,
-    ground_ref, depth_ref, rows_ref, sides_ref, sems, small_sems,
+    ground_ref, depth_ref, rows_ref, sides_ref, stage_ref, sems, small_sems,
 ):
     height, width = ground_hbm.shape
     tiles = width // (SUBS * LANES)
@@ -106,7 +107,7 @@
     copies = start_own(ground_hbm, depth_hbm, ground_ref, depth_ref, sems)
     start_all(small[:1])
     wait_all(small)
-    edges = fold_own(copies, ground_ref, depth_ref, rows_ref, sides_ref, ground_out, surface_out)
+    edges = fold_own(copies, ground_ref, depth_ref, rows_ref, sides_ref, ground_out, surface_out, stage_ref)
     place, _ = chain_place()
     top = place % 2 == 0
     size, packed = (tiles + 1) * SUBS, tiles * SUBS
@@ -142,7 +143,15 @@
     return copies
 
 
-def fold_own(copies, ground_ref, depth_ref, rows_ref, sides_ref, ground_out, surface_out):
+def staged(base, slot, number):
+    return pl.ds(base + (slot * SUBS + number) * SKEW, SUBS)
+
+
+def across(base, slot, number):
+    return pl.ds(base + slot * SUBS * SKEW + number, SUBS, stride=SKEW)
+
+
+def fold_own(copies, ground_ref, depth_ref, rows_ref, sides_ref, ground_out, surface_out, stage_ref):
     height, width = ground_ref.shape
     groups = height // SUBS
     tiles = width // (SUBS * LANES)
@@ -182,11 +191,17 @@
             for outlet in outlets:
                 surface = jnp.where(outlet, ground, surface)
             chunk, slot = tile // tiles, tile % tiles
-            start = (HALO + group * SUBS) * size + slot * SUBS + chunk
-            ground_out[pl.ds(start, SUBS, stride=size), :] = ground
-            surface_out[pl.ds(start, SUBS, stride=size), :] = surface
+            for kind, value in enumerate((ground, surface)):
+                stage_ref[staged((group * 2 + kind) * tiles * SUBS * SKEW, slot, chunk), :] = value
             if tile in (0, last_tile):
                 edges[group].append((ground, surface))
+    for group in range(groups):
+        for kind, out_ref in enumerate((ground_out, surface_out)):
+            base = (group * 2 + kind) * tiles * SUBS * SKEW
+            for slot in range(tiles):
+                for row in range(SUBS):
+                    where = register(HALO + group * SUBS + row, slot, size)
+                    out_ref[where, :] = stage_ref[across(base, slot, row), :]
     return edges
 
 
@@ -409,7 +424,7 @@
 
 def late_kernel(
     height, tiles, ground_ref, surface_ref, far_ref, near_ref, floors_ref, hops_ref, out_hbm,
-    one_ref, two_ref, out_ref, ceilings_ref, sems,
+    one_ref, two_ref, out_ref, ceilings_ref, stage_ref, sems,
 ):
     ring = tiles + 1
     size = ring * SUBS
@@ -465,11 +480,13 @@
     def unfold(group):
         first = HALO + group * SUBS
         half = tiles * SUBS // 2
+        for slot in range(tiles):
+            for row in range(SUBS):
+                stage_ref[staged(0, slot, row), :] = target[register(first + row, slot, size), :]
         for tile in range(tiles * SUBS):
             chunk, slot = tile // tiles, tile % tiles
-            out_ref[pl.ds(group * SUBS, SUBS), pl.ds(tile * LANES, LANES)] = target[
-                pl.ds(first * size + slot * SUBS + chunk, SUBS, stride=size), :
-            ]
+            columns = pl.ds(tile * LANES, LANES)
+            out_ref[pl.ds(group * SUBS, SUBS), columns] = stage_ref[across(0, slot, chunk), :]
             if tile % half == half - 1:
                 side = tile // half
                 where = (pl.ds(group * SUBS, SUBS), pl.ds(side * half * LANES, half * LANES))
@@ -520,6 +537,7 @@
             pltpu.VMEM((height, width), f32),
             pltpu.VMEM(edge_rows.shape, jnp.int32),
             pltpu.VMEM(edge_sides.shape, jnp.int32),
+            pltpu.VMEM((2 * groups * packed * SKEW, LANES), f32),
             pltpu.SemaphoreType.DMA((2, 4)),
             pltpu.SemaphoreType.DMA((3,)),
         ],
@@ -609,6 +627,7 @@
             work,
             pltpu.VMEM((height, width), f32),
             pltpu.VMEM((WANTED, LANES), f32),
+            pltpu.VMEM((packed * SKEW, LANES), f32),
             pltpu.SemaphoreType.DMA((groups, 2)),
         ],
         compiler_params=limit,

time: 29.5 us -> 29.5 us (level)
  no operation moved by 1% of the time
where the time goes in v10:
time: 29.5 us; the launch traced here: 29.3 us
  blocking collectives  10.7 us (36%)
  Pallas kernels  9.16 us (31%)
  starting transfers between devices  8.3 us (28%)
  waiting for transfers between devices  1.1 us (4%)
    all_to_all x1, blocking collectives, per_device(): floors = lax.all_to_all(floors, device_axes, 0, 0, tiled=True)  10.7 us
    ppermute x2, starting transfers between devices, per_device(): far_rows = lax.ppermute(far, ('groups',) + device_axes, far_all)  4.14 us
    ppermute x3, starting transfers between devices, swap_strips(): arrived.append(lax.ppermute(piece, device_axes, pairs) if pairs else piece)  3.29 us
    pallas_call x1, Pallas kernels, per_device(): pl.pallas_call(inner, out_shape=[work, work, work, again], in_specs=in_vm...  2.62 us
    pallas_call x1, Pallas kernels, per_device(): pl.pallas_call(late, out_shape=jax.ShapeDtypeStruct((height, width), f32)...  2.41 us
    pallas_call x1, Pallas kernels, per_device(): pl.pallas_call(outer, out_shape=[work, work, work, pltpu.VMEM((devices, L...  1.76 us
    pallas_call x1, Pallas kernels, per_device(): pl.pallas_call(edge_kernel, out_shape=[sent, sent, strip, strip, work, wo...  1.75 us
    ppermute x3, waiting for transfers between devices, swap_strips(): arrived.append(lax.ppermute(piece, device_axes, pairs) if pairs else piece)  1.09 us
  transfers between devices with their start and end apart: 7, of which 1 were waited for; matrix products, arithmetic and copies ran while one was open for 0% of the time, Pallas kernels for 11%

profile of v10, /device:TPU:0, one launch (start us, length us, event | category | flops | bytes accessed | tf_op | source)
XLA Modules:
  0.0 29.3 jit_solution(1739825848244701972)
XLA Ops:
  0.0 1.8 %edge_rows.1 = (f32[960,128]{1,0:T(8,128)S(1)}, f32[960,128]{1,0:T(8,128)S(1)}, f32[32,128]{1,0:T(8,128)S(1)}, f32[32,128]{1,0:T(8,128)S(1)}, f32[2304,128]{1,0:...) custom-call(f32[16,8192]{1,0:T(8,128)} %ground_hbm.1, f32[16,8192]{1,0:T(8,128)} %depth_hbm.1, ...), custom_call_target="tpu_custom_call" | custom-call | flops 1024 | bytes 1024 | tf_op jit(solution)/shard_map/edge_rows/pallas_call | solution.py:530
  1.8 0.5 %collective-permute-start.2 = (f32[960,128]{1,0:T(8,128)S(1)}, f32[960,128]{1,0:T(8,128)S(1)}, u32[]{:S(2)}, u32[]{:S(2)}) collective-permute-start(f32[960,128]{1,0:T(8,128)S(1)} %get-tuple-element.23), channel_id=1, source_target_pairs={{0,1},{1,0},{4,5},{5,4},{8,9},{9,8},{12,13},{13,12},{2,3},{3,2},{6... | collective-permute-start | bytes 1474568 | tf_op jit(solution)/shard_map/ppermute | solution.py:570
  2.3 2.6 %collective-permute-start = (f32[960,128]{1,0:T(8,128)S(1)}, f32[960,128]{1,0:T(8,128)S(1)}, u32[]{:S(2)}, u32[]{:S(2)}) collective-permute-start(f32[960,128]{1,0:T(8,128)S(1)} %get-tuple-element.20), channel_id=1, source_target_pairs={{1,4},{3,6},{4,1},{6,3},{5,8},{7,10},{8,5},{10,7},{9,12},{11,14},{... | collective-permute-start | bytes 1474568 | tf_op jit(solution)/shard_map/ppermute | solution.py:569
  4.9 1.3 %collective-permute-start.4 = (f32[32,128]{1,0:T(8,128)S(1)}, f32[32,128]{1,0:T(8,128)S(1)}, u32[]{:S(2)}, u32[]{:S(2)}) collective-permute-start(f32[32,128]{1,0:T(8,128)S(1)} %get-tuple-element.21), channel_id=1, source_target_pairs={{0,3},{2,1},{1,2},{3,0},{4,7},{6,5},{5,6},{7,4},{8,11},{10,9},{9,1... | collective-permute-start | bytes 49160 | tf_op jit(solution)/shard_map/ppermute | solution.py:565
  6.1 0.5 %collective-permute-start.3 = (f32[32,128]{1,0:T(8,128)S(1)}, f32[32,128]{1,0:T(8,128)S(1)}, u32[]{:S(2)}, u32[]{:S(2)}) collective-permute-start(f32[32,128]{1,0:T(8,128)S(1)} %get-tuple-element.21), channel_id=1, source_target_pairs={{0,2},{2,0},{1,3},{3,1},{4,6},{6,4},{5,7},{7,5},{8,10},{10,8},{9,1... | collective-permute-start | bytes 49160 | tf_op jit(solution)/shard_map/ppermute | solution.py:565
  6.7 1.5 %collective-permute-start.1 = (f32[32,128]{1,0:T(8,128)S(1)}, f32[32,128]{1,0:T(8,128)S(1)}, u32[]{:S(2)}, u32[]{:S(2)}) collective-permute-start(f32[32,128]{1,0:T(8,128)S(1)} %get-tuple-element.21), channel_id=1, source_target_pairs={{1,6},{3,4},{4,3},{6,1},{5,10},{7,8},{8,7},{10,5},{9,14},{11,12},{... | collective-permute-start | bytes 49160 | tf_op jit(solution)/shard_map/ppermute | solution.py:565
  8.2 0.6 %tile_hops.1.refs_7_.refs_5_ = f32[128,128]{1,0:T(8,128)S(1)} custom-call(s32[8,6]{1,0:T(8,128)S(1)} %get-tuple-element.26.links_ref), custom_call_target="tpu_custom_call" | custom-call | flops 1024 | bytes 1024 | tf_op jit(solution)/shard_map/tile_hops/pallas_call | solution.py:573
  8.8 0.0 collective-permute-done.4.refs_3_
  8.8 1.1 %collective-permute-done.3.refs_1_ = f32[32,128]{1,0:T(8,128)S(1)} collective-permute-done((f32[32,128]{1,0:T(8,128)S(1)}, f32[32,128]{1,0:T(8,128)S(1)}, u32[]{:S(2)}, u32[]{:S(2)}) %collective-permute-start.3) | collective-permute-done | bytes 16416 | tf_op jit(solution)/shard_map/ppermute | solution.py:565
  9.9 0.0 collective-permute-done.2.refs_0_
  9.9 2.6 %inner_passes.1 = (f32[2304,128]{1,0:T(8,128)S(1)}, f32[2304,128]{1,0:T(8,128)S(1)}, f32[2304,128]{1,0:T(8,128)S(1)}, f32[288,128]{1,0:T(8,128)S(1)}) custom-call(f32[960,128]{1,0:T(8,128)S(1)} %collective-permute-done.2.refs_0_, f32[32,128]{1,0:T(8,128)S(1)} %collective-permute-done.3.refs_1_, ...), custom_call_target="tpu_custom_call", output_to_operand_aliasing={{0}: (5, {}), {1}: (6, {})} | custom-call | flops 1024 | bytes 1024 | tf_op jit(solution)/shard_map/inner_passes/pallas_call | solution.py:587
  12.5 0.0 collective-permute-done.1.refs_0_
  12.5 0.0 collective-permute-done.far_ref
  12.5 1.8 %outer_passes.1 = (f32[2304,128]{1,0:T(8,128)S(1)}, f32[2304,128]{1,0:T(8,128)S(1)}, f32[2304,128]{1,0:T(8,128)S(1)}, f32[16,128]{1,0:T(8,128)S(1)}, f32[288,128]{1,0:T(8,128)S(1)}) custom-call(f32[960,128]{1,0:T(8,128)S(1)} %collective-permute-done.far_ref, ...), custom_call_target="tpu_custom_call", output_to_operand_aliasing={{0}: (3, {}), {1}: (4, {}), {2}: (5, {})} | custom-call | flops 1024 | bytes 1024 | tf_op jit(solution)/shard_map/outer_passes/pallas_call | solution.py:602
  14.3 1.6 %collective-permute-start.5 = (f32[288,128]{1,0:T(8,128)S(1)}, f32[288,128]{1,0:T(8,128)S(1)}, u32[]{:S(2)}, u32[]{:S(2)}) collective-permute-start(f32[288,128]{1,0:T(8,128)S(1)} %get-tuple-element.32), channel_id=1, source_target_pairs={{1,4},{3,6},{4,1},{6,3},{5,8},{7,10},{8,5},{10,7},{9,12},{11,14},{... | collective-permute-start | bytes 442376 | tf_op jit(solution)/shard_map/ppermute | solution.py:613
  15.8 0.3 %collective-permute-start.6 = (f32[288,128]{1,0:T(8,128)S(1)}, f32[288,128]{1,0:T(8,128)S(1)}, u32[]{:S(2)}, u32[]{:S(2)}) collective-permute-start(f32[288,128]{1,0:T(8,128)S(1)} %get-tuple-element.33), channel_id=1, source_target_pairs={{0,1},{1,0},{4,5},{5,4},{8,9},{9,8},{12,13},{13,12},{2,3},{3,2},{6... | collective-permute-start | bytes 442376 | tf_op jit(solution)/shard_map/ppermute | solution.py:614
  16.2 10.7 %all_to_all.11 = f32[16,1,128]{2,1,0:T(1,128)S(1)} all-to-all(f32[16,1,128]{2,1,0:T(1,128)S(1)} %bitcast.5), channel_id=1, replica_groups=mesh['groups'=2,'rows'=4,'cols'=2,'sub'=2] {'rows','cols','sub'}, dimensions={0} | all-to-all | bytes 16384 | tf_op jit(solution)/shard_map/all_to_all | solution.py:615
  26.9 0.0 collective-permute-done.5.refs_2_
  26.9 0.0 collective-permute-done.6.refs_3_
  26.9 2.4 %final_passes.1 = f32[16,8192]{1,0:T(8,128)} custom-call(f32[2304,128]{1,0:T(8,128)S(1)} %get-tuple-element.30.refs_0_, f32[2304,128]{1,0:T(8,128)S(1)} %get-tuple-element.31.refs_1_, f32[288,128]{1,0:T(8,128)S(1)} %collective-permute-done.5.refs_2_, f32[288,128]{1,0:T(8,128)S(1)} %collective-permute-done.6.refs_3_, f32[16,128]{1,0:T(8,128)S(1)} %bitcast.4, ...), custom_call_target="tpu_custom_call" | custom-call | flops 1024 | bytes 1024 | tf_op jit(solution)/shard_map/final_passes/pallas_call | solution.py:620
Async XLA Ops:
  1.8 8.1 %collective-permute-start.2 = (f32[960,128]{1,0:T(8,128)S(1)}, f32[960,128]{1,0:T(8,128)S(1)}, u32[]{:S(2)}, u32[]{:S(2)}) collective-permute-start(f32[960,128]{1,0:T(8,128)S(1)} %get-tuple-element.23), channel_id=1, source_target_pairs={{0,1},{1,0},{4,5},{5,4},{8,9},{9,8},{12,13},{13,12},{2,3},{3,2},{6... | collective-permute-start | bytes 1474568 | tf_op jit(solution)/shard_map/ppermute | solution.py:570
  2.3 10.2 %collective-permute-start = (f32[960,128]{1,0:T(8,128)S(1)}, f32[960,128]{1,0:T(8,128)S(1)}, u32[]{:S(2)}, u32[]{:S(2)}) collective-permute-start(f32[960,128]{1,0:T(8,128)S(1)} %get-tuple-element.20), channel_id=1, source_target_pairs={{1,4},{3,6},{4,1},{6,3},{5,8},{7,10},{8,5},{10,7},{9,12},{11,14},{... | collective-permute-start | bytes 1474568 | tf_op jit(solution)/shard_map/ppermute | solution.py:569
  4.9 3.9 %collective-permute-start.4 = (f32[32,128]{1,0:T(8,128)S(1)}, f32[32,128]{1,0:T(8,128)S(1)}, u32[]{:S(2)}, u32[]{:S(2)}) collective-permute-start(f32[32,128]{1,0:T(8,128)S(1)} %get-tuple-element.21), channel_id=1, source_target_pairs={{0,3},{2,1},{1,2},{3,0},{4,7},{6,5},{5,6},{7,4},{8,11},{10,9},{9,1... | collective-permute-start | bytes 49160 | tf_op jit(solution)/shard_map/ppermute | solution.py:565
  6.1 3.7 %collective-permute-start.3 = (f32[32,128]{1,0:T(8,128)S(1)}, f32[32,128]{1,0:T(8,128)S(1)}, u32[]{:S(2)}, u32[]{:S(2)}) collective-permute-start(f32[32,128]{1,0:T(8,128)S(1)} %get-tuple-element.21), channel_id=1, source_target_pairs={{0,2},{2,0},{1,3},{3,1},{4,6},{6,4},{5,7},{7,5},{8,10},{10,8},{9,1... | collective-permute-start | bytes 49160 | tf_op jit(solution)/shard_map/ppermute | solution.py:565
  6.7 5.8 %collective-permute-start.1 = (f32[32,128]{1,0:T(8,128)S(1)}, f32[32,128]{1,0:T(8,128)S(1)}, u32[]{:S(2)}, u32[]{:S(2)}) collective-permute-start(f32[32,128]{1,0:T(8,128)S(1)} %get-tuple-element.21), channel_id=1, source_target_pairs={{1,6},{3,4},{4,3},{6,1},{5,10},{7,8},{8,7},{10,5},{9,14},{11,12},{... | collective-permute-start | bytes 49160 | tf_op jit(solution)/shard_map/ppermute | solution.py:565
  14.3 12.6 %collective-permute-start.5 = (f32[288,128]{1,0:T(8,128)S(1)}, f32[288,128]{1,0:T(8,128)S(1)}, u32[]{:S(2)}, u32[]{:S(2)}) collective-permute-start(f32[288,128]{1,0:T(8,128)S(1)} %get-tuple-element.32), channel_id=1, source_target_pairs={{1,4},{3,6},{4,1},{6,3},{5,8},{7,10},{8,5},{10,7},{9,12},{11,14},{... | collective-permute-start | bytes 442376 | tf_op jit(solution)/shard_map/ppermute | solution.py:613
  15.8 11.0 %collective-permute-start.6 = (f32[288,128]{1,0:T(8,128)S(1)}, f32[288,128]{1,0:T(8,128)S(1)}, u32[]{:S(2)}, u32[]{:S(2)}) collective-permute-start(f32[288,128]{1,0:T(8,128)S(1)} %get-tuple-element.33), channel_id=1, source_target_pairs={{0,1},{1,0},{4,5},{5,4},{8,9},{9,8},{12,13},{13,12},{2,3},{3,2},{6... | collective-permute-start | bytes 442376 | tf_op jit(solution)/shard_map/ppermute | solution.py:614

commit v11 on v10

--- a/solution.py
+++ b/solution.py
@@ -93,7 +93,7 @@
 
 def edge_kernel(
     ground_hbm, depth_hbm, rows_hbm, sides_hbm, links_hbm,
-    far_ref, near_ref, even_ref, odd_ref, ground_out, surface_out, links_ref,
+    far_ref, near_low_ref, near_high_ref, even_ref, odd_ref, ground_out, surface_out, links_ref,
     ground_ref, depth_ref, rows_ref, sides_ref, stage_ref, sems, small_sems,
 ):
     height, width = ground_hbm.shape
@@ -110,14 +110,16 @@
     edges = fold_own(copies, ground_ref, depth_ref, rows_ref, sides_ref, ground_out, surface_out, stage_ref)
     place, _ = chain_place()
     top = place % 2 == 0
-    size, packed = (tiles + 1) * SUBS, tiles * SUBS
-    for out_ref, is_top in ((far_ref, top), (near_ref, jnp.logical_not(top))):
+    size = (tiles + 1) * SUBS
+    for out_refs, is_top in (((far_ref,), top), ((near_low_ref, near_high_ref), jnp.logical_not(top))):
+        share = tiles // len(out_refs)
         first = HALO + jnp.where(is_top, 0, height - HALO)
         bases = (jnp.where(is_top, 0, HALO - 1), jnp.where(is_top, HALO - 1, 0))
         for source, base in zip((ground_out, surface_out), bases):
             for row in range(HALO):
                 for slot in range(tiles):
-                    out_ref[register(base + row, slot, packed), :] = source[register(first + row, slot, size), :]
+                    where = register(base + row, slot % share, share * SUBS)
+                    out_refs[slot // share][where, :] = source[register(first + row, slot, size), :]
     rightward = lax.axis_index("cols") % 2 == 0
     for group, values in enumerate(edges):
         for kind in range(2):
@@ -205,14 +207,16 @@
     return edges
 
 
-def unpack_rows(rows_ref, first, is_top, present, strip_refs, strip_rows, ground_ref, surface_ref, tiles):
-    packed = tiles * SUBS
-    size = packed + SUBS
+def unpack_rows(rows_refs, first, is_top, present, strip_refs, strip_rows, ground_ref, surface_ref, tiles):
+    share = tiles // len(rows_refs)
+    size = (tiles + 1) * SUBS
     bases = (jnp.where(is_top, HALO - 1, 0), jnp.where(is_top, 0, HALO - 1))
     for base, out_ref, strip_row in zip(bases, (ground_ref, surface_ref), strip_rows):
         for row in range(HALO):
             values = [
-                jnp.where(present, rows_ref[register(base + row, slot, packed), :], unreached)
+                jnp.where(
+                    present, rows_refs[slot // share][register(base + row, slot % share, share * SUBS), :], unreached
+                )
                 for slot in range(tiles)
             ]
             for slot in range(tiles):
@@ -326,7 +330,7 @@
             target[register(row, slot, ring * SUBS), :] = source[register(first + row, slot, ring * SUBS), :]
 
 
-def inner_kernel(height, tiles, near_ref, own_even_ref, own_odd_ref, near_even_ref, near_odd_ref, *refs):
+def inner_kernel(height, tiles, near_low_ref, near_high_ref, own_even_ref, own_odd_ref, near_even_ref, near_odd_ref, *refs):
     ground_ref, surface_ref, other_ref, near_out = refs[3:]
     own_strips, near_strips = (own_even_ref, own_odd_ref), (near_even_ref, near_odd_ref)
     ring = tiles + 1
@@ -335,7 +339,7 @@
     top = place % 2 == 0
     has_near = jnp.where(top, place < places - 1, place > 0)
     unpack_rows(
-        near_ref,
+        (near_low_ref, near_high_ref),
         jnp.where(top, HALO + height, 0),
         jnp.logical_not(top),
         has_near,
@@ -369,7 +373,7 @@
     top = place % 2 == 0
     has_far = jnp.where(top, place > 0, place < places - 1)
     unpack_rows(
-        far_ref,
+        (far_ref,),
         jnp.where(top, 0, HALO + height),
         top,
         has_far,
@@ -527,11 +531,12 @@
     sent = pltpu.VMEM(((2 * HALO - 1) * packed, LANES), f32)
     strip = pltpu.VMEM((2 * height, LANES), f32)
     work = pltpu.VMEM(((height + 2 * HALO) * size, LANES), f32)
-    far, near, even, odd, ground, surface, links = pl.pallas_call(
+    half = pltpu.VMEM(((2 * HALO - 1) * packed // 2, LANES), f32)
+    far, near_low, near_high, even, odd, ground, surface, links = pl.pallas_call(
         edge_kernel,
-        out_shape=[sent, sent, strip, strip, work, work, pltpu.VMEM(adjacency.shape, jnp.int32)],
+        out_shape=[sent, half, half, strip, strip, work, work, pltpu.VMEM(adjacency.shape, jnp.int32)],
         in_specs=in_hbm(5),
-        out_specs=in_vmem(7),
+        out_specs=in_vmem(8),
         scratch_shapes=[
             pltpu.VMEM((height, width), f32),
             pltpu.VMEM((height, width), f32),
@@ -567,7 +572,7 @@
 
     far_strips = swap_strips((even, odd), far_pairs + ends)
     far_rows = lax.ppermute(far, ("groups",) + device_axes, far_all)
-    near_rows = lax.ppermute(near, ("rows", "sub"), near_pairs)
+    near_rows = [lax.ppermute(part, ("rows", "sub"), near_pairs) for part in (near_low, near_high)]
     strips = swap_strips((even, odd), stay) + swap_strips((even, odd), near_pairs)
 
     hops = pl.pallas_call(
@@ -587,13 +592,13 @@
     ground, surface, other, near = pl.pallas_call(
         inner,
         out_shape=[work, work, work, again],
-        in_specs=in_vmem(8),
+        in_specs=in_vmem(9),
         out_specs=in_vmem(4),
-        input_output_aliases={5: 0, 6: 1},
+        input_output_aliases={6: 0, 7: 1},
         compiler_params=limit,
         cost_estimate=short,
         name="inner_passes",
-    )(near_rows, *strips, ground, surface, hops)
+    )(*near_rows, *strips, ground, surface, hops)
 
     def outer(far_ref, *refs):
         outer_kernel(height, tiles, far_ref, *refs)

time: 29.5 us -> 30.9 us (1.047)
  blocking collectives: 10.7 us -> 0 us
  waiting for transfers between devices: 1.1 us -> 7.7 us
  starting transfers between devices: 8.3 us -> 13.2 us
  Pallas kernels: 9.16 us -> 9.76 us
    all_to_all x1 -> x0, blocking collectives: 10.7 us -> none  [per_device(): floors = lax.all_to_all(floors, device_axes, 0, 0, tiled=True)]
    all_to_all x0 -> x1, waiting for transfers between devices: none -> 6.32 us  [per_device(): floors = lax.all_to_all(floors, device_axes, 0, 0, tiled=True)]
    all_to_all x0 -> x1, starting transfers between devices: none -> 3.97 us  [per_device(): floors = lax.all_to_all(floors, device_axes, 0, 0, tiled=True)]
    pallas_call x1, Pallas kernels: 1.76 us -> 2.35 us  [per_device(): pl.pallas_call(outer, out_shape=[work, work, work, pltpu.VMEM((devices, L...]
    ppermute x0 -> x2, starting transfers between devices: none -> 0.51 us  [per_device(): lax.ppermute(part, ('rows', 'sub'), near_pairs)]
    ppermute x2, starting transfers between devices: 4.14 us -> 4.55 us  [per_device(): far_rows = lax.ppermute(far, ('groups',) + device_axes, far_all)]
    ppermute x2 -> x1, starting transfers between devices: 0.86 us -> 0.85 us  [per_device(): near_rows = lax.ppermute(near, ('rows', 'sub'), near_pairs)]
  transfers between devices with their start and end apart: 7 -> 9, of which waited for: 1 -> 2; matrix products, arithmetic and copies ran while one was open for 0% -> 0% of each run, Pallas kernels for 11% -> 18%
where the time goes in v11:
time: 30.9 us; the launch traced here: 30.7 us
  starting transfers between devices  13.2 us (43%)
  Pallas kernels  9.76 us (32%)
  waiting for transfers between devices  7.7 us (25%)
    all_to_all x1, waiting for transfers between devices, per_device(): floors = lax.all_to_all(floors, device_axes, 0, 0, tiled=True)  6.32 us
    ppermute x2, starting transfers between devices, per_device(): far_rows = lax.ppermute(far, ('groups',) + device_axes, far_all)  4.55 us
    all_to_all x1, starting transfers between devices, per_device(): floors = lax.all_to_all(floors, device_axes, 0, 0, tiled=True)  3.97 us
    ppermute x3, starting transfers between devices, swap_strips(): arrived.append(lax.ppermute(piece, device_axes, pairs) if pairs else piece)  3.29 us
    pallas_call x1, Pallas kernels, per_device(): pl.pallas_call(inner, out_shape=[work, work, work, again], in_specs=in_vm...  2.65 us
    pallas_call x1, Pallas kernels, per_device(): pl.pallas_call(late, out_shape=jax.ShapeDtypeStruct((height, width), f32)...  2.4 us
    pallas_call x1, Pallas kernels, per_device(): pl.pallas_call(outer, out_shape=[work, work, work, pltpu.VMEM((devices, L...  2.35 us
    pallas_call x1, Pallas kernels, per_device(): pl.pallas_call(edge_kernel, out_shape=[sent, half, half, strip, strip, wo...  1.75 us
  transfers between devices with their start and end apart: 9, of which 2 were waited for; matrix products, arithmetic and copies ran while one was open for 0% of the time, Pallas kernels for 18%

profile of v11, /device:TPU:0, one launch (start us, length us, event | category | flops | bytes accessed | tf_op | source)
XLA Modules:
  0.0 30.7 jit_solution(5966410682793917188)
XLA Ops:
  0.0 1.8 %edge_rows.1 = (f32[960,128]{1,0:T(8,128)S(1)}, f32[480,128]{1,0:T(8,128)S(1)}, f32[480,128]{1,0:T(8,128)S(1)}, f32[32,128]{1,0:T(8,128)S(1)}, f32[32,128]{1,0:T...) custom-call(f32[16,8192]{1,0:T(8,128)} %ground_hbm.1, f32[16,8192]{1,0:T(8,128)} %depth_hbm.1, ...), custom_call_target="tpu_custom_call" | custom-call | flops 1024 | bytes 1024 | tf_op jit(solution)/shard_map/edge_rows/pallas_call | solution.py:535
  1.8 3.0 %collective-permute-start = (f32[960,128]{1,0:T(8,128)S(1)}, f32[960,128]{1,0:T(8,128)S(1)}, u32[]{:S(2)}, u32[]{:S(2)}) collective-permute-start(f32[960,128]{1,0:T(8,128)S(1)} %get-tuple-element.21), channel_id=1, source_target_pairs={{1,4},{3,6},{4,1},{6,3},{5,8},{7,10},{8,5},{10,7},{9,12},{11,14},{... | collective-permute-start | bytes 1474568 | tf_op jit(solution)/shard_map/ppermute | solution.py:574
  4.8 0.2 collective-permute-start.2
  5.0 0.3 %collective-permute-start.3 = (f32[480,128]{1,0:T(8,128)S(1)}, f32[480,128]{1,0:T(8,128)S(1)}, u32[]{:S(2)}, u32[]{:S(2)}) collective-permute-start(f32[480,128]{1,0:T(8,128)S(1)} %get-tuple-element.25), channel_id=1, source_target_pairs={{0,1},{1,0},{4,5},{5,4},{8,9},{9,8},{12,13},{13,12},{2,3},{3,2},{6... | collective-permute-start | bytes 737288 | tf_op jit(solution)/shard_map/ppermute | solution.py:575
  5.3 1.3 %collective-permute-start.5 = (f32[32,128]{1,0:T(8,128)S(1)}, f32[32,128]{1,0:T(8,128)S(1)}, u32[]{:S(2)}, u32[]{:S(2)}) collective-permute-start(f32[32,128]{1,0:T(8,128)S(1)} %get-tuple-element.22), channel_id=1, source_target_pairs={{0,3},{2,1},{1,2},{3,0},{4,7},{6,5},{5,6},{7,4},{8,11},{10,9},{9,1... | collective-permute-start | bytes 49160 | tf_op jit(solution)/shard_map/ppermute | solution.py:570
  6.6 0.5 %collective-permute-start.4 = (f32[32,128]{1,0:T(8,128)S(1)}, f32[32,128]{1,0:T(8,128)S(1)}, u32[]{:S(2)}, u32[]{:S(2)}) collective-permute-start(f32[32,128]{1,0:T(8,128)S(1)} %get-tuple-element.22), channel_id=1, source_target_pairs={{0,2},{2,0},{1,3},{3,1},{4,6},{6,4},{5,7},{7,5},{8,10},{10,8},{9,1... | collective-permute-start | bytes 49160 | tf_op jit(solution)/shard_map/ppermute | solution.py:570
  7.1 1.4 %collective-permute-done.5.refs_4_ = f32[32,128]{1,0:T(8,128)S(1)} collective-permute-done((f32[32,128]{1,0:T(8,128)S(1)}, f32[32,128]{1,0:T(8,128)S(1)}, u32[]{:S(2)}, u32[]{:S(2)}) %collective-permute-start.5) | collective-permute-done | bytes 16416 | tf_op jit(solution)/shard_map/ppermute | solution.py:570
  8.5 1.5 %collective-permute-start.1 = (f32[32,128]{1,0:T(8,128)S(1)}, f32[32,128]{1,0:T(8,128)S(1)}, u32[]{:S(2)}, u32[]{:S(2)}) collective-permute-start(f32[32,128]{1,0:T(8,128)S(1)} %get-tuple-element.22), channel_id=1, source_target_pairs={{1,6},{3,4},{4,3},{6,1},{5,10},{7,8},{8,7},{10,5},{9,14},{11,12},{... | collective-permute-start | bytes 49160 | tf_op jit(solution)/shard_map/ppermute | solution.py:570
  10.0 0.6 %tile_hops.1.refs_8_.refs_5_ = f32[128,128]{1,0:T(8,128)S(1)} custom-call(s32[8,6]{1,0:T(8,128)S(1)} %get-tuple-element.28.links_ref), custom_call_target="tpu_custom_call" | custom-call | flops 1024 | bytes 1024 | tf_op jit(solution)/shard_map/tile_hops/pallas_call | solution.py:578
  10.6 0.0 collective-permute-done.4.refs_2_
  10.6 0.0 collective-permute-done.2.refs_0_
  10.6 0.0 collective-permute-done.3.refs_1_
  10.6 2.6 %inner_passes.1 = (f32[2304,128]{1,0:T(8,128)S(1)}, f32[2304,128]{1,0:T(8,128)S(1)}, f32[2304,128]{1,0:T(8,128)S(1)}, f32[288,128]{1,0:T(8,128)S(1)}) custom-call(f32[480,128]{1,0:T(8,128)S(1)} %collective-permute-done.2.refs_0_, f32[480,128]{1,0:T(8,128)S(1)} %collective-permute-done.3.refs_1_, ...), custom_call_target="tpu_custom_call", output_to_operand_aliasing={{0}: (6, {}), {1}: (7, {})} | custom-call | flops 1024 | bytes 1024 | tf_op jit(solution)/shard_map/inner_passes/pallas_call | solution.py:592
  13.3 0.9 %collective-permute-start.7 = (f32[288,128]{1,0:T(8,128)S(1)}, f32[288,128]{1,0:T(8,128)S(1)}, u32[]{:S(2)}, u32[]{:S(2)}) collective-permute-start(f32[288,128]{1,0:T(8,128)S(1)} %get-tuple-element.35), channel_id=1, source_target_pairs={{0,1},{1,0},{4,5},{5,4},{8,9},{9,8},{12,13},{13,12},{2,3},{3,2},{6... | collective-permute-start | bytes 442376 | tf_op jit(solution)/shard_map/ppermute | solution.py:619
  14.1 0.0 collective-permute-done.1.refs_0_
  14.1 0.0 collective-permute-done.far_ref
  14.1 2.3 %outer_passes.1 = (f32[2304,128]{1,0:T(8,128)S(1)}, f32[2304,128]{1,0:T(8,128)S(1)}, f32[2304,128]{1,0:T(8,128)S(1)}, f32[16,128]{1,0:T(8,128)}, f32[288,128]{1,0:T(8,128)S(1)}) custom-call(f32[960,128]{1,0:T(8,128)S(1)} %collective-permute-done.far_ref, ...), custom_call_target="tpu_custom_call", output_to_operand_aliasing={{0}: (3, {}), {1}: (4, {}), {2}: (5, {})} | custom-call | flops 1024 | bytes 1024 | tf_op jit(solution)/shard_map/outer_passes/pallas_call | solution.py:607
  16.5 1.5 %collective-permute-start.6 = (f32[288,128]{1,0:T(8,128)S(1)}, f32[288,128]{1,0:T(8,128)S(1)}, u32[]{:S(2)}, u32[]{:S(2)}) collective-permute-start(f32[288,128]{1,0:T(8,128)S(1)} %get-tuple-element.34), channel_id=1, source_target_pairs={{1,4},{3,6},{4,1},{6,3},{5,8},{7,10},{8,5},{10,7},{9,12},{11,14},{... | collective-permute-start | bytes 442376 | tf_op jit(solution)/shard_map/ppermute | solution.py:618
  18.0 4.0 %all-to-all-start = ((f32[16,1,128]{2,1,0:T(1,128)}), f32[16,1,128]{2,1,0:T(1,128)S(1)}, u32[]{:S(2)}, u32[]{:S(2)}) async-start(f32[16,1,128]{2,1,0:T(1,128)} %bitcast.1), calls=%async_computation | async-start | bytes 16384 | tf_op jit(solution)/shard_map/all_to_all | solution.py:620
  22.0 0.0 collective-permute-done.7.refs_3_
  22.0 6.3 %all-to-all-done = f32[16,1,128]{2,1,0:T(1,128)S(1)} async-done(((f32[16,1,128]{2,1,0:T(1,128)}), f32[16,1,128]{2,1,0:T(1,128)S(1)}, u32[]{:S(2)}, u32[]{:S(2)}) %all-to-all-start) | async-done | bytes 8224 | tf_op jit(solution)/shard_map/all_to_all | solution.py:620
  28.3 0.0 collective-permute-done.6.refs_2_
  28.3 2.4 %final_passes.1 = f32[16,8192]{1,0:T(8,128)} custom-call(f32[2304,128]{1,0:T(8,128)S(1)} %get-tuple-element.32.refs_0_, f32[2304,128]{1,0:T(8,128)S(1)} %get-tuple-element.33.refs_1_, f32[288,128]{1,0:T(8,128)S(1)} %collective-permute-done.6.refs_2_, f32[288,128]{1,0:T(8,128)S(1)} %collective-permute-done.7.refs_3_, f32[16,128]{1,0:T(8,128)S(1)} %bitcast.4, ...), custom_call_target="tpu_custom_call" | custom-call | flops 1024 | bytes 1024 | tf_op jit(solution)/shard_map/final_passes/pallas_call | solution.py:625
Async XLA Ops:
  1.8 12.4 %collective-permute-start = (f32[960,128]{1,0:T(8,128)S(1)}, f32[960,128]{1,0:T(8,128)S(1)}, u32[]{:S(2)}, u32[]{:S(2)}) collective-permute-start(f32[960,128]{1,0:T(8,128)S(1)} %get-tuple-element.21), channel_id=1, source_target_pairs={{1,4},{3,6},{4,1},{6,3},{5,8},{7,10},{8,5},{10,7},{9,12},{11,14},{... | collective-permute-start | bytes 1474568 | tf_op jit(solution)/shard_map/ppermute | solution.py:574
  4.8 5.8 %collective-permute-start.2 = (f32[480,128]{1,0:T(8,128)S(1)}, f32[480,128]{1,0:T(8,128)S(1)}, u32[]{:S(2)}, u32[]{:S(2)}) collective-permute-start(f32[480,128]{1,0:T(8,128)S(1)} %get-tuple-element.24), channel_id=1, source_target_pairs={{0,1},{1,0},{4,5},{5,4},{8,9},{9,8},{12,13},{13,12},{2,3},{3,2},{6... | collective-permute-start | bytes 737288 | tf_op jit(solution)/shard_map/ppermute | solution.py:575
  5.0 5.6 %collective-permute-start.3 = (f32[480,128]{1,0:T(8,128)S(1)}, f32[480,128]{1,0:T(8,128)S(1)}, u32[]{:S(2)}, u32[]{:S(2)}) collective-permute-start(f32[480,128]{1,0:T(8,128)S(1)} %get-tuple-element.25), channel_id=1, source_target_pairs={{0,1},{1,0},{4,5},{5,4},{8,9},{9,8},{12,13},{13,12},{2,3},{3,2},{6... | collective-permute-start | bytes 737288 | tf_op jit(solution)/shard_map/ppermute | solution.py:575
  5.3 3.2 %collective-permute-start.5 = (f32[32,128]{1,0:T(8,128)S(1)}, f32[32,128]{1,0:T(8,128)S(1)}, u32[]{:S(2)}, u32[]{:S(2)}) collective-permute-start(f32[32,128]{1,0:T(8,128)S(1)} %get-tuple-element.22), channel_id=1, source_target_pairs={{0,3},{2,1},{1,2},{3,0},{4,7},{6,5},{5,6},{7,4},{8,11},{10,9},{9,1... | collective-permute-start | bytes 49160 | tf_op jit(solution)/shard_map/ppermute | solution.py:570
  6.6 4.0 %collective-permute-start.4 = (f32[32,128]{1,0:T(8,128)S(1)}, f32[32,128]{1,0:T(8,128)S(1)}, u32[]{:S(2)}, u32[]{:S(2)}) collective-permute-start(f32[32,128]{1,0:T(8,128)S(1)} %get-tuple-element.22), channel_id=1, source_target_pairs={{0,2},{2,0},{1,3},{3,1},{4,6},{6,4},{5,7},{7,5},{8,10},{10,8},{9,1... | collective-permute-start | bytes 49160 | tf_op jit(solution)/shard_map/ppermute | solution.py:570
  8.5 5.6 %collective-permute-start.1 = (f32[32,128]{1,0:T(8,128)S(1)}, f32[32,128]{1,0:T(8,128)S(1)}, u32[]{:S(2)}, u32[]{:S(2)}) collective-permute-start(f32[32,128]{1,0:T(8,128)S(1)} %get-tuple-element.22), channel_id=1, source_target_pairs={{1,6},{3,4},{4,3},{6,1},{5,10},{7,8},{8,7},{10,5},{9,14},{11,12},{... | collective-permute-start | bytes 49160 | tf_op jit(solution)/shard_map/ppermute | solution.py:570
  13.3 8.7 %collective-permute-start.7 = (f32[288,128]{1,0:T(8,128)S(1)}, f32[288,128]{1,0:T(8,128)S(1)}, u32[]{:S(2)}, u32[]{:S(2)}) collective-permute-start(f32[288,128]{1,0:T(8,128)S(1)} %get-tuple-element.35), channel_id=1, source_target_pairs={{0,1},{1,0},{4,5},{5,4},{8,9},{9,8},{12,13},{13,12},{2,3},{3,2},{6... | collective-permute-start | bytes 442376 | tf_op jit(solution)/shard_map/ppermute | solution.py:619
  16.5 11.8 %collective-permute-start.6 = (f32[288,128]{1,0:T(8,128)S(1)}, f32[288,128]{1,0:T(8,128)S(1)}, u32[]{:S(2)}, u32[]{:S(2)}) collective-permute-start(f32[288,128]{1,0:T(8,128)S(1)} %get-tuple-element.34), channel_id=1, source_target_pairs={{1,4},{3,6},{4,1},{6,3},{5,8},{7,10},{8,5},{10,7},{9,12},{11,14},{... | collective-permute-start | bytes 442376 | tf_op jit(solution)/shard_map/ppermute | solution.py:618
  18.0 10.3 %all-to-all-start = ((f32[16,1,128]{2,1,0:T(1,128)}), f32[16,1,128]{2,1,0:T(1,128)S(1)}, u32[]{:S(2)}, u32[]{:S(2)}) async-start(f32[16,1,128]{2,1,0:T(1,128)} %bitcast.1), calls=%async_computation | async-start | bytes 16384 | tf_op jit(solution)/shard_map/all_to_all | solution.py:620

commit v12 on v10

--- a/solution.py
+++ b/solution.py
@@ -538,7 +538,7 @@
             pltpu.VMEM(edge_rows.shape, jnp.int32),
             pltpu.VMEM(edge_sides.shape, jnp.int32),
             pltpu.VMEM((2 * groups * packed * SKEW, LANES), f32),
-            pltpu.SemaphoreType.DMA((2, 4)),
+            pltpu.SemaphoreType.DMA((2, 2)),
             pltpu.SemaphoreType.DMA((3,)),
         ],
         compiler_params=limit,

time: 29.5 us -> 29.3 us (level)
  no operation moved by 1% of the time
where the time goes in v12:
time: 29.3 us; the launch traced here: 29.1 us
  blocking collectives  10.7 us (37%)
  Pallas kernels  9.02 us (31%)
  starting transfers between devices  8.3 us (28%)
  waiting for transfers between devices  1.1 us (4%)
    all_to_all x1, blocking collectives, per_device(): floors = lax.all_to_all(floors, device_axes, 0, 0, tiled=True)  10.7 us
    ppermute x2, starting transfers between devices, per_device(): far_rows = lax.ppermute(far, ('groups',) + device_axes, far_all)  4.14 us
    ppermute x3, starting transfers between devices, swap_strips(): arrived.append(lax.ppermute(piece, device_axes, pairs) if pairs else piece)  3.29 us
    pallas_call x1, Pallas kernels, per_device(): pl.pallas_call(inner, out_shape=[work, work, work, again], in_specs=in_vm...  2.62 us
    pallas_call x1, Pallas kernels, per_device(): pl.pallas_call(late, out_shape=jax.ShapeDtypeStruct((height, width), f32)...  2.41 us
    pallas_call x1, Pallas kernels, per_device(): pl.pallas_call(outer, out_shape=[work, work, work, pltpu.VMEM((devices, L...  1.76 us
    pallas_call x1, Pallas kernels, per_device(): pl.pallas_call(edge_kernel, out_shape=[sent, sent, strip, strip, work, wo...  1.61 us
    ppermute x3, waiting for transfers between devices, swap_strips(): arrived.append(lax.ppermute(piece, device_axes, pairs) if pairs else piece)  1.09 us
  transfers between devices with their start and end apart: 7, of which 1 were waited for; matrix products, arithmetic and copies ran while one was open for 0% of the time, Pallas kernels for 11%

profile of v12, /device:TPU:0, one launch (start us, length us, event | category | flops | bytes accessed | tf_op | source)
XLA Modules:
  0.0 29.1 jit_solution(6455918343277198938)
XLA Ops:
  0.0 1.6 %edge_rows.1 = (f32[960,128]{1,0:T(8,128)S(1)}, f32[960,128]{1,0:T(8,128)S(1)}, f32[32,128]{1,0:T(8,128)S(1)}, f32[32,128]{1,0:T(8,128)S(1)}, f32[2304,128]{1,0:...) custom-call(f32[16,8192]{1,0:T(8,128)} %ground_hbm.1, f32[16,8192]{1,0:T(8,128)} %depth_hbm.1, ...), custom_call_target="tpu_custom_call" | custom-call | flops 1024 | bytes 1024 | tf_op jit(solution)/shard_map/edge_rows/pallas_call | solution.py:530
  1.6 0.5 %collective-permute-start.2 = (f32[960,128]{1,0:T(8,128)S(1)}, f32[960,128]{1,0:T(8,128)S(1)}, u32[]{:S(2)}, u32[]{:S(2)}) collective-permute-start(f32[960,128]{1,0:T(8,128)S(1)} %get-tuple-element.23), channel_id=1, source_target_pairs={{0,1},{1,0},{4,5},{5,4},{8,9},{9,8},{12,13},{13,12},{2,3},{3,2},{6... | collective-permute-start | bytes 1474568 | tf_op jit(solution)/shard_map/ppermute | solution.py:570
  2.1 2.6 %collective-permute-start = (f32[960,128]{1,0:T(8,128)S(1)}, f32[960,128]{1,0:T(8,128)S(1)}, u32[]{:S(2)}, u32[]{:S(2)}) collective-permute-start(f32[960,128]{1,0:T(8,128)S(1)} %get-tuple-element.20), channel_id=1, source_target_pairs={{1,4},{3,6},{4,1},{6,3},{5,8},{7,10},{8,5},{10,7},{9,12},{11,14},{... | collective-permute-start | bytes 1474568 | tf_op jit(solution)/shard_map/ppermute | solution.py:569
  4.7 1.3 %collective-permute-start.4 = (f32[32,128]{1,0:T(8,128)S(1)}, f32[32,128]{1,0:T(8,128)S(1)}, u32[]{:S(2)}, u32[]{:S(2)}) collective-permute-start(f32[32,128]{1,0:T(8,128)S(1)} %get-tuple-element.21), channel_id=1, source_target_pairs={{0,3},{2,1},{1,2},{3,0},{4,7},{6,5},{5,6},{7,4},{8,11},{10,9},{9,1... | collective-permute-start | bytes 49160 | tf_op jit(solution)/shard_map/ppermute | solution.py:565
  6.0 0.5 %collective-permute-start.3 = (f32[32,128]{1,0:T(8,128)S(1)}, f32[32,128]{1,0:T(8,128)S(1)}, u32[]{:S(2)}, u32[]{:S(2)}) collective-permute-start(f32[32,128]{1,0:T(8,128)S(1)} %get-tuple-element.21), channel_id=1, source_target_pairs={{0,2},{2,0},{1,3},{3,1},{4,6},{6,4},{5,7},{7,5},{8,10},{10,8},{9,1... | collective-permute-start | bytes 49160 | tf_op jit(solution)/shard_map/ppermute | solution.py:565
  6.5 1.5 %collective-permute-start.1 = (f32[32,128]{1,0:T(8,128)S(1)}, f32[32,128]{1,0:T(8,128)S(1)}, u32[]{:S(2)}, u32[]{:S(2)}) collective-permute-start(f32[32,128]{1,0:T(8,128)S(1)} %get-tuple-element.21), channel_id=1, source_target_pairs={{1,6},{3,4},{4,3},{6,1},{5,10},{7,8},{8,7},{10,5},{9,14},{11,12},{... | collective-permute-start | bytes 49160 | tf_op jit(solution)/shard_map/ppermute | solution.py:565
  8.0 0.6 %tile_hops.1.refs_7_.refs_5_ = f32[128,128]{1,0:T(8,128)S(1)} custom-call(s32[8,6]{1,0:T(8,128)S(1)} %get-tuple-element.26.links_ref), custom_call_target="tpu_custom_call" | custom-call | flops 1024 | bytes 1024 | tf_op jit(solution)/shard_map/tile_hops/pallas_call | solution.py:573
  8.6 0.0 collective-permute-done.4.refs_3_
  8.7 1.1 %collective-permute-done.3.refs_1_ = f32[32,128]{1,0:T(8,128)S(1)} collective-permute-done((f32[32,128]{1,0:T(8,128)S(1)}, f32[32,128]{1,0:T(8,128)S(1)}, u32[]{:S(2)}, u32[]{:S(2)}) %collective-permute-start.3) | collective-permute-done | bytes 16416 | tf_op jit(solution)/shard_map/ppermute | solution.py:565
  9.7 0.0 collective-permute-done.2.refs_0_
  9.7 2.6 %inner_passes.1 = (f32[2304,128]{1,0:T(8,128)S(1)}, f32[2304,128]{1,0:T(8,128)S(1)}, f32[2304,128]{1,0:T(8,128)S(1)}, f32[288,128]{1,0:T(8,128)S(1)}) custom-call(f32[960,128]{1,0:T(8,128)S(1)} %collective-permute-done.2.refs_0_, f32[32,128]{1,0:T(8,128)S(1)} %collective-permute-done.3.refs_1_, ...), custom_call_target="tpu_custom_call", output_to_operand_aliasing={{0}: (5, {}), {1}: (6, {})} | custom-call | flops 1024 | bytes 1024 | tf_op jit(solution)/shard_map/inner_passes/pallas_call | solution.py:587
  12.4 0.0 collective-permute-done.1.refs_0_
  12.4 0.0 collective-permute-done.far_ref
  12.4 1.8 %outer_passes.1 = (f32[2304,128]{1,0:T(8,128)S(1)}, f32[2304,128]{1,0:T(8,128)S(1)}, f32[2304,128]{1,0:T(8,128)S(1)}, f32[16,128]{1,0:T(8,128)S(1)}, f32[288,128]{1,0:T(8,128)S(1)}) custom-call(f32[960,128]{1,0:T(8,128)S(1)} %collective-permute-done.far_ref, ...), custom_call_target="tpu_custom_call", output_to_operand_aliasing={{0}: (3, {}), {1}: (4, {}), {2}: (5, {})} | custom-call | flops 1024 | bytes 1024 | tf_op jit(solution)/shard_map/outer_passes/pallas_call | solution.py:602
  14.1 1.6 %collective-permute-start.5 = (f32[288,128]{1,0:T(8,128)S(1)}, f32[288,128]{1,0:T(8,128)S(1)}, u32[]{:S(2)}, u32[]{:S(2)}) collective-permute-start(f32[288,128]{1,0:T(8,128)S(1)} %get-tuple-element.32), channel_id=1, source_target_pairs={{1,4},{3,6},{4,1},{6,3},{5,8},{7,10},{8,5},{10,7},{9,12},{11,14},{... | collective-permute-start | bytes 442376 | tf_op jit(solution)/shard_map/ppermute | solution.py:613
  15.7 0.3 %collective-permute-start.6 = (f32[288,128]{1,0:T(8,128)S(1)}, f32[288,128]{1,0:T(8,128)S(1)}, u32[]{:S(2)}, u32[]{:S(2)}) collective-permute-start(f32[288,128]{1,0:T(8,128)S(1)} %get-tuple-element.33), channel_id=1, source_target_pairs={{0,1},{1,0},{4,5},{5,4},{8,9},{9,8},{12,13},{13,12},{2,3},{3,2},{6... | collective-permute-start | bytes 442376 | tf_op jit(solution)/shard_map/ppermute | solution.py:614
  16.0 10.7 %all_to_all.11 = f32[16,1,128]{2,1,0:T(1,128)S(1)} all-to-all(f32[16,1,128]{2,1,0:T(1,128)S(1)} %bitcast.5), channel_id=1, replica_groups=mesh['groups'=2,'rows'=4,'cols'=2,'sub'=2] {'rows','cols','sub'}, dimensions={0} | all-to-all | bytes 16384 | tf_op jit(solution)/shard_map/all_to_all | solution.py:615
  26.7 0.0 collective-permute-done.5.refs_2_
  26.7 0.0 collective-permute-done.6.refs_3_
  26.7 2.4 %final_passes.1 = f32[16,8192]{1,0:T(8,128)} custom-call(f32[2304,128]{1,0:T(8,128)S(1)} %get-tuple-element.30.refs_0_, f32[2304,128]{1,0:T(8,128)S(1)} %get-tuple-element.31.refs_1_, f32[288,128]{1,0:T(8,128)S(1)} %collective-permute-done.5.refs_2_, f32[288,128]{1,0:T(8,128)S(1)} %collective-permute-done.6.refs_3_, f32[16,128]{1,0:T(8,128)S(1)} %bitcast.4, ...), custom_call_target="tpu_custom_call" | custom-call | flops 1024 | bytes 1024 | tf_op jit(solution)/shard_map/final_passes/pallas_call | solution.py:620
Async XLA Ops:
  1.6 8.1 %collective-permute-start.2 = (f32[960,128]{1,0:T(8,128)S(1)}, f32[960,128]{1,0:T(8,128)S(1)}, u32[]{:S(2)}, u32[]{:S(2)}) collective-permute-start(f32[960,128]{1,0:T(8,128)S(1)} %get-tuple-element.23), channel_id=1, source_target_pairs={{0,1},{1,0},{4,5},{5,4},{8,9},{9,8},{12,13},{13,12},{2,3},{3,2},{6... | collective-permute-start | bytes 1474568 | tf_op jit(solution)/shard_map/ppermute | solution.py:570
  2.1 10.2 %collective-permute-start = (f32[960,128]{1,0:T(8,128)S(1)}, f32[960,128]{1,0:T(8,128)S(1)}, u32[]{:S(2)}, u32[]{:S(2)}) collective-permute-start(f32[960,128]{1,0:T(8,128)S(1)} %get-tuple-element.20), channel_id=1, source_target_pairs={{1,4},{3,6},{4,1},{6,3},{5,8},{7,10},{8,5},{10,7},{9,12},{11,14},{... | collective-permute-start | bytes 1474568 | tf_op jit(solution)/shard_map/ppermute | solution.py:569
  4.7 3.9 %collective-permute-start.4 = (f32[32,128]{1,0:T(8,128)S(1)}, f32[32,128]{1,0:T(8,128)S(1)}, u32[]{:S(2)}, u32[]{:S(2)}) collective-permute-start(f32[32,128]{1,0:T(8,128)S(1)} %get-tuple-element.21), channel_id=1, source_target_pairs={{0,3},{2,1},{1,2},{3,0},{4,7},{6,5},{5,6},{7,4},{8,11},{10,9},{9,1... | collective-permute-start | bytes 49160 | tf_op jit(solution)/shard_map/ppermute | solution.py:565
  6.0 3.7 %collective-permute-start.3 = (f32[32,128]{1,0:T(8,128)S(1)}, f32[32,128]{1,0:T(8,128)S(1)}, u32[]{:S(2)}, u32[]{:S(2)}) collective-permute-start(f32[32,128]{1,0:T(8,128)S(1)} %get-tuple-element.21), channel_id=1, source_target_pairs={{0,2},{2,0},{1,3},{3,1},{4,6},{6,4},{5,7},{7,5},{8,10},{10,8},{9,1... | collective-permute-start | bytes 49160 | tf_op jit(solution)/shard_map/ppermute | solution.py:565
  6.5 5.8 %collective-permute-start.1 = (f32[32,128]{1,0:T(8,128)S(1)}, f32[32,128]{1,0:T(8,128)S(1)}, u32[]{:S(2)}, u32[]{:S(2)}) collective-permute-start(f32[32,128]{1,0:T(8,128)S(1)} %get-tuple-element.21), channel_id=1, source_target_pairs={{1,6},{3,4},{4,3},{6,1},{5,10},{7,8},{8,7},{10,5},{9,14},{11,12},{... | collective-permute-start | bytes 49160 | tf_op jit(solution)/shard_map/ppermute | solution.py:565
  14.1 12.6 %collective-permute-start.5 = (f32[288,128]{1,0:T(8,128)S(1)}, f32[288,128]{1,0:T(8,128)S(1)}, u32[]{:S(2)}, u32[]{:S(2)}) collective-permute-start(f32[288,128]{1,0:T(8,128)S(1)} %get-tuple-element.32), channel_id=1, source_target_pairs={{1,4},{3,6},{4,1},{6,3},{5,8},{7,10},{8,5},{10,7},{9,12},{11,14},{... | collective-permute-start | bytes 442376 | tf_op jit(solution)/shard_map/ppermute | solution.py:613
  15.7 11.0 %collective-permute-start.6 = (f32[288,128]{1,0:T(8,128)S(1)}, f32[288,128]{1,0:T(8,128)S(1)}, u32[]{:S(2)}, u32[]{:S(2)}) collective-permute-start(f32[288,128]{1,0:T(8,128)S(1)} %get-tuple-element.33), channel_id=1, source_target_pairs={{0,1},{1,0},{4,5},{5,4},{8,9},{9,8},{12,13},{13,12},{2,3},{3,2},{6... | collective-permute-start | bytes 442376 | tf_op jit(solution)/shard_map/ppermute | solution.py:614
